TPU v7x, 32 devices: a whole 2x2x4 slice. The times are simulated.
32 devices in a mesh: lon: 16 (over z, y, core), lat: 2 (over x).
Axes of the slice: x: 2, y: 2, z: 4, core: 2. Of those that a mesh axis runs over, the one named last changes fastest.
Arguments:
- field: bfloat16 [96, 32, 2048], P(None, 'lat', 'lon'), may hold values from -6 to 6
- land_mask: int32 [32, 2048], P('lat', 'lon'), may hold values from 0 to 1, as said below
- depth_kernel: float32 [2, 96, 7, 7], replicated, may hold values from -0.875 to 0.875
- depth_bias: float32 [2, 96], replicated, may hold values from -3 to 3
- norm_gain: float32 [2, 96], replicated, may hold values from 0.1 to 1.9
- norm_bias: float32 [2, 96], replicated, may hold values from -3 to 3
- w_expand: bfloat16 [2, 384, 96], replicated, may hold values from -0.625 to 0.625
- b_expand: float32 [2, 384], replicated, may hold values from -3 to 3
- w_reduce: bfloat16 [2, 96, 384], replicated, may hold values from -0.3125 to 0.3125
- b_reduce: float32 [2, 96], replicated, may hold values from -3 to 3
Outputs:
- output_field: bfloat16 [96, 32, 2048], P(None, 'lat', 'lon')
Inputs may be any that keep to these rules, and one draw needn't show every extreme that they name: `land_mask`: land and ocean come in regions; some aligned blocks of 8 rows and 128 columns are all land.
All inputs are finite; a program needn't handle non-finite values.
Results may differ from a plain program's by a relative error of at most 0.0058.
Values may be sent and summed in bfloat16 or wider, within the bound.
No kernel may reach another device: no remote copies, remote signals or barrier semaphores. Data moves between devices by JAX's collectives and lax.ppermute only.
A program may use at most 64 MiB of HBM per device.

v0:
```python
import jax
import jax.numpy as jnp
from jax import lax
from jax.sharding import PartitionSpec as P

LAYERS = 2


def extended_2(value, sides, width, wrap):
    for axis, dim in sides:
        count, length = (lax.axis_size(axis), value.shape[dim])
        up = [(i, (i + 1) % count) for i in range(count if wrap else count - 1)]
        down = [(j, i) for i, j in up]
        last = lax.slice_in_dim(value, length - width, length, axis=dim)
        leading = lax.slice_in_dim(value, 0, width, axis=dim)
        before = lax.ppermute(last, axis, up)
        after = lax.ppermute(leading, axis, down)
        value = jnp.concatenate([before, value, after], axis=dim)
    return value


def depthwise(band_rows, kernel, conv_bias):
    band_rows = band_rows.astype(jnp.float32)
    height = band_rows.shape[1] - 6
    width = band_rows.shape[2] - 6
    summed = jnp.zeros((band_rows.shape[0], height, width), jnp.float32) + conv_bias[:, None, None]
    for shift_row in range(7):
        for shift_col in range(7):
            summed = (
                summed
                + kernel[:, shift_row, shift_col, None, None]
                * band_rows[:, shift_row : shift_row + height, shift_col : shift_col + width]
            )
    return summed


def finish(
    mixed_cells,
    old_values,
    ocean_flags,
    norm_gain,
    norm_bias,
    w_expand,
    b_expand,
    w_reduce,
    b_reduce,
):
    channels, height, width = mixed_cells.shape
    flat_cells = mixed_cells.reshape(channels, height * width)
    average = jnp.mean(flat_cells, axis=0)
    centered = flat_cells - average
    variance = jnp.mean(centered * centered, axis=0)
    normed = (
        centered / jnp.sqrt(variance + 1e-06) * norm_gain[:, None] + norm_bias[:, None]
    ).astype(jnp.bfloat16)
    hidden = jnp.dot(w_expand, normed, preferred_element_type=jnp.float32) + b_expand[:, None]
    hidden = jax.nn.gelu(hidden, approximate=False).astype(jnp.bfloat16)
    update = jnp.dot(w_reduce, hidden, preferred_element_type=jnp.float32) + b_reduce[:, None]
    flags = ocean_flags.reshape(height * width).astype(jnp.float32)
    result_band = flags[None, :] * (
        old_values.reshape(channels, height * width).astype(jnp.float32) + update
    )
    return result_band.astype(jnp.bfloat16).reshape(channels, height, width)


def convnext_layer(
    values,
    land_mask,
    kernel,
    conv_bias,
    norm_gain,
    norm_bias,
    w_expand,
    b_expand,
    w_reduce,
    b_reduce,
):
    own_strip = values[:, -3:, :][:, ::-1, ::-1]
    tiles = lax.axis_size("lon")
    pieces = own_strip.reshape(tiles, own_strip.size // tiles)
    spread = lax.all_to_all(pieces, "lon", split_axis=0, concat_axis=0, tiled=True)
    spread = spread[::-1]
    collected = lax.all_to_all(spread, "lon", split_axis=0, concat_axis=0, tiled=True)
    fold_rows = collected.reshape(own_strip.shape)
    extended = extended_2(values, (("lat", 1),), 3, False)
    at_top = lax.axis_index("lat") == lax.axis_size("lat") - 1
    upper_rows = jnp.where(at_top, fold_rows, extended[:, -3:, :])
    extended = jnp.concatenate([extended[:, :-3, :], upper_rows], axis=1)
    extended = extended_2(extended, (("lon", 2),), 3, True)
    mixed_all = depthwise(extended, kernel, conv_bias)

    def band_step(band, result):
        start = band * 8
        mixed_cells = lax.dynamic_slice_in_dim(mixed_all, start, 8, 1)
        old_values = lax.dynamic_slice_in_dim(values, start, 8, 1)
        ocean_flags = lax.dynamic_slice_in_dim(land_mask, start, 8, 0)
        result_band = finish(
            mixed_cells,
            old_values,
            ocean_flags,
            norm_gain,
            norm_bias,
            w_expand,
            b_expand,
            w_reduce,
            b_reduce,
        )
        return lax.dynamic_update_slice_in_dim(result, result_band, start, 1)

    blank = jnp.zeros(values.shape, jnp.bfloat16)
    return lax.fori_loop(0, values.shape[1] // 8, band_step, blank)


def per_device(
    field,
    land_mask,
    depth_kernel,
    depth_bias,
    norm_gain,
    norm_bias,
    w_expand,
    b_expand,
    w_reduce,
    b_reduce,
):
    values = field
    for layer_index in range(LAYERS):
        values = convnext_layer(
            values,
            land_mask,
            depth_kernel[layer_index],
            depth_bias[layer_index],
            norm_gain[layer_index],
            norm_bias[layer_index],
            w_expand[layer_index],
            b_expand[layer_index],
            w_reduce[layer_index],
            b_reduce[layer_index],
        )
    return values


def solution(mesh):
    placed = (P(None, "lat", "lon"), P("lat", "lon"), P(), P(), P(), P(), P(), P(), P(), P())
    return jax.shard_map(
        per_device, mesh=mesh, in_specs=placed, out_specs=P(None, "lat", "lon"), check_vma=False
    )
```

profile of v0, /device:TPU:0, one launch (start us, length us, event | category | flops | bytes accessed | tf_op | source)
XLA Modules:
  0.0 112.4 jit_solution(6106878895494314679)
XLA Ops:
  0.0 1.7 %copy.36 = bf16[96,16,128]{0,1,2:T(8,128)(2,1)S(1)} copy(bf16[96,16,128]{2,1,0:T(8,128)(2,1)} %param.14) | data formatting | bytes 786432 | tf_op args[0]
  1.8 4.9 %collective-permute-start = (bf16[96,3,128]{0,1,2:T(4,128)(2,1)S(1)}, bf16[96,3,128]{0,1,2:T(4,128)(2,1)S(1)}, u32[]{:S(2)}, u32[]{:S(2)}) collective-permute-start(bf16[96,3,128]{0,1,2:T(4,128)(2,1)S(1)} %slice.883), channel_id=1, source_target_pairs={{0,1},{2,3},{4,5},{6,7},{8,9},{10,11},{12,13},{14,15},{16,17},{18,... | collective-permute-start | bytes 221192 | tf_op jit(solution)/shard_map/ppermute | solution.py:16
  6.7 0.2 rev.12
  7.1 0.5 broadcast.770
  7.7 1.0 reduce.16
  8.6 0.7 reshape.170
  9.3 5.9 %all-to-all-start = ((bf16[16,2,1152]{2,1,0:T(2,128)(2,1)}), bf16[16,2,1152]{2,1,0:T(2,128)(2,1)S(1)}, u32[]{:S(2)}, u32[]{:S(2)}) async-start(bf16[16,2,1152]{2,1,0:T(2,128)(2,1)} %reshape.170), calls=%async_computation | async-start | bytes 147456 | tf_op jit(solution)/shard_map/all_to_all | solution.py:81
  15.3 1.3 %collective-permute-start.1 = (bf16[96,3,128]{2,1,0:T(4,128)(2,1)S(1)}, bf16[96,3,128]{2,1,0:T(4,128)(2,1)S(1)}, u32[]{:S(2)}, u32[]{:S(2)}) collective-permute-start(bf16[96,3,128]{2,1,0:T(4,128)(2,1)S(1)} %slice.666), channel_id=1, source_target_pairs={{1,0},{3,2},{5,4},{7,6},{9,8},{11,10},{13,12},{15,14},{17,16},{19,... | collective-permute-start | bytes 221192 | tf_op jit(solution)/shard_map/ppermute | solution.py:17
  16.8 5.4 %all-to-all-done = bf16[16,2,1152]{2,1,0:T(2,128)(2,1)S(1)} async-done(((bf16[16,2,1152]{2,1,0:T(2,128)(2,1)}), bf16[16,2,1152]{2,1,0:T(2,128)(2,1)S(1)}, u32[]{:S(2)}, u32[]{:S(2)}) %all-to-all-start) | async-done | bytes 73760 | tf_op jit(solution)/shard_map/all_to_all | solution.py:81
  22.3 0.4 rev.13
  22.7 0.6 reduce.17
  23.3 0.7 reshape.172
  23.9 3.5 %all-to-all-start.1 = ((bf16[16,2,1152]{2,1,0:T(2,128)(2,1)}), bf16[16,2,1152]{2,1,0:T(2,128)(2,1)S(1)}, u32[]{:S(2)}, u32[]{:S(2)}) async-start(bf16[16,2,1152]{2,1,0:T(2,128)(2,1)} %reshape.172), calls=%async_computation.1 | async-start | bytes 147456 | tf_op jit(solution)/shard_map/all_to_all | solution.py:83
  27.5 7.0 %all-to-all-done.1 = bf16[16,2,1152]{2,1,0:T(2,128)(2,1)S(1)} async-done(((bf16[16,2,1152]{2,1,0:T(2,128)(2,1)}), bf16[16,2,1152]{2,1,0:T(2,128)(2,1)S(1)}, u32[]{:S(2)}, u32[]{:S(2)}) %all-to-all-start.1) | async-done | bytes 73760 | tf_op jit(solution)/shard_map/all_to_all | solution.py:83
  34.5 0.4 reduce.14
  35.0 0.1 copy.41
  35.3 4.4 %collective-permute-start.3 = (bf16[96,22,3]{0,1,2:T(8,128)(2,1)S(1)}, bf16[96,22,3]{0,1,2:T(8,128)(2,1)S(1)}, u32[]{:S(2)}, u32[]{:S(2)}) collective-permute-start(bf16[96,22,3]{0,1,2:T(8,128)(2,1)S(1)} %get-tuple-element.474), channel_id=1, source_target_pairs={{2,0},{4,2},{6,4},{8,6},{10,8},{12,10},{14,12},{16,14},{18,16},{20... | collective-permute-start | bytes 38024 | tf_op jit(solution)/shard_map/ppermute | solution.py:17
  39.9 1.3 %collective-permute-done.2 = bf16[96,22,3]{0,1,2:T(8,128)(2,1)S(1)} collective-permute-done((bf16[96,22,3]{0,1,2:T(8,128)(2,1)S(1)}, bf16[96,22,3]{0,1,2:T(8,128)(2,1)S(1)}, u32[]{:S(2)}, u32[]{:S(2)}) %collective-permute-start.2) | collective-permute-done | bytes 12704 | tf_op jit(solution)/shard_map/ppermute | solution.py:16
  41.2 0.4 maximum_convert_fusion
  41.6 7.8 %fusion.251 = f32[96,16,128]{0,1,2:T(8,128)S(1)} fusion(f32[96,22,134]{0,1,2:T(8,128)S(1)} %maximum_convert_fusion, f32[96]{0:T(128)S(1)} %get-tuple-element.531, f32[96]{0:T(128)S(1)} %get-tuple-element.532, f32[96]{0:T(128)S(1)} %get-tuple-element.533, f32[96]{0:T(128)S(1)} %get-tuple-element.534, f32[96]{0:T(128)S(1)} %get-tuple-element.535, ...), kind=kLoop, calls=%fused_computation.317 | loop fusion | flops 19267584 | bytes 39340800 | tf_op jit(solution)/shard_map/add | solution.py:30
  49.4 0.7 copy.43
  50.1 9.0 %while.26 = (s32[]{:T(128)}, bf16[96,16,128]{2,1,0:T(8,128)(2,1)S(1)}, s32[16,128]{1,0:T(8,128)S(1)}, bf16[96,16,128]{2,1,0:T(8,128)(2,1)S(1)}, f32[96,16,128]{2...) while((s32[]{:T(128)}, ...), condition=%wide.region_3.4_spmd, body=%wide.region_0.3_spmd.sunk | while | flops 178325504 | bytes 3745623 | solution.py:111
  50.5 4.1 %fusion.329 = bf16[12,8,8,128]{3,1,2,0:T(8,128)(2,1)S(1)} fusion(bf16[96,384]{1,0:T(8,128)(2,1)S(1)} %get-tuple-element.784, bf16[384,96]{1,0:T(8,128)(2,1)S(1)} %get-tuple-element.782, f32[384]{0:T(512)S(1)} %reduce.22, f32[12,8,8,128]{3,2,1,0:T(8,128)S(1)} %bitcast.552, f32[12,8,8,128]{3,2,1,0:T(8,128)S(1)} %bitcast.548, f32[96]{0:T(128)S(1)} %bitcast.564, ...), kind=kOutput, calls=%fused_computation.30.clone.1 | convolution fusion | flops 177831936 | bytes 1145472 | tf_op jit(solution)/shard_map/while/body/eval_jaxpr/dot_general | solution.py:58
  55.0 4.1 %fusion.329 = bf16[12,8,8,128]{3,1,2,0:T(8,128)(2,1)S(1)} fusion(bf16[96,384]{1,0:T(8,128)(2,1)S(1)} %get-tuple-element.784, bf16[384,96]{1,0:T(8,128)(2,1)S(1)} %get-tuple-element.782, f32[384]{0:T(512)S(1)} %reduce.22, f32[12,8,8,128]{3,2,1,0:T(8,128)S(1)} %bitcast.552, f32[12,8,8,128]{3,2,1,0:T(8,128)S(1)} %bitcast.548, f32[96]{0:T(128)S(1)} %bitcast.564, ...), kind=kOutput, calls=%fused_computation.30.clone.1 | convolution fusion | flops 177831936 | bytes 1145472 | tf_op jit(solution)/shard_map/while/body/eval_jaxpr/dot_general | solution.py:58
  59.2 0.6 copy.45
  59.9 0.2 rev.14
  60.3 1.0 reduce.18
  61.3 0.7 reshape.174
  61.9 5.8 %all-to-all-start.2 = ((bf16[16,2,1152]{2,1,0:T(2,128)(2,1)}), bf16[16,2,1152]{2,1,0:T(2,128)(2,1)S(1)}, u32[]{:S(2)}, u32[]{:S(2)}) async-start(bf16[16,2,1152]{2,1,0:T(2,128)(2,1)} %reshape.174), calls=%async_computation.2 | async-start | bytes 147456 | tf_op jit(solution)/shard_map/all_to_all | solution.py:81
  67.8 1.3 %collective-permute-start.5 = (bf16[96,3,128]{2,1,0:T(4,128)(2,1)S(1)}, bf16[96,3,128]{2,1,0:T(4,128)(2,1)S(1)}, u32[]{:S(2)}, u32[]{:S(2)}) collective-permute-start(bf16[96,3,128]{2,1,0:T(4,128)(2,1)S(1)} %slice.776), channel_id=1, source_target_pairs={{1,0},{3,2},{5,4},{7,6},{9,8},{11,10},{13,12},{15,14},{17,16},{19,... | collective-permute-start | bytes 221192 | tf_op jit(solution)/shard_map/ppermute | solution.py:17
  69.1 5.7 %all-to-all-done.2 = bf16[16,2,1152]{2,1,0:T(2,128)(2,1)S(1)} async-done(((bf16[16,2,1152]{2,1,0:T(2,128)(2,1)}), bf16[16,2,1152]{2,1,0:T(2,128)(2,1)S(1)}, u32[]{:S(2)}, u32[]{:S(2)}) %all-to-all-start.2) | async-done | bytes 73760 | tf_op jit(solution)/shard_map/all_to_all | solution.py:81
  74.8 0.4 rev.15
  75.2 0.6 reduce.19
  75.8 0.7 reshape.176
  76.5 3.5 %all-to-all-start.3 = ((bf16[16,2,1152]{2,1,0:T(2,128)(2,1)}), bf16[16,2,1152]{2,1,0:T(2,128)(2,1)S(1)}, u32[]{:S(2)}, u32[]{:S(2)}) async-start(bf16[16,2,1152]{2,1,0:T(2,128)(2,1)} %reshape.176), calls=%async_computation.3 | async-start | bytes 147456 | tf_op jit(solution)/shard_map/all_to_all | solution.py:83
  80.0 1.7 %collective-permute-start.4 = (bf16[96,3,128]{0,1,2:T(4,128)(2,1)S(1)}, bf16[96,3,128]{0,1,2:T(4,128)(2,1)S(1)}, u32[]{:S(2)}, u32[]{:S(2)}) collective-permute-start(bf16[96,3,128]{0,1,2:T(4,128)(2,1)S(1)} %slice.982), channel_id=1, source_target_pairs={{0,1},{2,3},{4,5},{6,7},{8,9},{10,11},{12,13},{14,15},{16,17},{18,... | collective-permute-start | bytes 221192 | tf_op jit(solution)/shard_map/ppermute | solution.py:16
  81.7 5.2 %all-to-all-done.3 = bf16[16,2,1152]{2,1,0:T(2,128)(2,1)S(1)} async-done(((bf16[16,2,1152]{2,1,0:T(2,128)(2,1)}), bf16[16,2,1152]{2,1,0:T(2,128)(2,1)S(1)}, u32[]{:S(2)}, u32[]{:S(2)}) %all-to-all-start.3) | async-done | bytes 73760 | tf_op jit(solution)/shard_map/all_to_all | solution.py:83
  87.0 0.4 reduce.15
  87.6 0.1 copy.50
  87.8 4.4 %collective-permute-start.7 = (bf16[96,22,3]{0,1,2:T(8,128)(2,1)S(1)}, bf16[96,22,3]{0,1,2:T(8,128)(2,1)S(1)}, u32[]{:S(2)}, u32[]{:S(2)}) collective-permute-start(bf16[96,22,3]{0,1,2:T(8,128)(2,1)S(1)} %get-tuple-element.472), channel_id=1, source_target_pairs={{2,0},{4,2},{6,4},{8,6},{10,8},{12,10},{14,12},{16,14},{18,16},{20... | collective-permute-start | bytes 38024 | tf_op jit(solution)/shard_map/ppermute | solution.py:17
  92.4 1.3 %collective-permute-done.6 = bf16[96,22,3]{0,1,2:T(8,128)(2,1)S(1)} collective-permute-done((bf16[96,22,3]{0,1,2:T(8,128)(2,1)S(1)}, bf16[96,22,3]{0,1,2:T(8,128)(2,1)S(1)}, u32[]{:S(2)}, u32[]{:S(2)}) %collective-permute-start.6) | collective-permute-done | bytes 12704 | tf_op jit(solution)/shard_map/ppermute | solution.py:16
  93.7 0.4 maximum_convert_fusion.1
  94.1 7.8 %fusion.202 = f32[96,16,128]{0,1,2:T(8,128)S(1)} fusion(f32[96,22,134]{0,1,2:T(8,128)S(1)} %maximum_convert_fusion.1, f32[96]{0:T(128)S(1)} %get-tuple-element.482, f32[96]{0:T(128)S(1)} %get-tuple-element.483, f32[96]{0:T(128)S(1)} %get-tuple-element.484, f32[96]{0:T(128)S(1)} %get-tuple-element.485, f32[96]{0:T(128)S(1)} %get-tuple-element.486, ...), kind=kLoop, calls=%fused_computation.219 | loop fusion | flops 19267584 | bytes 39340800 | tf_op jit(solution)/shard_map/add | solution.py:30
  101.9 0.7 copy.52
  102.6 9.0 %while.27 = (s32[]{:T(128)}, bf16[96,16,128]{2,1,0:T(8,128)(2,1)S(1)}, s32[16,128]{1,0:T(8,128)S(1)}, bf16[96,16,128]{2,1,0:T(8,128)(2,1)S(1)}, f32[96,16,128]{2...) while((s32[]{:T(128)}, ...), condition=%wide.region_7.8_spmd, body=%wide.region_4.7_spmd.sunk | while | flops 178325504 | bytes 3745623 | solution.py:111
  102.9 4.1 %fusion.335 = bf16[12,8,8,128]{3,1,2,0:T(8,128)(2,1)S(1)} fusion(bf16[96,384]{1,0:T(8,128)(2,1)S(1)} %get-tuple-element.832, bf16[384,96]{1,0:T(8,128)(2,1)S(1)} %get-tuple-element.830, f32[384]{0:T(512)S(1)} %reduce.23, f32[12,8,8,128]{3,2,1,0:T(8,128)S(1)} %bitcast.553, f32[12,8,8,128]{3,2,1,0:T(8,128)S(1)} %bitcast.549, f32[96]{0:T(128)S(1)} %bitcast.562, ...), kind=kOutput, calls=%fused_computation.139.clone.1 | convolution fusion | flops 177831936 | bytes 1145472 | tf_op jit(solution)/shard_map/while/body/eval_jaxpr/dot_general | solution.py:58
  107.4 4.1 %fusion.335 = bf16[12,8,8,128]{3,1,2,0:T(8,128)(2,1)S(1)} fusion(bf16[96,384]{1,0:T(8,128)(2,1)S(1)} %get-tuple-element.832, bf16[384,96]{1,0:T(8,128)(2,1)S(1)} %get-tuple-element.830, f32[384]{0:T(512)S(1)} %reduce.23, f32[12,8,8,128]{3,2,1,0:T(8,128)S(1)} %bitcast.553, f32[12,8,8,128]{3,2,1,0:T(8,128)S(1)} %bitcast.549, f32[96]{0:T(128)S(1)} %bitcast.562, ...), kind=kOutput, calls=%fused_computation.139.clone.1 | convolution fusion | flops 177831936 | bytes 1145472 | tf_op jit(solution)/shard_map/while/body/eval_jaxpr/dot_general | solution.py:58
  111.6 0.7 copy-done.1
  (103 shorter events, 3.4 us)
Async XLA Ops:
  0.0 15.2 %copy-start = (bf16[96,16,128]{2,1,0:T(8,128)(2,1)S(1)}, bf16[96,16,128]{2,1,0:T(8,128)(2,1)}, u32[]{:S(2)}) copy-start(bf16[96,16,128]{2,1,0:T(8,128)(2,1)} %param.14) | copy-start | bytes 1179652
  0.0 16.6 %copy-start.5 = (f32[2,96,7,7]{1,0,3,2:T(2,128)S(1)}, f32[2,96,7,7]{1,0,3,2:T(2,128)}, u32[]{:S(2)}) copy-start(f32[2,96,7,7]{1,0,3,2:T(2,128)} %param.16) | copy-start | bytes 112900
  0.0 16.7 %copy-start.3 = (bf16[2,384,96]{1,2,0:T(8,128)(2,1)S(1)}, bf16[2,384,96]{1,2,0:T(8,128)(2,1)}, u32[]{:S(2)}) copy-start(bf16[2,384,96]{1,2,0:T(8,128)(2,1)} %param.20) | copy-start | bytes 442372
  0.0 16.7 %copy-start.4 = (bf16[2,96,384]{2,1,0:T(8,128)(2,1)S(1)}, bf16[2,96,384]{2,1,0:T(8,128)(2,1)}, u32[]{:S(2)}) copy-start(bf16[2,96,384]{2,1,0:T(8,128)(2,1)} %param.22) | copy-start | bytes 442372
  0.0 16.8 %copy-start.6 = (f32[2,384]{1,0:T(2,128)S(1)}, f32[2,384]{1,0:T(2,128)}, u32[]{:S(2)}) copy-start(f32[2,384]{1,0:T(2,128)} %param.21) | copy-start | bytes 9220
  0.0 16.8 %copy-start.10 = (f32[2,96]{1,0:T(2,128)S(1)}, f32[2,96]{1,0:T(2,128)}, u32[]{:S(2)}) copy-start(f32[2,96]{1,0:T(2,128)} %param.19) | copy-start | bytes 2308
  0.0 16.8 %copy-start.9 = (f32[2,96]{1,0:T(2,128)S(1)}, f32[2,96]{1,0:T(2,128)}, u32[]{:S(2)}) copy-start(f32[2,96]{1,0:T(2,128)} %param.23) | copy-start | bytes 2308
  1.8 33.4 %collective-permute-start = (bf16[96,3,128]{0,1,2:T(4,128)(2,1)S(1)}, bf16[96,3,128]{0,1,2:T(4,128)(2,1)S(1)}, u32[]{:S(2)}, u32[]{:S(2)}) collective-permute-start(bf16[96,3,128]{0,1,2:T(4,128)(2,1)S(1)} %slice.883), channel_id=1, source_target_pairs={{0,1},{2,3},{4,5},{6,7},{8,9},{10,11},{12,13},{14,15},{16,17},{18,... | collective-permute-start | bytes 221192 | tf_op jit(solution)/shard_map/ppermute | solution.py:16
  6.9 20.6 %copy-start.7 = (f32[2,96]{1,0:T(2,128)S(1)}, f32[2,96]{1,0:T(2,128)}, u32[]{:S(2)}) copy-start(f32[2,96]{1,0:T(2,128)} %param.17) | copy-start | bytes 2308
  9.3 13.0 %all-to-all-start = ((bf16[16,2,1152]{2,1,0:T(2,128)(2,1)}), bf16[16,2,1152]{2,1,0:T(2,128)(2,1)S(1)}, u32[]{:S(2)}, u32[]{:S(2)}) async-start(bf16[16,2,1152]{2,1,0:T(2,128)(2,1)} %reshape.170), calls=%async_computation | async-start | bytes 147456 | tf_op jit(solution)/shard_map/all_to_all | solution.py:81
  15.3 19.7 %collective-permute-start.1 = (bf16[96,3,128]{2,1,0:T(4,128)(2,1)S(1)}, bf16[96,3,128]{2,1,0:T(4,128)(2,1)S(1)}, u32[]{:S(2)}, u32[]{:S(2)}) collective-permute-start(bf16[96,3,128]{2,1,0:T(4,128)(2,1)S(1)} %slice.666), channel_id=1, source_target_pairs={{1,0},{3,2},{5,4},{7,6},{9,8},{11,10},{13,12},{15,14},{17,16},{19,... | collective-permute-start | bytes 221192 | tf_op jit(solution)/shard_map/ppermute | solution.py:17
  16.8 22.9 %copy-start.8 = (f32[2,96]{1,0:T(2,128)S(1)}, f32[2,96]{1,0:T(2,128)}, u32[]{:S(2)}) copy-start(f32[2,96]{1,0:T(2,128)} %param.18) | copy-start | bytes 2308
  23.9 10.5 %all-to-all-start.1 = ((bf16[16,2,1152]{2,1,0:T(2,128)(2,1)}), bf16[16,2,1152]{2,1,0:T(2,128)(2,1)S(1)}, u32[]{:S(2)}, u32[]{:S(2)}) async-start(bf16[16,2,1152]{2,1,0:T(2,128)(2,1)} %reshape.172), calls=%async_computation.1 | async-start | bytes 147456 | tf_op jit(solution)/shard_map/all_to_all | solution.py:83
  35.2 5.9 %collective-permute-start.2 = (bf16[96,22,3]{0,1,2:T(8,128)(2,1)S(1)}, bf16[96,22,3]{0,1,2:T(8,128)(2,1)S(1)}, u32[]{:S(2)}, u32[]{:S(2)}) collective-permute-start(bf16[96,22,3]{0,1,2:T(8,128)(2,1)S(1)} %get-tuple-element.473), channel_id=1, source_target_pairs={{0,2},{2,4},{4,6},{6,8},{8,10},{10,12},{12,14},{14,16},{16,18},{18... | collective-permute-start | bytes 38024 | tf_op jit(solution)/shard_map/ppermute | solution.py:16
  35.3 5.9 %collective-permute-start.3 = (bf16[96,22,3]{0,1,2:T(8,128)(2,1)S(1)}, bf16[96,22,3]{0,1,2:T(8,128)(2,1)S(1)}, u32[]{:S(2)}, u32[]{:S(2)}) collective-permute-start(bf16[96,22,3]{0,1,2:T(8,128)(2,1)S(1)} %get-tuple-element.474), channel_id=1, source_target_pairs={{2,0},{4,2},{6,4},{8,6},{10,8},{12,10},{14,12},{16,14},{18,16},{20... | collective-permute-start | bytes 38024 | tf_op jit(solution)/shard_map/ppermute | solution.py:17
  49.4 0.7 copy-start.2
  61.9 12.8 %all-to-all-start.2 = ((bf16[16,2,1152]{2,1,0:T(2,128)(2,1)}), bf16[16,2,1152]{2,1,0:T(2,128)(2,1)S(1)}, u32[]{:S(2)}, u32[]{:S(2)}) async-start(bf16[16,2,1152]{2,1,0:T(2,128)(2,1)} %reshape.174), calls=%async_computation.2 | async-start | bytes 147456 | tf_op jit(solution)/shard_map/all_to_all | solution.py:81
  67.8 19.7 %collective-permute-start.5 = (bf16[96,3,128]{2,1,0:T(4,128)(2,1)S(1)}, bf16[96,3,128]{2,1,0:T(4,128)(2,1)S(1)}, u32[]{:S(2)}, u32[]{:S(2)}) collective-permute-start(bf16[96,3,128]{2,1,0:T(4,128)(2,1)S(1)} %slice.776), channel_id=1, source_target_pairs={{1,0},{3,2},{5,4},{7,6},{9,8},{11,10},{13,12},{15,14},{17,16},{19,... | collective-permute-start | bytes 221192 | tf_op jit(solution)/shard_map/ppermute | solution.py:17
  76.5 10.5 %all-to-all-start.3 = ((bf16[16,2,1152]{2,1,0:T(2,128)(2,1)}), bf16[16,2,1152]{2,1,0:T(2,128)(2,1)S(1)}, u32[]{:S(2)}, u32[]{:S(2)}) async-start(bf16[16,2,1152]{2,1,0:T(2,128)(2,1)} %reshape.176), calls=%async_computation.3 | async-start | bytes 147456 | tf_op jit(solution)/shard_map/all_to_all | solution.py:83
  80.0 7.7 %collective-permute-start.4 = (bf16[96,3,128]{0,1,2:T(4,128)(2,1)S(1)}, bf16[96,3,128]{0,1,2:T(4,128)(2,1)S(1)}, u32[]{:S(2)}, u32[]{:S(2)}) collective-permute-start(bf16[96,3,128]{0,1,2:T(4,128)(2,1)S(1)} %slice.982), channel_id=1, source_target_pairs={{0,1},{2,3},{4,5},{6,7},{8,9},{10,11},{12,13},{14,15},{16,17},{18,... | collective-permute-start | bytes 221192 | tf_op jit(solution)/shard_map/ppermute | solution.py:16
  87.7 5.9 %collective-permute-start.6 = (bf16[96,22,3]{0,1,2:T(8,128)(2,1)S(1)}, bf16[96,22,3]{0,1,2:T(8,128)(2,1)S(1)}, u32[]{:S(2)}, u32[]{:S(2)}) collective-permute-start(bf16[96,22,3]{0,1,2:T(8,128)(2,1)S(1)} %get-tuple-element.471), channel_id=1, source_target_pairs={{0,2},{2,4},{4,6},{6,8},{8,10},{10,12},{12,14},{14,16},{16,18},{18... | collective-permute-start | bytes 38024 | tf_op jit(solution)/shard_map/ppermute | solution.py:16
  87.8 5.9 %collective-permute-start.7 = (bf16[96,22,3]{0,1,2:T(8,128)(2,1)S(1)}, bf16[96,22,3]{0,1,2:T(8,128)(2,1)S(1)}, u32[]{:S(2)}, u32[]{:S(2)}) collective-permute-start(bf16[96,22,3]{0,1,2:T(8,128)(2,1)S(1)} %get-tuple-element.472), channel_id=1, source_target_pairs={{2,0},{4,2},{6,4},{8,6},{10,8},{12,10},{14,12},{16,14},{18,16},{20... | collective-permute-start | bytes 38024 | tf_op jit(solution)/shard_map/ppermute | solution.py:17
  111.6 0.7 copy-start.1
where the time goes:
time: 113 us; the launch traced here: 112 us
  starting transfers between devices  36.9 us (33%)
  waiting for transfers between devices  25.9 us (23%)
  other arithmetic  21.7 us (19%)
  matrix products  16.2 us (14%)
  local copies, waits for them, and re-layouts  10.8 us (10%)
    dot_general x4, matrix products, finish(): jnp.dot(w_reduce, hidden, preferred_element_type=jnp.float32)  16.2 us
    add x2, other arithmetic, depthwise(): summed + kernel[:, shift_row, shift_col, None, None] * band_rows[:, shift...  15.6 us
    all_to_all x2, waiting for transfers between devices, convnext_layer(): lax.all_to_all(spread, 'lon', split_axis=0, concat_axis=0, tiled=True)  12.2 us
    all_to_all x2, starting transfers between devices, convnext_layer(): lax.all_to_all(pieces, 'lon', split_axis=0, concat_axis=0, tiled=True)  11.7 us
    ppermute x4, starting transfers between devices, extended_2(): after = lax.ppermute(leading, axis, down)  11.4 us
    all_to_all x2, waiting for transfers between devices, convnext_layer(): lax.all_to_all(pieces, 'lon', split_axis=0, concat_axis=0, tiled=True)  11.1 us
    all_to_all x2, starting transfers between devices, convnext_layer(): lax.all_to_all(spread, 'lon', split_axis=0, concat_axis=0, tiled=True)  7.01 us
    ppermute x4, starting transfers between devices, extended_2(): before = lax.ppermute(last, axis, up)  6.69 us
  transfers between devices with their start and end apart: 12, of which 6 were waited for; matrix products, arithmetic and copies ran while one was open for 7% of the time, Pallas kernels for 0%

commit v1 on v0

v1 whole, which is shorter than its diff:
```python
import functools

import jax
import jax.numpy as jnp
from jax import lax
from jax.experimental import pallas as pl
from jax.experimental.pallas import tpu as pltpu
from jax.sharding import PartitionSpec as P


HALO = 6
VMEM_LIMIT = 20 * 1024 * 1024


def params():
    return pltpu.CompilerParams(vmem_limit_bytes=VMEM_LIMIT)


def cost(flops):
    return pl.CostEstimate(flops=int(flops), bytes_accessed=1 << 20, transcendentals=0)


def vmem(count):
    return [pl.BlockSpec(memory_space=pltpu.VMEM)] * count


def lanes(shape):
    return lax.broadcasted_iota(jnp.int32, shape, len(shape) - 1)


def first_step(out_ref):
    out_ref[...] = jnp.zeros_like(out_ref)


def pack_rows(upper_if_even, field_ref, mask_ref, after_ref, out_ref, wide, wide_mask):
    del after_ref
    channels, rows, width = field_ref.shape
    even = lax.rem(lax.axis_index("lat"), 2) == 0
    take_upper = even if upper_if_even else jnp.logical_not(even)
    wide[...] = field_ref[...].astype(jnp.float32).reshape(channels * rows, width)
    wide_mask[...] = mask_ref[...].astype(jnp.float32)
    for k in range(HALO):
        lower = wide[pl.ds(k, channels, stride=rows), :]
        upper = wide[pl.ds(rows - HALO + k, channels, stride=rows), :]
        at = pl.ds(k * channels, channels)
        out_ref[at, :] = jnp.where(take_upper, upper, lower).astype(jnp.bfloat16)
    pad = jnp.zeros((16 - HALO, width), jnp.float32)
    lower = jnp.concatenate([wide_mask[0:HALO, :], pad], axis=0)
    upper = jnp.concatenate([wide_mask[rows - HALO : rows, :], pad], axis=0)
    at = pl.ds(HALO * channels, 16)
    out_ref[at, :] = jnp.where(take_upper, upper, lower).astype(jnp.bfloat16)


def south_place(k):
    return k - 3 if k >= 3 else 8 + k


def channel_of(channels, group, slot):
    return slot // 4 * (channels // 4) + group * 4 + slot % 4


def join_rows(
    field_ref,
    mask_ref,
    first_ref,
    second_ref,
    after_ref,
    halo_ref,
    halo_mask_ref,
    core_ref,
    cross_ref,
    wide,
):
    del after_ref
    channels, rows, width = field_ref.shape
    lat = lax.axis_index("lat")
    even = lax.rem(lat, 2) == 0
    folded = lat == lax.axis_size("lat") - 1
    lon_even = lax.rem(lax.axis_index("lon"), 2) == 0
    wide[...] = jnp.zeros_like(wide)
    halo_mask_ref[...] = jnp.zeros_like(halo_mask_ref)
    sub = lax.broadcasted_iota(jnp.int32, (width, width), 0)
    target = lanes((width, width))
    turn = sub == jnp.where(folded, width - 1 - target, target)
    turn = turn.astype(jnp.float32).astype(jnp.bfloat16)

    def split(one, two):
        north = jnp.where(even, one, two)
        south = jnp.where(even, two, one)
        north = jnp.dot(north, turn, preferred_element_type=jnp.float32)
        return north, south.astype(jnp.float32)

    at = slice(HALO * channels, HALO * channels + 16)
    mask_north, mask_south = split(first_ref[at, :], second_ref[at, :])
    for k in range(HALO):
        at = slice(k * channels, (k + 1) * channels)
        north, south = split(first_ref[at, :], second_ref[at, :])
        beyond = jnp.where(folded, HALO - 1 - k, k)
        place = jnp.where(beyond < 3, 4 + beyond, 9 + beyond)
        wide[pl.ds(place, channels, stride=16), :] = north
        wide[pl.ds(south_place(k), channels, stride=16), :] = south
        halo_mask_ref[pl.ds(place, 1), :] = mask_north[k : k + 1, :]
        halo_mask_ref[south_place(k) : south_place(k) + 1, :] = mask_south[k : k + 1, :]
    halo_ref[...] = wide[...].astype(jnp.bfloat16).reshape(channels, 16, width)

    lane = lanes((32, width))
    slots = [(lane >= 8 * q) & (lane < 8 * q + HALO) for q in range(16)]

    def group(blocks):
        west = jnp.zeros((32, width), jnp.bfloat16)
        east = jnp.zeros((32, width), jnp.bfloat16)
        for q, block in enumerate(blocks):
            west = jnp.where(slots[q], pltpu.roll(block, 8 * q, 1), west)
            east = jnp.where(slots[q], pltpu.roll(block, (8 * q + HALO) % width, 1), east)
        return jnp.where(lon_even, east, west), jnp.where(lon_even, west, east)

    for g in range(channels // 16):
        blocks = []
        for q in range(16):
            c = channel_of(channels, g, q)
            blocks.append(jnp.concatenate([field_ref[c], halo_ref[c]], axis=0))
        core_ref[g * 32 : g * 32 + 32, :], cross_ref[g * 32 : g * 32 + 32, :] = group(blocks)
    mask_block = jnp.concatenate(
        [mask_ref[...].astype(jnp.float32), halo_mask_ref[...]], axis=0
    ).astype(jnp.bfloat16)
    core_ref[channels * 2 :, :], cross_ref[channels * 2 :, :] = group([mask_block])


def in_row(place, first_layer):
    none = jnp.full_like(place, 1000)
    row = jnp.where(place < 16, place, none)
    row = jnp.where((place >= 16) & (place < 19), place - 19, row)
    row = jnp.where((place >= 20) & (place < 23), place - 4, row)
    if first_layer:
        row = jnp.where((place >= 24) & (place < 27), place - 30, row)
        row = jnp.where((place >= 28) & (place < 31), place - 9, row)
    return row


EDGE = (-3, -2, -1, 16, 17, 18, 0, 1, 2, 13, 14, 15)
INNER = (3, 4, 5, 6, 7, 8, 9, 10, 11, 12)


def place_of(row):
    if row < 0:
        return row + 19
    return row if row < 16 else row + 4


def conv_matrices(table, out_ref, left, right, row, rows_out):
    channels, taps = table.shape
    count = len(rows_out)
    folded = lax.axis_index("lat") == lax.axis_size("lat") - 1
    k = lanes((1, 256))
    shift = k // 32
    place = k - shift * 32
    tap = lax.broadcasted_iota(jnp.int32, (taps, 256), 0)
    row = row(place)
    for i, here in enumerate(rows_out):
        if here is None:
            wanted = jnp.full_like(k, -1)
        else:
            a = row - here + 3
            inside = (a >= 0) & (a <= 6) & (shift < 7)
            wanted = a * 7 + shift
            if here > 15:
                wanted = jnp.where(folded, 48 - wanted, wanted)
            wanted = jnp.where(inside, wanted, -1)
            wanted = jnp.where((shift == 7) & (place < 3), 49 + place, wanted)
        picks = (tap == wanted).astype(jnp.float32).astype(jnp.bfloat16)
        matrix = jnp.dot(table, picks, preferred_element_type=jnp.float32)
        left[pl.ds(i, channels, stride=count), :] = matrix[:, :128]
        right[pl.ds(i, channels, stride=count), :] = matrix[:, 128:]
    size = channels * count
    out_ref[:, :128] = left[:size, :].astype(jnp.bfloat16)
    out_ref[:, 128:] = right[:size, :].astype(jnp.bfloat16)


def split_bias(bias):
    high = bias.astype(jnp.bfloat16).astype(jnp.float32)
    rest = bias - high
    mid = rest.astype(jnp.bfloat16).astype(jnp.float32)
    return high, mid, rest - mid


def weights(
    kernel_ref,
    bias_ref,
    gain_ref,
    norm_bias_ref,
    expand_ref,
    expand_bias_ref,
    reduce_bias_ref,
    one_ref,
    two_ref,
    rows_ref,
    expand_out_ref,
    left,
    right,
    turn,
    tall,
):
    taps, layers, channels = kernel_ref.shape
    hidden = expand_ref.shape[2]
    turn[...] = jnp.zeros_like(turn)
    tall[...] = jnp.zeros_like(tall)
    for layer in range(layers):
        for tap in range(taps):
            turn[tap : tap + 1, :channels] = kernel_ref[tap, layer : layer + 1, :]
        parts = split_bias(bias_ref[layer : layer + 1, :])
        for n, part in enumerate(parts):
            turn[taps + n : taps + n + 1, :channels] = part
        table = turn[...].T[:channels, :64].astype(jnp.bfloat16)
        if layer == 0:
            every = EDGE + INNER + (None,) * 2
            row = functools.partial(in_row, first_layer=True)
            conv_matrices(table, one_ref, left, right, row, every)
        else:
            row = functools.partial(in_row, first_layer=False)
            conv_matrices(table, two_ref, left, right, row, tuple(range(16)))
    for layer in range(layers):
        for n, ref in enumerate((gain_ref, norm_bias_ref, reduce_bias_ref)):
            turn[:, :channels] = jnp.broadcast_to(ref[layer : layer + 1, :], (128, channels))
            rows_ref[layer, n] = turn[...].T[:channels, :]
        tall[:channels, :] = expand_ref[layer].astype(jnp.float32) * 0.5
        parts = split_bias(expand_bias_ref[layer : layer + 1, :] * 0.5)
        for n, part in enumerate(parts):
            tall[channels + n : channels + n + 1, :] = part
        for n in range(hidden // 128):
            piece = tall[:, n * 128 : (n + 1) * 128].T
            at = pl.ds(n * 128, 128)
            expand_out_ref[layer, at, :] = piece[:, : channels + 16].astype(jnp.bfloat16)


ERF = (7.97869712e-01, 3.63922860e-02, -8.78263977e-05, -3.66934787e-05, 1.42500782e-06)


def gelu_of_double(half):
    square = half * half
    total = jnp.full_like(half, 2.0 * 4.0 ** (len(ERF) - 1) * ERF[-1])
    for power in range(len(ERF) - 2, -1, -1):
        total = total * square + jnp.full_like(half, 2.0 * 4.0**power * ERF[power])
    return half * jnp.tanh(half * total) + half


def norm(rows_ref, layer, cells):
    average = jnp.mean(cells, axis=0, keepdims=True)
    centered = cells - average
    variance = jnp.mean(centered * centered, axis=0, keepdims=True)
    scaled = centered * lax.rsqrt(variance + 1e-06)
    return (scaled * rows_ref[layer, 0] + rows_ref[layer, 1]).astype(jnp.bfloat16)


def mlp(rows_ref, expand_ref, reduce_ref, layer, blocks, normed_ref, inner_ref, put):
    count = len(blocks)
    channels, width = rows_ref.shape[2:]
    hidden = inner_ref.shape[0]
    wide = count * width
    normed_ref[channels:, :wide] = jnp.ones((16, wide), jnp.bfloat16)
    for n, block in enumerate(blocks):
        at = slice(n * width, (n + 1) * width)
        normed_ref[:channels, at] = norm(rows_ref, layer, block())
    tiles = [slice(n, min(n + 2 * width, wide)) for n in range(0, wide, 2 * width)]
    for at in tiles:
        normed = normed_ref[:, at]
        for part in range(0, hidden, 128):
            matrix = expand_ref[layer, part : part + 128, :]
            half = jnp.dot(matrix, normed, preferred_element_type=jnp.float32)
            for k in range(0, 128, 16):
                values = gelu_of_double(half[k : k + 16, :].astype(jnp.bfloat16))
                inner_ref[part + k : part + k + 16, at] = values
    extra = rows_ref[layer, 2]
    for t, at in enumerate(tiles):
        change = jnp.dot(reduce_ref[layer], inner_ref[:, at], preferred_element_type=jnp.float32)
        for n in range((at.stop - at.start) // width):
            put(t * 2 + n, change[:, n * width : (n + 1) * width] + extra)


def columns_stack(block, ones):
    width = block.shape[1]
    stack = [block if s == 0 else pltpu.roll(block, (-s) % width, 1) for s in range(-3, 4)]
    return jnp.concatenate(stack + [ones], axis=0)


def conv_rows(matrix_ref, stack_of, conv, channels, stride, first, count):
    ones = jnp.ones((matrix_ref.shape[1] // 8, 128), jnp.bfloat16)

    def step(c, carry):
        matrix = matrix_ref[pl.ds(pl.multiple_of(c * stride + first, 8), count), :]
        result = jnp.dot(matrix, stack_of(c, ones), preferred_element_type=jnp.float32)
        conv[pl.ds(c, count, stride=channels), :] = result
        return carry

    lax.fori_loop(0, channels, step, 0, unroll=channels)


def conv_row(conv, channels, i):
    return lambda: conv[i * channels : (i + 1) * channels, :]


def inner_rows(
    field_ref, matrix_ref, rows_ref, expand_ref, reduce_ref, update_ref, conv, normed, inner
):
    channels, rows, width = field_ref.shape
    none = jnp.zeros((16, width), jnp.bfloat16)

    def stack_of(c, ones):
        return columns_stack(jnp.concatenate([field_ref[c], none], axis=0), ones)

    conv_rows(matrix_ref, stack_of, conv, channels, 24, 8, 16)

    def put(n, change):
        update_ref[pl.ds(INNER[n], channels, stride=24), :] = change

    blocks = [conv_row(conv, channels, i + len(EDGE) - 8) for i in range(len(INNER))]
    mlp(rows_ref, expand_ref, reduce_ref, 0, blocks, normed, inner, put)


def edge_rows(
    field_ref,
    halo_ref,
    matrix_ref,
    rows_ref,
    expand_ref,
    reduce_ref,
    old_ref,
    update_ref,
    conv,
    normed,
    inner,
):
    del old_ref
    channels, _, width = field_ref.shape

    def stack_of(c, ones):
        return columns_stack(jnp.concatenate([field_ref[c], halo_ref[c]], axis=0), ones)

    conv_rows(matrix_ref, stack_of, conv, channels, 24, 0, 16)
    for empty in (19, 23):
        update_ref[pl.ds(empty, channels, stride=24), :] = jnp.zeros((channels, width), jnp.float32)

    def put(n, change):
        update_ref[pl.ds(place_of(EDGE[n]), channels, stride=24), :] = change

    blocks = [conv_row(conv, channels, i) for i in range(len(EDGE))]
    mlp(rows_ref, expand_ref, reduce_ref, 0, blocks, normed, inner, put)


def by_side(core, cross):
    lon_even = lax.rem(lax.axis_index("lon"), 2) == 0
    return jnp.where(lon_even, core, cross), jnp.where(lon_even, cross, core)


def edge_columns(
    core_ref,
    cross_ref,
    core_sent_ref,
    cross_sent_ref,
    matrix_ref,
    rows_ref,
    expand_ref,
    reduce_ref,
    strips,
    conv,
    normed,
    inner,
):
    channels, width = rows_ref.shape[2:]
    quarter = channels // 4
    groups = channels // 16
    lane32 = lanes((32, width))
    within = lane32 % 32
    in_west, in_own_west, in_own_east = within < 6, within < 12, within < 18
    ones = jnp.ones((32, width), jnp.bfloat16)
    for g in range(groups):
        at = slice(g * 32, g * 32 + 32)
        east, west = by_side(core_ref[at, :], cross_ref[at, :])
        own_east, own_west = by_side(core_sent_ref[at, :], cross_sent_ref[at, :])
        for t in range(4):
            parts = [
                pltpu.roll(part, (6 * n - 8 * t) % width, 1)
                for n, part in enumerate((west, own_west, own_east, east))
            ]
            block = jnp.where(in_own_east, parts[2], parts[3])
            block = jnp.where(in_own_west, parts[1], block)
            block = jnp.where(in_west, parts[0], block)
            some = [channel_of(channels, g, 4 * n + t) for n in range(4)]
            matrix = jnp.concatenate(
                [matrix_ref[c * 24 : c * 24 + 24, :] for c in some], axis=0
            )
            stack = columns_stack(block, ones)
            result = jnp.dot(matrix, stack, preferred_element_type=jnp.float32)
            for n, c in enumerate(some):
                conv[pl.ds(c, 24, stride=channels), :] = result[n * 24 : n * 24 + 24, :]

    order = {place_of(row): i for i, row in enumerate(EDGE + INNER)}
    slot = lanes((quarter, width)) // 8
    packs = []
    for p in range(3):
        parts = []
        for n in range(4):
            packed = jnp.zeros((quarter, width), jnp.float32)
            for q in range(8):
                if p * 8 + q in order:
                    start = order[p * 8 + q] * channels + n * quarter
                    block = conv[start : start + quarter, :]
                    near = pltpu.roll(block, (53 - 8 * q - 32 * n) % width, 1)
                    far = pltpu.roll(block, (105 - 8 * q - 32 * n) % width, 1)
                    packed = jnp.where(slot == 7 - q, near, packed)
                    packed = jnp.where(slot == 15 - q, far, packed)
            parts.append(packed)
        packs.append(jnp.concatenate(parts, axis=0))

    def put(p, change):
        for q in range(8):
            near = pltpu.roll(change, (69 + 8 * q) % width, 1)
            strips[pl.ds(p * 8 + q, channels, stride=24), :] = near

    blocks = [functools.partial(lambda block: block, packed) for packed in packs]
    mlp(rows_ref, expand_ref, reduce_ref, 0, blocks, normed, inner, put)


def second_layer(
    field_ref,
    mask_ref,
    halo_ref,
    halo_mask_ref,
    core_ref,
    cross_ref,
    strips,
    update_ref,
    matrix_ref,
    rows_ref,
    expand_ref,
    reduce_ref,
    out_ref,
    main_ref,
    conv,
    normed,
    inner,
):
    channels, rows, width = out_ref.shape
    half = width // 2
    groups = channels // 16
    lane32 = lanes((32, width))
    lane24 = lanes((24, width))
    to_east = lane32 < half

    def beside_of(east, west, q):
        east = pltpu.roll(east, (width - 8 * q) % width, 1)
        west = pltpu.roll(west, width - HALO - 8 * q, 1)
        return jnp.where(to_east, east, west).astype(jnp.float32)[0:24, :]

    def received(g):
        at = slice(g * 32, g * 32 + 32)
        return by_side(core_ref[at, :], cross_ref[at, :])

    main_mask = jnp.concatenate(
        [mask_ref[...].astype(jnp.float32), halo_mask_ref[0:8, :]], axis=0
    )
    side_mask = beside_of(*received(groups), 0)
    low = lane24 < 3
    high = lane24 >= width - 3
    blank = jnp.zeros((8, width), jnp.float32)
    ones = jnp.ones((32, width), jnp.bfloat16)
    away = {s: lane32 < s if s > 0 else lane32 >= width + s for s in range(-3, 4) if s}
    for g in range(groups):
        east, west = received(g)
        for q in range(16):
            c = channel_of(channels, g, q)
            near = strips[c * 24 : c * 24 + 24, :]
            far = pltpu.roll(near, half, 1)
            change = update_ref[c * 24 : c * 24 + 24, :]
            change = jnp.where(low, near, jnp.where(high, far, change))
            old = jnp.concatenate([field_ref[c], halo_ref[c]], axis=0).astype(jnp.float32)
            main = main_mask * (old[:24, :] + change)
            main = jnp.concatenate([main, blank], axis=0).astype(jnp.bfloat16)
            main_ref[c] = main[:rows, :]
            change = jnp.where(high, near, far)
            beside = side_mask * (beside_of(east, west, q) + change)
            beside = jnp.concatenate([beside, blank], axis=0).astype(jnp.bfloat16)
            stack = []
            for s in range(-3, 4):
                moved = main
                if s:
                    moved = pltpu.roll(jnp.where(away[s], beside, main), (-s) % width, 1)
                stack.append(moved)
            stack = jnp.concatenate(stack + [ones], axis=0)
            matrix = matrix_ref[c * 16 : c * 16 + 16, :]
            result = jnp.dot(matrix, stack, preferred_element_type=jnp.float32)
            conv[pl.ds(c, 16, stride=channels), :] = result

    mask = mask_ref[...].astype(jnp.float32)
    changes = []

    def put(n, change):
        changes.append(change)
        if n < rows - 1:
            return
        for c in range(0, channels, 8):
            parts = []
            for half in range(0, rows, 8):
                part = [changes[i][c : c + 8, :] for i in range(half, half + 8)]
                parts.append(jnp.swapaxes(jnp.stack(part, axis=0), 0, 1))
            change = jnp.concatenate(parts, axis=1)
            old = main_ref[c : c + 8].astype(jnp.float32)
            out_ref[c : c + 8] = (mask[None] * (old + change)).astype(jnp.bfloat16)

    blocks = [conv_row(conv, channels, i) for i in range(rows)]
    mlp(rows_ref, expand_ref, reduce_ref, 1, blocks, normed, inner, put)


def per_device(
    nlat,
    nlon,
    field,
    land_mask,
    depth_kernel,
    depth_bias,
    norm_gain,
    norm_bias,
    w_expand,
    b_expand,
    w_reduce,
    b_reduce,
):
    channels, rows, width = field.shape
    layers, hidden = b_expand.shape
    bf16, f32 = jnp.bfloat16, jnp.float32
    edge = HALO * channels + 16

    def buffers(count):
        return [
            pltpu.VMEM((channels + 16, count * width), bf16),
            pltpu.VMEM((hidden, count * width), bf16),
        ]

    def pack(upper_if_even, after):
        return pl.pallas_call(
            functools.partial(pack_rows, upper_if_even),
            out_shape=jax.ShapeDtypeStruct((edge, width), bf16),
            in_specs=vmem(2) + [pl.BlockSpec(memory_space=pl.ANY)],
            out_specs=pl.BlockSpec(memory_space=pltpu.VMEM),
            scratch_shapes=[
                pltpu.VMEM((channels * rows, width), f32),
                pltpu.VMEM((rows, width), f32),
            ],
            compiler_params=params(),
            cost_estimate=cost(4e9),
        )(field, land_mask, after)

    begun = pl.pallas_call(
        first_step,
        out_shape=jax.ShapeDtypeStruct((8, 128), f32),
        out_specs=pl.BlockSpec(memory_space=pltpu.VMEM),
        compiler_params=params(),
        cost_estimate=cost(4e9),
    )()
    first = pack(True, begun)
    second = pack(False, first)

    pairs = []
    for d in range(nlon):
        at = d * nlat
        for low in range(1, nlat - 1, 2):
            pairs += [(at + low, at + low + 1), (at + low + 1, at + low)]
        pairs.append((at + nlat - 1, (nlon - 1 - d) * nlat + nlat - 1))
    second = lax.ppermute(second, ("lon", "lat"), pairs)
    pairs = []
    for low in range(0, nlat - 1, 2):
        pairs += [(low, low + 1), (low + 1, low)]
    first = lax.ppermute(first, "lat", pairs)

    kernel = depth_kernel.transpose(2, 3, 0, 1).reshape(49, layers, channels)
    matrix_one, matrix_two, by_channel, expand = pl.pallas_call(
        weights,
        out_shape=[
            jax.ShapeDtypeStruct((channels * 24, 256), bf16),
            jax.ShapeDtypeStruct((channels * 16, 256), bf16),
            jax.ShapeDtypeStruct((layers, 3, channels, 128), f32),
            jax.ShapeDtypeStruct((layers, hidden, channels + 16), bf16),
        ],
        in_specs=vmem(7),
        out_specs=vmem(4),
        scratch_shapes=[
            pltpu.VMEM((channels * 24, 128), f32),
            pltpu.VMEM((channels * 24, 128), f32),
            pltpu.VMEM((128, 128), f32),
            pltpu.VMEM((128, hidden), f32),
        ],
        compiler_params=params(),
        cost_estimate=cost(2e9),
    )(
        kernel,
        depth_bias,
        norm_gain,
        norm_bias,
        w_expand.transpose(0, 2, 1),
        b_expand,
        b_reduce,
    )
    update = pl.pallas_call(
        inner_rows,
        out_shape=jax.ShapeDtypeStruct((channels * 24, width), f32),
        in_specs=vmem(5),
        out_specs=pl.BlockSpec(memory_space=pltpu.VMEM),
        scratch_shapes=[pltpu.VMEM((channels * 16, width), f32)] + buffers(len(INNER)),
        compiler_params=params(),
        cost_estimate=cost(4e9),
    )(field, matrix_one, by_channel, expand, w_reduce)

    strip_rows = (channels // 16 + 1) * 32
    halo, halo_mask, core, cross = pl.pallas_call(
        join_rows,
        out_shape=[
            jax.ShapeDtypeStruct((channels, 16, width), bf16),
            jax.ShapeDtypeStruct((16, width), f32),
            jax.ShapeDtypeStruct((strip_rows, width), bf16),
            jax.ShapeDtypeStruct((strip_rows, width), bf16),
        ],
        in_specs=vmem(4) + [pl.BlockSpec(memory_space=pl.ANY)],
        out_specs=vmem(4),
        scratch_shapes=[pltpu.VMEM((channels * 16, width), f32)],
        compiler_params=params(),
    )(field, land_mask, first, second, update)

    pairs = []
    for low in range(0, nlon, 2):
        pairs += [(low, low + 1), (low + 1, low)]
    core_sent, cross_sent = core, cross
    core = lax.ppermute(core, "lon", pairs)
    pairs = []
    for low in range(1, nlon, 2):
        after = (low + 1) % nlon
        pairs += [(low, after), (after, low)]
    cross = lax.ppermute(cross, "lon", pairs)

    update = pl.pallas_call(
        edge_rows,
        out_shape=jax.ShapeDtypeStruct((channels * 24, width), f32),
        in_specs=vmem(7),
        out_specs=pl.BlockSpec(memory_space=pltpu.VMEM),
        scratch_shapes=[pltpu.VMEM((channels * 16, width), f32)] + buffers(len(EDGE)),
        input_output_aliases={6: 0},
        compiler_params=params(),
        cost_estimate=cost(4e9),
    )(field, halo, matrix_one, by_channel, expand, w_reduce, update)

    strips = pl.pallas_call(
        edge_columns,
        out_shape=jax.ShapeDtypeStruct((channels * 24, width), f32),
        in_specs=vmem(8),
        out_specs=pl.BlockSpec(memory_space=pltpu.VMEM),
        scratch_shapes=[pltpu.VMEM((channels * 24, width), f32)] + buffers(3),
        compiler_params=params(),
    )(core, cross, core_sent, cross_sent, matrix_one, by_channel, expand, w_reduce)

    return pl.pallas_call(
        second_layer,
        out_shape=jax.ShapeDtypeStruct((channels, rows, width), bf16),
        in_specs=vmem(12),
        out_specs=pl.BlockSpec(memory_space=pltpu.VMEM),
        scratch_shapes=[
            pltpu.VMEM((channels, rows, width), bf16),
            pltpu.VMEM((channels * 16, width), f32),
        ]
        + buffers(rows),
        compiler_params=params(),
    )(
        field,
        land_mask,
        halo,
        halo_mask,
        core,
        cross,
        strips,
        update,
        matrix_two,
        by_channel,
        expand,
        w_reduce,
    )


def solution(mesh):
    placed = (P(None, "lat", "lon"), P("lat", "lon"), P(), P(), P(), P(), P(), P(), P(), P())
    return jax.shard_map(
        functools.partial(per_device, mesh.shape["lat"], mesh.shape["lon"]),
        mesh=mesh,
        in_specs=placed,
        out_specs=P(None, "lat", "lon"),
        check_vma=False,
    )
```

time: 113 us -> 30.1 us (0.27)
  the two profiles are of different devices: /device:TPU:0 before, /device:TPU:2 now
where the time goes in v1:
time: 30.1 us; the launch traced here: 29.9 us
  Pallas kernels  16.4 us (54%)
  starting transfers between devices  11.9 us (40%)
  local copies, waits for them, and re-layouts  1.04 us (3%)
  waiting for transfers between devices  0.37 us (1%)
    ppermute x1, starting transfers between devices, per_device(): second = lax.ppermute(second, ('lon', 'lat'), pairs)  6.14 us
    pallas_call x1, Pallas kernels, per_device(): pl.pallas_call(second_layer, out_shape=jax.ShapeDtypeStruct((channels, ro...  5.1 us
    ppermute x1, starting transfers between devices, per_device(): cross = lax.ppermute(cross, 'lon', pairs)  5.01 us
    pallas_call x1, Pallas kernels, per_device(): pl.pallas_call(edge_columns, out_shape=jax.ShapeDtypeStruct((channels * 2...  3.73 us
    pallas_call x1, Pallas kernels, per_device(): pl.pallas_call(edge_rows, out_shape=jax.ShapeDtypeStruct((channels * 24,...  2.59 us
    pallas_call x1, Pallas kernels, per_device(): pl.pallas_call(inner_rows, out_shape=jax.ShapeDtypeStruct((channels * 24,...  1.97 us
    pallas_call x1, Pallas kernels, per_device(): pl.pallas_call(weights, out_shape=[jax.ShapeDtypeStruct((channels * 24, 2...  1.65 us
    unnamed x20, local copies, waits for them, and re-layouts  1.04 us
  transfers between devices with their start and end apart: 4, of which 1 were waited for; matrix products, arithmetic and copies ran while one was open for 0% of the time, Pallas kernels for 21%

profile of v1, /device:TPU:2, one launch (start us, length us, event | category | flops | bytes accessed | tf_op | source)
XLA Modules:
  0.0 29.9 jit_solution(14727495904238396319)
XLA Ops:
  0.0 0.0 copy-start
  0.0 0.0 copy-start.2
  0.0 1.0 %copy-done = bf16[96,16,128]{2,1,0:T(8,128)(2,1)S(1)} copy-done((bf16[96,16,128]{2,1,0:T(8,128)(2,1)S(1)}, bf16[96,16,128]{2,1,0:T(8,128)(2,1)}, u32[]{:S(2)}) %copy-start) | copy-done | bytes 393240
  1.0 0.0 copy-done.2
  1.0 0.2 shard_map.101.after_ref
  1.2 0.0 copy-start.3
  1.2 0.0 copy-start.4
  1.2 0.0 copy-start.5
  1.3 0.0 copy-start.6
  1.3 0.0 copy-start.7
  1.3 0.0 copy-start.8
  1.3 0.0 copy-start.9
  1.3 0.1 collective-permute-start
  1.4 0.2 shard_map.102
  1.6 6.1 %collective-permute-start.1 = (bf16[592,128]{1,0:T(8,128)(2,1)S(1)}, bf16[592,128]{1,0:T(8,128)(2,1)S(1)}, u32[]{:S(2)}, u32[]{:S(2)}) collective-permute-start(bf16[592,128]{1,0:T(8,128)(2,1)S(1)} %shard_map.102), channel_id=1, source_target_pairs={{1,31},{3,29},{5,27},{7,25},{9,23},{11,21},{13,19},{15,17},{17,15}... | collective-permute-start | bytes 454664 | tf_op jit(solution)/shard_map/ppermute | solution.py:568
  7.8 0.0 copy-done.3
  7.8 0.0 copy-done.4
  7.8 0.0 copy-done.5
  7.8 0.0 copy-done.6
  7.8 0.0 copy-done.7
  7.8 0.0 copy-done.8
  7.8 0.0 copy-done.9
  7.8 0.0 copy-start.1
  7.8 1.6 %shard_map.103 = (bf16[2304,256]{1,0:T(8,128)(2,1)S(1)}, bf16[1536,256]{1,0:T(8,128)(2,1)S(1)}, f32[2,3,96,128]{3,2,1,0:T(8,128)S(1)}, bf16[2,384,112]{2,1,0:T(8,128)(2,1)S(1)}) custom-call(f32[49,2,96]{2,1,0:T(2,128)S(1)} %bitcast.5, f32[2,96]{1,0:T(2,128)S(1)} %copy-done.6, f32[2,96]{1,0:T(2,128)S(1)} %copy-done.7, f32[2,96]{1,0:T(2,128)S(1)} %copy-done.8, ...), custom_call_target="tpu_custom_call" | custom-call | flops 2000000000 | bytes 1048576 | tf_op jit(solution)/shard_map/pallas_call | solution.py:575
  9.5 0.0 copy-done.1
  9.5 2.0 %shard_map.104.after_ref.old_ref = f32[2304,128]{1,0:T(8,128)S(1)} custom-call(bf16[96,16,128]{2,1,0:T(8,128)(2,1)S(1)} %copy-done, bf16[2304,256]{1,0:T(8,128)(2,1)S(1)} %get-tuple-element.13.matrix_ref, f32[2,3,96,128]{3,2,1,0:T(8,128)S(1)} %get-tuple-element.14.rows_ref, bf16[2,384,112]{2,1,0:T(8,128)(2,1)S(1)} %get-tuple-element.15.expand_ref, ...), custom_call_target="tpu_custom_call" | custom-call | flops 4000000000 | bytes 1048576 | tf_op jit(solution)/shard_map/pallas_call | solution.py:602
  11.5 0.4 %collective-permute-done.1.second_ref = bf16[592,128]{1,0:T(8,128)(2,1)S(1)} collective-permute-done((bf16[592,128]{1,0:T(8,128)(2,1)S(1)}, bf16[592,128]{1,0:T(8,128)(2,1)S(1)}, u32[]{:S(2)}, u32[]{:S(2)}) %collective-permute-start.1) | collective-permute-done | bytes 151584 | tf_op jit(solution)/shard_map/ppermute | solution.py:568
  11.8 0.0 collective-permute-done.first_ref
  11.8 0.9 %shard_map.105 = (bf16[96,16,128]{2,1,0:T(8,128)(2,1)S(1)}, f32[16,128]{1,0:T(8,128)S(1)}, bf16[224,128]{1,0:T(8,128)(2,1)S(1)}, bf16[224,128]{1,0:T(8,128)(2,1)S(1)}) custom-call(bf16[96,16,128]{2,1,0:T(8,128)(2,1)S(1)} %copy-done, s32[16,128]{1,0:T(8,128)S(1)} %copy-done.2, bf16[592,128]{1,0:T(8,128)(2,1)S(1)} %collective-permute-done.first_ref, ...), custom_call_target="tpu_custom_call" | custom-call | tf_op jit(solution)/shard_map/pallas_call | solution.py:613
  12.8 0.7 %collective-permute-start.2 = (bf16[224,128]{1,0:T(8,128)(2,1)S(1)}, bf16[224,128]{1,0:T(8,128)(2,1)S(1)}, u32[]{:S(2)}, u32[]{:S(2)}) collective-permute-start(bf16[224,128]{1,0:T(8,128)(2,1)S(1)} %get-tuple-element.18.core_sent_ref), channel_id=1, source_target_pairs={{0,2},{2,0},{4,6},{6,4},{8,10},{10,8},{12,14},{14,12},{16,18},{18,... | collective-permute-start | bytes 172040 | tf_op jit(solution)/shard_map/ppermute | solution.py:631
  13.4 5.0 %collective-permute-start.3 = (bf16[224,128]{1,0:T(8,128)(2,1)S(1)}, bf16[224,128]{1,0:T(8,128)(2,1)S(1)}, u32[]{:S(2)}, u32[]{:S(2)}) collective-permute-start(bf16[224,128]{1,0:T(8,128)(2,1)S(1)} %get-tuple-element.19.cross_sent_ref), channel_id=1, source_target_pairs={{2,4},{4,2},{6,8},{8,6},{10,12},{12,10},{14,16},{16,14},{18,20},{2... | collective-permute-start | bytes 172040 | tf_op jit(solution)/shard_map/ppermute | solution.py:636
  18.4 2.6 %shard_map.107.update_ref = f32[2304,128]{1,0:T(8,128)S(1)} custom-call(bf16[96,16,128]{2,1,0:T(8,128)(2,1)S(1)} %copy-done, bf16[96,16,128]{2,1,0:T(8,128)(2,1)S(1)} %get-tuple-element.16.halo_ref, bf16[2304,256]{1,0:T(8,128)(2,1)S(1)} %get-tuple-element.13.matrix_ref, ...), custom_call_target="tpu_custom_call", output_to_operand_aliasing={{}: (6, {})} | custom-call | flops 4000000000 | bytes 1048576 | tf_op jit(solution)/shard_map/pallas_call | solution.py:638
  21.0 0.0 collective-permute-done.2.core_ref
  21.1 0.0 collective-permute-done.3.cross_ref
  21.1 3.7 %shard_map.106.strips = f32[2304,128]{1,0:T(8,128)S(1)} custom-call(bf16[224,128]{1,0:T(8,128)(2,1)S(1)} %collective-permute-done.2.core_ref, bf16[224,128]{1,0:T(8,128)(2,1)S(1)} %collective-permute-done.3.cross_ref, bf16[224,128]{1,0:T(8,128)(2,1)S(1)} %get-tuple-element.18.core_sent_ref, bf16[224,128]{1,0:T(8,128)(2,1)S(1)} %get-tuple-element.19.cross_sent_ref, ...), custom_call_target="tpu_custom_call" | custom-call | tf_op jit(solution)/shard_map/pallas_call | solution.py:649
  24.8 5.1 %shard_map.108 = bf16[96,16,128]{2,1,0:T(8,128)(2,1)} custom-call(bf16[96,16,128]{2,1,0:T(8,128)(2,1)S(1)} %copy-done, s32[16,128]{1,0:T(8,128)S(1)} %copy-done.2, bf16[96,16,128]{2,1,0:T(8,128)(2,1)S(1)} %get-tuple-element.16.halo_ref, f32[16,128]{1,0:T(8,128)S(1)} %get-tuple-element.17.halo_mask_ref, bf16[224,128]{1,0:T(8,128)(2,1)S(1)} %collective-permute-done.2.core_ref, ...), custom_call_target="tpu_custom_call" | custom-call | tf_op jit(solution)/shard_map/pallas_call | solution.py:658
  (1 shorter events, 0.0 us)
Async XLA Ops:
  0.0 1.0 %copy-start = (bf16[96,16,128]{2,1,0:T(8,128)(2,1)S(1)}, bf16[96,16,128]{2,1,0:T(8,128)(2,1)}, u32[]{:S(2)}) copy-start(bf16[96,16,128]{2,1,0:T(8,128)(2,1)} %field_ref.11) | copy-start | bytes 1179652
  0.0 1.0 %copy-start.2 = (s32[16,128]{1,0:T(8,128)S(1)}, s32[16,128]{1,0:T(8,128)}, u32[]{:S(2)}) copy-start(s32[16,128]{1,0:T(8,128)} %mask_ref.7) | copy-start | bytes 24580
  1.2 6.5 %copy-start.3 = (bf16[2,384,96]{1,2,0:T(8,128)(2,1)S(1)}, bf16[2,384,96]{1,2,0:T(8,128)(2,1)}, u32[]{:S(2)}) copy-start(bf16[2,384,96]{1,2,0:T(8,128)(2,1)} %param.16) | copy-start | bytes 442372
  1.2 6.5 %copy-start.4 = (f32[2,96,7,7]{1,0,3,2:T(2,128)S(1)}, f32[2,96,7,7]{1,0,3,2:T(2,128)}, u32[]{:S(2)}) copy-start(f32[2,96,7,7]{1,0,3,2:T(2,128)} %param.12) | copy-start | bytes 112900
  1.2 6.5 %copy-start.5 = (f32[2,384]{1,0:T(2,128)S(1)}, f32[2,384]{1,0:T(2,128)}, u32[]{:S(2)}) copy-start(f32[2,384]{1,0:T(2,128)} %expand_bias_ref.1) | copy-start | bytes 9220
  1.3 6.5 %copy-start.6 = (f32[2,96]{1,0:T(2,128)S(1)}, f32[2,96]{1,0:T(2,128)}, u32[]{:S(2)}) copy-start(f32[2,96]{1,0:T(2,128)} %bias_ref.1) | copy-start | bytes 2308
  1.3 6.5 %copy-start.7 = (f32[2,96]{1,0:T(2,128)S(1)}, f32[2,96]{1,0:T(2,128)}, u32[]{:S(2)}) copy-start(f32[2,96]{1,0:T(2,128)} %gain_ref.1) | copy-start | bytes 2308
  1.3 6.5 %copy-start.8 = (f32[2,96]{1,0:T(2,128)S(1)}, f32[2,96]{1,0:T(2,128)}, u32[]{:S(2)}) copy-start(f32[2,96]{1,0:T(2,128)} %norm_bias_ref.1) | copy-start | bytes 2308
  1.3 6.5 %copy-start.9 = (f32[2,96]{1,0:T(2,128)S(1)}, f32[2,96]{1,0:T(2,128)}, u32[]{:S(2)}) copy-start(f32[2,96]{1,0:T(2,128)} %reduce_bias_ref.1) | copy-start | bytes 2308
  1.3 10.5 %collective-permute-start = (bf16[592,128]{1,0:T(8,128)(2,1)S(1)}, bf16[592,128]{1,0:T(8,128)(2,1)S(1)}, u32[]{:S(2)}, u32[]{:S(2)}) collective-permute-start(bf16[592,128]{1,0:T(8,128)(2,1)S(1)} %shard_map.101.after_ref), channel_id=1, source_target_pairs={{0,1},{1,0},{2,3},{3,2},{4,5},{5,4},{6,7},{7,6},{8,9},{9,8},{10,11... | collective-permute-start | bytes 454664 | tf_op jit(solution)/shard_map/ppermute | solution.py:572
  1.6 10.2 %collective-permute-start.1 = (bf16[592,128]{1,0:T(8,128)(2,1)S(1)}, bf16[592,128]{1,0:T(8,128)(2,1)S(1)}, u32[]{:S(2)}, u32[]{:S(2)}) collective-permute-start(bf16[592,128]{1,0:T(8,128)(2,1)S(1)} %shard_map.102), channel_id=1, source_target_pairs={{1,31},{3,29},{5,27},{7,25},{9,23},{11,21},{13,19},{15,17},{17,15}... | collective-permute-start | bytes 454664 | tf_op jit(solution)/shard_map/ppermute | solution.py:568
  7.8 1.7 %copy-start.1 = (bf16[2,96,384]{2,1,0:T(8,128)(2,1)S(1)}, bf16[2,96,384]{2,1,0:T(8,128)(2,1)}, u32[]{:S(2)}) copy-start(bf16[2,96,384]{2,1,0:T(8,128)(2,1)} %reduce_ref.7) | copy-start | bytes 442372
  12.8 8.3 %collective-permute-start.2 = (bf16[224,128]{1,0:T(8,128)(2,1)S(1)}, bf16[224,128]{1,0:T(8,128)(2,1)S(1)}, u32[]{:S(2)}, u32[]{:S(2)}) collective-permute-start(bf16[224,128]{1,0:T(8,128)(2,1)S(1)} %get-tuple-element.18.core_sent_ref), channel_id=1, source_target_pairs={{0,2},{2,0},{4,6},{6,4},{8,10},{10,8},{12,14},{14,12},{16,18},{18,... | collective-permute-start | bytes 172040 | tf_op jit(solution)/shard_map/ppermute | solution.py:631
  13.4 7.6 %collective-permute-start.3 = (bf16[224,128]{1,0:T(8,128)(2,1)S(1)}, bf16[224,128]{1,0:T(8,128)(2,1)S(1)}, u32[]{:S(2)}, u32[]{:S(2)}) collective-permute-start(bf16[224,128]{1,0:T(8,128)(2,1)S(1)} %get-tuple-element.19.cross_sent_ref), channel_id=1, source_target_pairs={{2,4},{4,2},{6,8},{8,6},{10,12},{12,10},{14,16},{16,14},{18,20},{2... | collective-permute-start | bytes 172040 | tf_op jit(solution)/shard_map/ppermute | solution.py:636

commit v2 on v1

--- a/solution.py
+++ b/solution.py
@@ -56,7 +56,7 @@
 
 
 def channel_of(channels, group, slot):
-    return slot // 4 * (channels // 4) + group * 4 + slot % 4
+    return slot // 2 * (channels // 4) + group * 2 + slot % 2
 
 
 def join_rows(
@@ -67,8 +67,7 @@
     after_ref,
     halo_ref,
     halo_mask_ref,
-    core_ref,
-    cross_ref,
+    ends_ref,
     wide,
 ):
     del after_ref
@@ -76,7 +75,6 @@
     lat = lax.axis_index("lat")
     even = lax.rem(lat, 2) == 0
     folded = lat == lax.axis_size("lat") - 1
-    lon_even = lax.rem(lax.axis_index("lon"), 2) == 0
     wide[...] = jnp.zeros_like(wide)
     halo_mask_ref[...] = jnp.zeros_like(halo_mask_ref)
     sub = lax.broadcasted_iota(jnp.int32, (width, width), 0)
@@ -103,27 +101,23 @@
         halo_mask_ref[south_place(k) : south_place(k) + 1, :] = mask_south[k : k + 1, :]
     halo_ref[...] = wide[...].astype(jnp.bfloat16).reshape(channels, 16, width)
 
-    lane = lanes((32, width))
-    slots = [(lane >= 8 * q) & (lane < 8 * q + HALO) for q in range(16)]
-
-    def group(blocks):
-        west = jnp.zeros((32, width), jnp.bfloat16)
-        east = jnp.zeros((32, width), jnp.bfloat16)
-        for q, block in enumerate(blocks):
-            west = jnp.where(slots[q], pltpu.roll(block, 8 * q, 1), west)
-            east = jnp.where(slots[q], pltpu.roll(block, (8 * q + HALO) % width, 1), east)
-        return jnp.where(lon_even, east, west), jnp.where(lon_even, west, east)
-
-    for g in range(channels // 16):
-        blocks = []
-        for q in range(16):
-            c = channel_of(channels, g, q)
-            blocks.append(jnp.concatenate([field_ref[c], halo_ref[c]], axis=0))
-        core_ref[g * 32 : g * 32 + 32, :], cross_ref[g * 32 : g * 32 + 32, :] = group(blocks)
+    slot = lanes((32, width)) // 16
+
+    def ends(blocks):
+        packed = jnp.zeros((32, width), jnp.bfloat16)
+        for j, block in enumerate(blocks):
+            packed = jnp.where(slot == j, pltpu.roll(block, 16 * j + HALO, 1), packed)
+        return packed
+
+    groups = channels // 8
+    for g in range(groups):
+        some = [channel_of(channels, g, j) for j in range(8)]
+        blocks = [jnp.concatenate([field_ref[c], halo_ref[c]], axis=0) for c in some]
+        ends_ref[g * 32 : g * 32 + 32, :] = ends(blocks)
     mask_block = jnp.concatenate(
         [mask_ref[...].astype(jnp.float32), halo_mask_ref[...]], axis=0
     ).astype(jnp.bfloat16)
-    core_ref[channels * 2 :, :], cross_ref[channels * 2 :, :] = group([mask_block])
+    ends_ref[groups * 32 :, :] = ends([mask_block])
 
 
 def in_row(place, first_layer):
@@ -354,8 +348,7 @@
 def edge_columns(
     core_ref,
     cross_ref,
-    core_sent_ref,
-    cross_sent_ref,
+    ends_ref,
     matrix_ref,
     rows_ref,
     expand_ref,
@@ -367,24 +360,22 @@
 ):
     channels, width = rows_ref.shape[2:]
     quarter = channels // 4
-    groups = channels // 16
+    groups = channels // 8
     lane32 = lanes((32, width))
-    within = lane32 % 32
-    in_west, in_own_west, in_own_east = within < 6, within < 12, within < 18
+    first_six = lane32 % 16 < HALO
+    first_twelve = lane32 % 32 < 2 * HALO
     ones = jnp.ones((32, width), jnp.bfloat16)
     for g in range(groups):
         at = slice(g * 32, g * 32 + 32)
         east, west = by_side(core_ref[at, :], cross_ref[at, :])
-        own_east, own_west = by_side(core_sent_ref[at, :], cross_sent_ref[at, :])
-        for t in range(4):
-            parts = [
-                pltpu.roll(part, (6 * n - 8 * t) % width, 1)
-                for n, part in enumerate((west, own_west, own_east, east))
-            ]
-            block = jnp.where(in_own_east, parts[2], parts[3])
-            block = jnp.where(in_own_west, parts[1], block)
-            block = jnp.where(in_west, parts[0], block)
-            some = [channel_of(channels, g, 4 * n + t) for n in range(4)]
+        own = ends_ref[at, :]
+        at_west = jnp.where(first_six, west, own)
+        at_east = jnp.where(first_six, own, east)
+        for t in range(2):
+            left = pltpu.roll(at_west, width - 16, 1) if t else at_west
+            right = pltpu.roll(at_east, (2 * HALO - 16 * t) % width, 1)
+            block = jnp.where(first_twelve, left, right)
+            some = [channel_of(channels, g, 2 * n + t) for n in range(4)]
             matrix = jnp.concatenate(
                 [matrix_ref[c * 24 : c * 24 + 24, :] for c in some], axis=0
             )
@@ -394,26 +385,28 @@
                 conv[pl.ds(c, 24, stride=channels), :] = result[n * 24 : n * 24 + 24, :]
 
     order = {place_of(row): i for i, row in enumerate(EDGE + INNER)}
-    slot = lanes((quarter, width)) // 8
+    lane = lanes((quarter, width))
+    starts = [32 * (q // 2) + 6 * (q % 2) for q in range(8)]
+    inside = [
+        ((lane >= s + 3) & (lane < s + 9)) | ((lane >= s + 15) & (lane < s + 21)) for s in starts
+    ]
     packs = []
     for p in range(3):
         parts = []
         for n in range(4):
             packed = jnp.zeros((quarter, width), jnp.float32)
-            for q in range(8):
+            for q, start in enumerate(starts):
                 if p * 8 + q in order:
-                    start = order[p * 8 + q] * channels + n * quarter
-                    block = conv[start : start + quarter, :]
-                    near = pltpu.roll(block, (53 - 8 * q - 32 * n) % width, 1)
-                    far = pltpu.roll(block, (105 - 8 * q - 32 * n) % width, 1)
-                    packed = jnp.where(slot == 7 - q, near, packed)
-                    packed = jnp.where(slot == 15 - q, far, packed)
+                    row = order[p * 8 + q] * channels + n * quarter
+                    block = conv[row : row + quarter, :]
+                    block = pltpu.roll(block, (start - 32 * n) % width, 1)
+                    packed = jnp.where(inside[q], block, packed)
             parts.append(packed)
         packs.append(jnp.concatenate(parts, axis=0))
 
     def put(p, change):
-        for q in range(8):
-            near = pltpu.roll(change, (69 + 8 * q) % width, 1)
+        for q, start in enumerate(starts):
+            near = pltpu.roll(change, (width - 6 - start) % width, 1)
             strips[pl.ds(p * 8 + q, channels, stride=24), :] = near
 
     blocks = [functools.partial(lambda block: block, packed) for packed in packs]
@@ -440,36 +433,35 @@
     inner,
 ):
     channels, rows, width = out_ref.shape
-    half = width // 2
-    groups = channels // 16
+    groups = channels // 8
     lane32 = lanes((32, width))
     lane24 = lanes((24, width))
-    to_east = lane32 < half
-
-    def beside_of(east, west, q):
-        east = pltpu.roll(east, (width - 8 * q) % width, 1)
-        west = pltpu.roll(west, width - HALO - 8 * q, 1)
-        return jnp.where(to_east, east, west).astype(jnp.float32)[0:24, :]
+    first_six = lane32 % 16 < HALO
+
+    def beside_of(received, slot):
+        beside = pltpu.roll(received, (width - HALO - 16 * slot) % width, 1)
+        return beside.astype(jnp.float32)[0:24, :]
 
     def received(g):
         at = slice(g * 32, g * 32 + 32)
-        return by_side(core_ref[at, :], cross_ref[at, :])
+        east, west = by_side(core_ref[at, :], cross_ref[at, :])
+        return jnp.where(first_six, west, east)
 
     main_mask = jnp.concatenate(
         [mask_ref[...].astype(jnp.float32), halo_mask_ref[0:8, :]], axis=0
     )
-    side_mask = beside_of(*received(groups), 0)
+    side_mask = beside_of(received(groups), 0)
     low = lane24 < 3
     high = lane24 >= width - 3
     blank = jnp.zeros((8, width), jnp.float32)
     ones = jnp.ones((32, width), jnp.bfloat16)
     away = {s: lane32 < s if s > 0 else lane32 >= width + s for s in range(-3, 4) if s}
     for g in range(groups):
-        east, west = received(g)
-        for q in range(16):
-            c = channel_of(channels, g, q)
+        both = received(g)
+        for j in range(8):
+            c = channel_of(channels, g, j)
             near = strips[c * 24 : c * 24 + 24, :]
-            far = pltpu.roll(near, half, 1)
+            far = pltpu.roll(near, width - 2 * HALO, 1)
             change = update_ref[c * 24 : c * 24 + 24, :]
             change = jnp.where(low, near, jnp.where(high, far, change))
             old = jnp.concatenate([field_ref[c], halo_ref[c]], axis=0).astype(jnp.float32)
@@ -477,7 +469,7 @@
             main = jnp.concatenate([main, blank], axis=0).astype(jnp.bfloat16)
             main_ref[c] = main[:rows, :]
             change = jnp.where(high, near, far)
-            beside = side_mask * (beside_of(east, west, q) + change)
+            beside = side_mask * (beside_of(both, j) + change)
             beside = jnp.concatenate([beside, blank], axis=0).astype(jnp.bfloat16)
             stack = []
             for s in range(-3, 4):
@@ -609,17 +601,16 @@
         cost_estimate=cost(4e9),
     )(field, matrix_one, by_channel, expand, w_reduce)
 
-    strip_rows = (channels // 16 + 1) * 32
-    halo, halo_mask, core, cross = pl.pallas_call(
+    strip_rows = (channels // 8 + 1) * 32
+    halo, halo_mask, ends = pl.pallas_call(
         join_rows,
         out_shape=[
             jax.ShapeDtypeStruct((channels, 16, width), bf16),
             jax.ShapeDtypeStruct((16, width), f32),
             jax.ShapeDtypeStruct((strip_rows, width), bf16),
-            jax.ShapeDtypeStruct((strip_rows, width), bf16),
         ],
         in_specs=vmem(4) + [pl.BlockSpec(memory_space=pl.ANY)],
-        out_specs=vmem(4),
+        out_specs=vmem(3),
         scratch_shapes=[pltpu.VMEM((channels * 16, width), f32)],
         compiler_params=params(),
     )(field, land_mask, first, second, update)
@@ -627,13 +618,12 @@
     pairs = []
     for low in range(0, nlon, 2):
         pairs += [(low, low + 1), (low + 1, low)]
-    core_sent, cross_sent = core, cross
-    core = lax.ppermute(core, "lon", pairs)
+    core = lax.ppermute(ends, "lon", pairs)
     pairs = []
     for low in range(1, nlon, 2):
         after = (low + 1) % nlon
         pairs += [(low, after), (after, low)]
-    cross = lax.ppermute(cross, "lon", pairs)
+    cross = lax.ppermute(ends, "lon", pairs)
 
     update = pl.pallas_call(
         edge_rows,
@@ -649,11 +639,11 @@
     strips = pl.pallas_call(
         edge_columns,
         out_shape=jax.ShapeDtypeStruct((channels * 24, width), f32),
-        in_specs=vmem(8),
+        in_specs=vmem(7),
         out_specs=pl.BlockSpec(memory_space=pltpu.VMEM),
         scratch_shapes=[pltpu.VMEM((channels * 24, width), f32)] + buffers(3),
         compiler_params=params(),
-    )(core, cross, core_sent, cross_sent, matrix_one, by_channel, expand, w_reduce)
+    )(core, cross, ends, matrix_one, by_channel, expand, w_reduce)
 
     return pl.pallas_call(
         second_layer,

time: 30.1 us -> 27.7 us (0.920)
  the two profiles are of different devices: /device:TPU:2 before, /device:TPU:3 now
where the time goes in v2:
time: 27.7 us; the launch traced here: 27.6 us
  Pallas kernels  14.1 us (51%)
  starting transfers between devices  12.2 us (44%)
  local copies, waits for them, and re-layouts  1.04 us (4%)
    ppermute x1, starting transfers between devices, per_device(): second = lax.ppermute(second, ('lon', 'lat'), pairs)  7.26 us
    pallas_call x1, Pallas kernels, per_device(): pl.pallas_call(second_layer, out_shape=jax.ShapeDtypeStruct((channels, ro...  4.53 us
    ppermute x1, starting transfers between devices, per_device(): core = lax.ppermute(ends, 'lon', pairs)  2.83 us
    pallas_call x1, Pallas kernels, per_device(): pl.pallas_call(edge_rows, out_shape=jax.ShapeDtypeStruct((channels * 24,...  2.6 us
    pallas_call x1, Pallas kernels, per_device(): pl.pallas_call(edge_columns, out_shape=jax.ShapeDtypeStruct((channels * 2...  2.24 us
    ppermute x1, starting transfers between devices, per_device(): cross = lax.ppermute(ends, 'lon', pairs)  2.04 us
    pallas_call x1, Pallas kernels, per_device(): pl.pallas_call(inner_rows, out_shape=jax.ShapeDtypeStruct((channels * 24,...  1.96 us
    pallas_call x1, Pallas kernels, per_device(): pl.pallas_call(weights, out_shape=[jax.ShapeDtypeStruct((channels * 24, 2...  1.64 us
  transfers between devices with their start and end apart: 4, of which 0 were waited for; matrix products, arithmetic and copies ran while one was open for 0% of the time, Pallas kernels for 23%

profile of v2, /device:TPU:3, one launch (start us, length us, event | category | flops | bytes accessed | tf_op | source)
XLA Modules:
  0.0 27.6 jit_solution(7868703931308145197)
XLA Ops:
  0.0 0.0 copy-start
  0.0 0.0 copy-start.2
  0.0 1.0 %copy-done = bf16[96,16,128]{2,1,0:T(8,128)(2,1)S(1)} copy-done((bf16[96,16,128]{2,1,0:T(8,128)(2,1)S(1)}, bf16[96,16,128]{2,1,0:T(8,128)(2,1)}, u32[]{:S(2)}) %copy-start) | copy-done | bytes 393240
  1.0 0.0 copy-done.2
  1.0 0.2 shard_map.101.after_ref
  1.2 0.0 copy-start.3
  1.2 0.0 copy-start.4
  1.2 0.0 copy-start.5
  1.3 0.0 copy-start.6
  1.3 0.0 copy-start.7
  1.3 0.0 copy-start.8
  1.3 0.0 copy-start.9
  1.3 0.1 collective-permute-start
  1.4 0.2 shard_map.102
  1.6 7.3 %collective-permute-start.1 = (bf16[592,128]{1,0:T(8,128)(2,1)S(1)}, bf16[592,128]{1,0:T(8,128)(2,1)S(1)}, u32[]{:S(2)}, u32[]{:S(2)}) collective-permute-start(bf16[592,128]{1,0:T(8,128)(2,1)S(1)} %shard_map.102), channel_id=1, source_target_pairs={{1,31},{3,29},{5,27},{7,25},{9,23},{11,21},{13,19},{15,17},{17,15}... | collective-permute-start | bytes 454664 | tf_op jit(solution)/shard_map/ppermute | solution.py:560
  8.9 0.0 copy-done.3
  8.9 0.0 copy-done.4
  8.9 0.0 copy-done.5
  8.9 0.0 copy-done.6
  8.9 0.0 copy-done.7
  8.9 0.0 copy-done.8
  8.9 0.0 copy-done.9
  8.9 0.0 copy-start.1
  9.0 1.6 %shard_map.103 = (bf16[2304,256]{1,0:T(8,128)(2,1)S(1)}, bf16[1536,256]{1,0:T(8,128)(2,1)S(1)}, f32[2,3,96,128]{3,2,1,0:T(8,128)S(1)}, bf16[2,384,112]{2,1,0:T(8,128)(2,1)S(1)}) custom-call(f32[49,2,96]{2,1,0:T(2,128)S(1)} %bitcast.5, f32[2,96]{1,0:T(2,128)S(1)} %copy-done.6, f32[2,96]{1,0:T(2,128)S(1)} %copy-done.7, f32[2,96]{1,0:T(2,128)S(1)} %copy-done.8, ...), custom_call_target="tpu_custom_call" | custom-call | flops 2000000000 | bytes 1048576 | tf_op jit(solution)/shard_map/pallas_call | solution.py:567
  10.6 0.0 copy-done.1
  10.6 2.0 %shard_map.104.after_ref.old_ref = f32[2304,128]{1,0:T(8,128)S(1)} custom-call(bf16[96,16,128]{2,1,0:T(8,128)(2,1)S(1)} %copy-done, bf16[2304,256]{1,0:T(8,128)(2,1)S(1)} %get-tuple-element.12.matrix_ref, f32[2,3,96,128]{3,2,1,0:T(8,128)S(1)} %get-tuple-element.13.rows_ref, bf16[2,384,112]{2,1,0:T(8,128)(2,1)S(1)} %get-tuple-element.14.expand_ref, ...), custom_call_target="tpu_custom_call" | custom-call | flops 4000000000 | bytes 1048576 | tf_op jit(solution)/shard_map/pallas_call | solution.py:594
  12.6 0.0 collective-permute-done.1.second_ref
  12.6 0.0 collective-permute-done.first_ref
  12.6 0.7 %shard_map.105 = (bf16[96,16,128]{2,1,0:T(8,128)(2,1)S(1)}, f32[16,128]{1,0:T(8,128)S(1)}, bf16[416,128]{1,0:T(8,128)(2,1)S(1)}) custom-call(bf16[96,16,128]{2,1,0:T(8,128)(2,1)S(1)} %copy-done, s32[16,128]{1,0:T(8,128)S(1)} %copy-done.2, bf16[592,128]{1,0:T(8,128)(2,1)S(1)} %collective-permute-done.first_ref, ...), custom_call_target="tpu_custom_call" | custom-call | tf_op jit(solution)/shard_map/pallas_call | solution.py:605
  13.3 2.0 %collective-permute-start.3 = (bf16[416,128]{1,0:T(8,128)(2,1)S(1)}, bf16[416,128]{1,0:T(8,128)(2,1)S(1)}, u32[]{:S(2)}, u32[]{:S(2)}) collective-permute-start(bf16[416,128]{1,0:T(8,128)(2,1)S(1)} %get-tuple-element.17.ends_ref), channel_id=1, source_target_pairs={{2,4},{4,2},{6,8},{8,6},{10,12},{12,10},{14,16},{16,14},{18,20},{2... | collective-permute-start | bytes 319496 | tf_op jit(solution)/shard_map/ppermute | solution.py:626
  15.3 2.8 %collective-permute-start.2 = (bf16[416,128]{1,0:T(8,128)(2,1)S(1)}, bf16[416,128]{1,0:T(8,128)(2,1)S(1)}, u32[]{:S(2)}, u32[]{:S(2)}) collective-permute-start(bf16[416,128]{1,0:T(8,128)(2,1)S(1)} %get-tuple-element.17.ends_ref), channel_id=1, source_target_pairs={{0,2},{2,0},{4,6},{6,4},{8,10},{10,8},{12,14},{14,12},{16,18},{18,... | collective-permute-start | bytes 319496 | tf_op jit(solution)/shard_map/ppermute | solution.py:621
  18.2 2.6 %shard_map.107.update_ref = f32[2304,128]{1,0:T(8,128)S(1)} custom-call(bf16[96,16,128]{2,1,0:T(8,128)(2,1)S(1)} %copy-done, bf16[96,16,128]{2,1,0:T(8,128)(2,1)S(1)} %get-tuple-element.15.halo_ref, bf16[2304,256]{1,0:T(8,128)(2,1)S(1)} %get-tuple-element.12.matrix_ref, ...), custom_call_target="tpu_custom_call", output_to_operand_aliasing={{}: (6, {})} | custom-call | flops 4000000000 | bytes 1048576 | tf_op jit(solution)/shard_map/pallas_call | solution.py:628
  20.8 0.0 collective-permute-done.3.cross_ref
  20.8 0.0 collective-permute-done.2.core_ref
  20.8 2.2 %shard_map.106.strips = f32[2304,128]{1,0:T(8,128)S(1)} custom-call(bf16[416,128]{1,0:T(8,128)(2,1)S(1)} %collective-permute-done.2.core_ref, bf16[416,128]{1,0:T(8,128)(2,1)S(1)} %collective-permute-done.3.cross_ref, bf16[416,128]{1,0:T(8,128)(2,1)S(1)} %get-tuple-element.17.ends_ref, bf16[2304,256]{1,0:T(8,128)(2,1)S(1)} %get-tuple-element.12.matrix_ref, ...), custom_call_target="tpu_custom_call" | custom-call | tf_op jit(solution)/shard_map/pallas_call | solution.py:639
  23.0 4.5 %shard_map.108 = bf16[96,16,128]{2,1,0:T(8,128)(2,1)} custom-call(bf16[96,16,128]{2,1,0:T(8,128)(2,1)S(1)} %copy-done, s32[16,128]{1,0:T(8,128)S(1)} %copy-done.2, bf16[96,16,128]{2,1,0:T(8,128)(2,1)S(1)} %get-tuple-element.15.halo_ref, f32[16,128]{1,0:T(8,128)S(1)} %get-tuple-element.16.halo_mask_ref, bf16[416,128]{1,0:T(8,128)(2,1)S(1)} %collective-permute-done.2.core_ref, ...), custom_call_target="tpu_custom_call" | custom-call | tf_op jit(solution)/shard_map/pallas_call | solution.py:648
  (1 shorter events, 0.0 us)
Async XLA Ops:
  0.0 1.0 %copy-start = (bf16[96,16,128]{2,1,0:T(8,128)(2,1)S(1)}, bf16[96,16,128]{2,1,0:T(8,128)(2,1)}, u32[]{:S(2)}) copy-start(bf16[96,16,128]{2,1,0:T(8,128)(2,1)} %field_ref.11) | copy-start | bytes 1179652
  0.0 1.0 %copy-start.2 = (s32[16,128]{1,0:T(8,128)S(1)}, s32[16,128]{1,0:T(8,128)}, u32[]{:S(2)}) copy-start(s32[16,128]{1,0:T(8,128)} %mask_ref.7) | copy-start | bytes 24580
  1.2 7.7 %copy-start.3 = (bf16[2,384,96]{1,2,0:T(8,128)(2,1)S(1)}, bf16[2,384,96]{1,2,0:T(8,128)(2,1)}, u32[]{:S(2)}) copy-start(bf16[2,384,96]{1,2,0:T(8,128)(2,1)} %param.16) | copy-start | bytes 442372
  1.2 7.7 %copy-start.4 = (f32[2,96,7,7]{1,0,3,2:T(2,128)S(1)}, f32[2,96,7,7]{1,0,3,2:T(2,128)}, u32[]{:S(2)}) copy-start(f32[2,96,7,7]{1,0,3,2:T(2,128)} %param.12) | copy-start | bytes 112900
  1.2 7.7 %copy-start.5 = (f32[2,384]{1,0:T(2,128)S(1)}, f32[2,384]{1,0:T(2,128)}, u32[]{:S(2)}) copy-start(f32[2,384]{1,0:T(2,128)} %expand_bias_ref.1) | copy-start | bytes 9220
  1.3 7.7 %copy-start.6 = (f32[2,96]{1,0:T(2,128)S(1)}, f32[2,96]{1,0:T(2,128)}, u32[]{:S(2)}) copy-start(f32[2,96]{1,0:T(2,128)} %bias_ref.1) | copy-start | bytes 2308
  1.3 7.7 %copy-start.7 = (f32[2,96]{1,0:T(2,128)S(1)}, f32[2,96]{1,0:T(2,128)}, u32[]{:S(2)}) copy-start(f32[2,96]{1,0:T(2,128)} %gain_ref.1) | copy-start | bytes 2308
  1.3 7.6 %copy-start.8 = (f32[2,96]{1,0:T(2,128)S(1)}, f32[2,96]{1,0:T(2,128)}, u32[]{:S(2)}) copy-start(f32[2,96]{1,0:T(2,128)} %norm_bias_ref.1) | copy-start | bytes 2308
  1.3 7.6 %copy-start.9 = (f32[2,96]{1,0:T(2,128)S(1)}, f32[2,96]{1,0:T(2,128)}, u32[]{:S(2)}) copy-start(f32[2,96]{1,0:T(2,128)} %reduce_bias_ref.1) | copy-start | bytes 2308
  1.3 11.3 %collective-permute-start = (bf16[592,128]{1,0:T(8,128)(2,1)S(1)}, bf16[592,128]{1,0:T(8,128)(2,1)S(1)}, u32[]{:S(2)}, u32[]{:S(2)}) collective-permute-start(bf16[592,128]{1,0:T(8,128)(2,1)S(1)} %shard_map.101.after_ref), channel_id=1, source_target_pairs={{0,1},{1,0},{2,3},{3,2},{4,5},{5,4},{6,7},{7,6},{8,9},{9,8},{10,11... | collective-permute-start | bytes 454664 | tf_op jit(solution)/shard_map/ppermute | solution.py:564
  1.6 11.0 %collective-permute-start.1 = (bf16[592,128]{1,0:T(8,128)(2,1)S(1)}, bf16[592,128]{1,0:T(8,128)(2,1)S(1)}, u32[]{:S(2)}, u32[]{:S(2)}) collective-permute-start(bf16[592,128]{1,0:T(8,128)(2,1)S(1)} %shard_map.102), channel_id=1, source_target_pairs={{1,31},{3,29},{5,27},{7,25},{9,23},{11,21},{13,19},{15,17},{17,15}... | collective-permute-start | bytes 454664 | tf_op jit(solution)/shard_map/ppermute | solution.py:560
  8.9 1.7 %copy-start.1 = (bf16[2,96,384]{2,1,0:T(8,128)(2,1)S(1)}, bf16[2,96,384]{2,1,0:T(8,128)(2,1)}, u32[]{:S(2)}) copy-start(bf16[2,96,384]{2,1,0:T(8,128)(2,1)} %reduce_ref.7) | copy-start | bytes 442372
  13.3 7.5 %collective-permute-start.3 = (bf16[416,128]{1,0:T(8,128)(2,1)S(1)}, bf16[416,128]{1,0:T(8,128)(2,1)S(1)}, u32[]{:S(2)}, u32[]{:S(2)}) collective-permute-start(bf16[416,128]{1,0:T(8,128)(2,1)S(1)} %get-tuple-element.17.ends_ref), channel_id=1, source_target_pairs={{2,4},{4,2},{6,8},{8,6},{10,12},{12,10},{14,16},{16,14},{18,20},{2... | collective-permute-start | bytes 319496 | tf_op jit(solution)/shard_map/ppermute | solution.py:626
  15.3 5.4 %collective-permute-start.2 = (bf16[416,128]{1,0:T(8,128)(2,1)S(1)}, bf16[416,128]{1,0:T(8,128)(2,1)S(1)}, u32[]{:S(2)}, u32[]{:S(2)}) collective-permute-start(bf16[416,128]{1,0:T(8,128)(2,1)S(1)} %get-tuple-element.17.ends_ref), channel_id=1, source_target_pairs={{0,2},{2,0},{4,6},{6,4},{8,10},{10,8},{12,14},{14,12},{16,18},{18,... | collective-permute-start | bytes 319496 | tf_op jit(solution)/shard_map/ppermute | solution.py:621

commit v3 on v2

--- a/solution.py
+++ b/solution.py
@@ -51,73 +51,117 @@
     out_ref[at, :] = jnp.where(take_upper, upper, lower).astype(jnp.bfloat16)
 
 
+def north_place(row):
+    return jnp.where(row < 3, 4 + row, 9 + row)
+
+
 def south_place(k):
     return k - 3 if k >= 3 else 8 + k
 
 
+def place_rows(received_ref, is_north, turned, wide, mask_rows, channels):
+    width = received_ref.shape[1]
+    wide[...] = jnp.zeros_like(wide)
+    mask_rows[...] = jnp.zeros_like(mask_rows)
+    turn = None
+    if turned is not None:
+        sub = lax.broadcasted_iota(jnp.int32, (width, width), 0)
+        target = lanes((width, width))
+        turn = sub == jnp.where(turned, width - 1 - target, target)
+        turn = turn.astype(jnp.float32).astype(jnp.bfloat16)
+
+    def rows_at(start, count):
+        block = received_ref[start : start + count, :]
+        if turn is None:
+            return block.astype(jnp.float32)
+        return jnp.dot(block, turn, preferred_element_type=jnp.float32)
+
+    masks = rows_at(HALO * channels, 16)
+    for k in range(HALO):
+        row = k if turned is None else jnp.where(turned, HALO - 1 - k, k)
+        place = jnp.where(is_north, north_place(row), south_place(k))
+        wide[pl.ds(place, channels, stride=16), :] = rows_at(k * channels, channels)
+        mask_rows[pl.ds(place, 1), :] = masks[k : k + 1, :]
+
+
+def pack_ends(blocks):
+    rows, width = blocks[0].shape
+    slot = lanes((rows, width)) // 16
+    packed = jnp.zeros((rows, width), jnp.bfloat16)
+    for j, block in enumerate(blocks):
+        packed = jnp.where(slot == j, pltpu.roll(block, 16 * j + HALO, 1), packed)
+    return packed
+
+
 def channel_of(channels, group, slot):
     return slot // 2 * (channels // 4) + group * 2 + slot % 2
 
 
-def join_rows(
-    field_ref,
-    mask_ref,
-    first_ref,
+def near_rows(field_ref, mask_ref, first_ref, halo_ref, mask_rows, ends_ref, wide):
+    channels, rows, width = field_ref.shape
+    even = lax.rem(lax.axis_index("lat"), 2) == 0
+    place_rows(first_ref, even, None, wide, mask_rows, channels)
+    halo_ref[...] = wide[...].astype(jnp.bfloat16).reshape(channels, 16, width)
+    groups = channels // 8
+    for g in range(groups):
+        blocks = [field_ref[channel_of(channels, g, j)] for j in range(8)]
+        ends_ref[g * 16 : g * 16 + 16, :] = pack_ends(blocks)
+    mask = mask_ref[...].astype(jnp.float32).astype(jnp.bfloat16)
+    ends_ref[groups * 16 :, :] = pack_ends([mask])
+
+
+def pack_side(ends_ref, out_ref, to_east):
+    width = ends_ref.shape[1]
+    groups = ends_ref.shape[0] // 32 - 1
+    lower = lanes((32, width)) % 16 < 8
+    for m in range(groups // 2 + 1):
+        n = m if m < groups // 2 else groups
+        one = ends_ref[n * 32 : n * 32 + 32, :]
+        one = jnp.where(to_east, one, pltpu.roll(one, width - HALO, 1))
+        if n < groups:
+            two = ends_ref[(n + groups // 2) * 32 : (n + groups // 2) * 32 + 32, :]
+            two = jnp.where(to_east, pltpu.roll(two, 8, 1), pltpu.roll(two, 8 - HALO, 1))
+            one = jnp.where(lower, one, two)
+        out_ref[m * 32 : m * 32 + 32, :] = one
+
+
+def far_rows(
     second_ref,
+    near_halo_ref,
+    near_mask_ref,
+    own_ends_ref,
     after_ref,
     halo_ref,
     halo_mask_ref,
     ends_ref,
+    cross_ref,
     wide,
+    mask_rows,
 ):
     del after_ref
-    channels, rows, width = field_ref.shape
+    channels, _, width = halo_ref.shape
     lat = lax.axis_index("lat")
-    even = lax.rem(lat, 2) == 0
+    odd = lax.rem(lat, 2) == 1
     folded = lat == lax.axis_size("lat") - 1
-    wide[...] = jnp.zeros_like(wide)
-    halo_mask_ref[...] = jnp.zeros_like(halo_mask_ref)
-    sub = lax.broadcasted_iota(jnp.int32, (width, width), 0)
-    target = lanes((width, width))
-    turn = sub == jnp.where(folded, width - 1 - target, target)
-    turn = turn.astype(jnp.float32).astype(jnp.bfloat16)
-
-    def split(one, two):
-        north = jnp.where(even, one, two)
-        south = jnp.where(even, two, one)
-        north = jnp.dot(north, turn, preferred_element_type=jnp.float32)
-        return north, south.astype(jnp.float32)
-
-    at = slice(HALO * channels, HALO * channels + 16)
-    mask_north, mask_south = split(first_ref[at, :], second_ref[at, :])
-    for k in range(HALO):
-        at = slice(k * channels, (k + 1) * channels)
-        north, south = split(first_ref[at, :], second_ref[at, :])
-        beyond = jnp.where(folded, HALO - 1 - k, k)
-        place = jnp.where(beyond < 3, 4 + beyond, 9 + beyond)
-        wide[pl.ds(place, channels, stride=16), :] = north
-        wide[pl.ds(south_place(k), channels, stride=16), :] = south
-        halo_mask_ref[pl.ds(place, 1), :] = mask_north[k : k + 1, :]
-        halo_mask_ref[south_place(k) : south_place(k) + 1, :] = mask_south[k : k + 1, :]
-    halo_ref[...] = wide[...].astype(jnp.bfloat16).reshape(channels, 16, width)
-
-    slot = lanes((32, width)) // 16
-
-    def ends(blocks):
-        packed = jnp.zeros((32, width), jnp.bfloat16)
-        for j, block in enumerate(blocks):
-            packed = jnp.where(slot == j, pltpu.roll(block, 16 * j + HALO, 1), packed)
-        return packed
-
+    place_rows(second_ref, odd, folded, wide, mask_rows, channels)
+    far = wide[...].astype(jnp.bfloat16).reshape(channels, 16, width)
+    halo_ref[...] = near_halo_ref[...] + far
+    halo_mask = near_mask_ref[...] + mask_rows[...]
+    halo_mask_ref[...] = halo_mask
     groups = channels // 8
-    for g in range(groups):
-        some = [channel_of(channels, g, j) for j in range(8)]
-        blocks = [jnp.concatenate([field_ref[c], halo_ref[c]], axis=0) for c in some]
-        ends_ref[g * 32 : g * 32 + 32, :] = ends(blocks)
-    mask_block = jnp.concatenate(
-        [mask_ref[...].astype(jnp.float32), halo_mask_ref[...]], axis=0
-    ).astype(jnp.bfloat16)
-    ends_ref[groups * 32 :, :] = ends([mask_block])
+    for g in range(groups + 1):
+        if g < groups:
+            blocks = [halo_ref[channel_of(channels, g, j)] for j in range(8)]
+        else:
+            blocks = [halo_mask.astype(jnp.bfloat16)]
+        ends_ref[g * 32 : g * 32 + 16, :] = own_ends_ref[g * 16 : g * 16 + 16, :]
+        ends_ref[g * 32 + 16 : g * 32 + 32, :] = pack_ends(blocks)
+    pack_side(ends_ref, cross_ref, lax.rem(lax.axis_index("lon"), 2) == 1)
+
+
+def core_columns(ends_ref, after_ref, core_ref):
+    del after_ref
+    pack_side(ends_ref, core_ref, lax.rem(lax.axis_index("lon"), 2) == 0)
 
 
 def in_row(place, first_layer):
@@ -340,9 +384,17 @@
     mlp(rows_ref, expand_ref, reduce_ref, 0, blocks, normed, inner, put)
 
 
-def by_side(core, cross):
+def neighbours(core_ref, cross_ref, group, groups):
+    width = core_ref.shape[1]
+    half = groups // 2
+    m, upper = (half, 0) if group == groups else (group % half, group // half)
+    core = core_ref[m * 32 : m * 32 + 32, :]
+    cross = cross_ref[m * 32 : m * 32 + 32, :]
     lon_even = lax.rem(lax.axis_index("lon"), 2) == 0
-    return jnp.where(lon_even, core, cross), jnp.where(lon_even, cross, core)
+    east = jnp.where(lon_even, core, cross)
+    west = jnp.where(lon_even, cross, core)
+    east = pltpu.roll(east, (HALO - 8 * upper) % width, 1)
+    return east, pltpu.roll(west, width - 8, 1) if upper else west
 
 
 def edge_columns(
@@ -367,7 +419,7 @@
     ones = jnp.ones((32, width), jnp.bfloat16)
     for g in range(groups):
         at = slice(g * 32, g * 32 + 32)
-        east, west = by_side(core_ref[at, :], cross_ref[at, :])
+        east, west = neighbours(core_ref, cross_ref, g, groups)
         own = ends_ref[at, :]
         at_west = jnp.where(first_six, west, own)
         at_east = jnp.where(first_six, own, east)
@@ -443,8 +495,7 @@
         return beside.astype(jnp.float32)[0:24, :]
 
     def received(g):
-        at = slice(g * 32, g * 32 + 32)
-        east, west = by_side(core_ref[at, :], cross_ref[at, :])
+        east, west = neighbours(core_ref, cross_ref, g, groups)
         return jnp.where(first_six, west, east)
 
     main_mask = jnp.concatenate(
@@ -601,29 +652,54 @@
         cost_estimate=cost(4e9),
     )(field, matrix_one, by_channel, expand, w_reduce)
 
-    strip_rows = (channels // 8 + 1) * 32
-    halo, halo_mask, ends = pl.pallas_call(
-        join_rows,
+    groups = channels // 8 + 1
+    sent_rows = (channels // 16 + 1) * 32
+    near_halo, near_mask, own_ends = pl.pallas_call(
+        near_rows,
         out_shape=[
             jax.ShapeDtypeStruct((channels, 16, width), bf16),
             jax.ShapeDtypeStruct((16, width), f32),
-            jax.ShapeDtypeStruct((strip_rows, width), bf16),
+            jax.ShapeDtypeStruct((groups * 16, width), bf16),
+        ],
+        in_specs=vmem(3),
+        out_specs=vmem(3),
+        scratch_shapes=[pltpu.VMEM((channels * 16, width), f32)],
+        compiler_params=params(),
+        cost_estimate=cost(1e9),
+    )(field, land_mask, first)
+    halo, halo_mask, ends, cross = pl.pallas_call(
+        far_rows,
+        out_shape=[
+            jax.ShapeDtypeStruct((channels, 16, width), bf16),
+            jax.ShapeDtypeStruct((16, width), f32),
+            jax.ShapeDtypeStruct((groups * 32, width), bf16),
+            jax.ShapeDtypeStruct((sent_rows, width), bf16),
         ],
         in_specs=vmem(4) + [pl.BlockSpec(memory_space=pl.ANY)],
-        out_specs=vmem(3),
-        scratch_shapes=[pltpu.VMEM((channels * 16, width), f32)],
-        compiler_params=params(),
-    )(field, land_mask, first, second, update)
+        out_specs=vmem(4),
+        scratch_shapes=[
+            pltpu.VMEM((channels * 16, width), f32),
+            pltpu.VMEM((16, width), f32),
+        ],
+        compiler_params=params(),
+    )(second, near_halo, near_mask, own_ends, update)
+    core = pl.pallas_call(
+        core_columns,
+        out_shape=jax.ShapeDtypeStruct((sent_rows, width), bf16),
+        in_specs=vmem(1) + [pl.BlockSpec(memory_space=pl.ANY)],
+        out_specs=pl.BlockSpec(memory_space=pltpu.VMEM),
+        compiler_params=params(),
+    )(ends, cross)
 
     pairs = []
     for low in range(0, nlon, 2):
         pairs += [(low, low + 1), (low + 1, low)]
-    core = lax.ppermute(ends, "lon", pairs)
+    core = lax.ppermute(core, "lon", pairs)
     pairs = []
     for low in range(1, nlon, 2):
         after = (low + 1) % nlon
         pairs += [(low, after), (after, low)]
-    cross = lax.ppermute(ends, "lon", pairs)
+    cross = lax.ppermute(cross, "lon", pairs)
 
     update = pl.pallas_call(
         edge_rows,

time: 27.7 us -> 28 us (1.011)
  Pallas kernels: 14.1 us -> 14.6 us
  starting transfers between devices: 12.2 us -> 11.9 us
    pallas_call x1 -> x3, Pallas kernels: 0.68 us -> 1.08 us  [the longest x1 0.64 us: per_device(): pl.pallas_call(far_rows, out_shape=[jax.ShapeDtypeStruct((channels, 16, w...]
    ppermute x2, starting transfers between devices: 4.87 us -> 4.58 us  [the longest x1 2.89 us: per_device(): core = lax.ppermute(core, 'lon', pairs)]
  transfers between devices with their start and end apart: 4 -> 4, of which waited for: 0 -> 0; matrix products, arithmetic and copies ran while one was open for 0% -> 0% of each run, Pallas kernels for 23% -> 25%
where the time goes in v3:
time: 28 us; the launch traced here: 27.8 us
  Pallas kernels  14.6 us (52%)
  starting transfers between devices  11.9 us (42%)
  local copies, waits for them, and re-layouts  1.04 us (4%)
    ppermute x1, starting transfers between devices, per_device(): second = lax.ppermute(second, ('lon', 'lat'), pairs)  7.26 us
    pallas_call x1, Pallas kernels, per_device(): pl.pallas_call(second_layer, out_shape=jax.ShapeDtypeStruct((channels, ro...  4.59 us
    ppermute x1, starting transfers between devices, per_device(): core = lax.ppermute(core, 'lon', pairs)  2.89 us
    pallas_call x1, Pallas kernels, per_device(): pl.pallas_call(edge_rows, out_shape=jax.ShapeDtypeStruct((channels * 24,...  2.6 us
    pallas_call x1, Pallas kernels, per_device(): pl.pallas_call(edge_columns, out_shape=jax.ShapeDtypeStruct((channels * 2...  2.3 us
    pallas_call x1, Pallas kernels, per_device(): pl.pallas_call(inner_rows, out_shape=jax.ShapeDtypeStruct((channels * 24,...  1.96 us
    ppermute x1, starting transfers between devices, per_device(): cross = lax.ppermute(cross, 'lon', pairs)  1.69 us
    pallas_call x1, Pallas kernels, per_device(): pl.pallas_call(weights, out_shape=[jax.ShapeDtypeStruct((channels * 24, 2...  1.64 us
  transfers between devices with their start and end apart: 4, of which 0 were waited for; matrix products, arithmetic and copies ran while one was open for 0% of the time, Pallas kernels for 25%

profile of v3, /device:TPU:3, one launch (start us, length us, event | category | flops | bytes accessed | tf_op | source)
XLA Modules:
  0.0 27.8 jit_solution(8848393996876978494)
XLA Ops:
  0.0 0.0 copy-start.1
  0.0 0.0 copy-start.2
  0.0 1.0 %copy-done.1 = bf16[96,16,128]{2,1,0:T(8,128)(2,1)S(1)} copy-done((bf16[96,16,128]{2,1,0:T(8,128)(2,1)S(1)}, bf16[96,16,128]{2,1,0:T(8,128)(2,1)}, u32[]{:S(2)}) %copy-start.1) | copy-done | bytes 393240
  1.0 0.0 copy-done.2
  1.0 0.2 shard_map.101.after_ref
  1.2 0.0 copy-start.3
  1.2 0.0 copy-start.4
  1.2 0.0 copy-start.5
  1.3 0.0 copy-start.6
  1.3 0.0 copy-start.7
  1.3 0.0 copy-start.8
  1.3 0.0 copy-start.9
  1.3 0.1 collective-permute-start.1
  1.4 0.2 shard_map.102
  1.6 7.3 %collective-permute-start = (bf16[592,128]{1,0:T(8,128)(2,1)S(1)}, bf16[592,128]{1,0:T(8,128)(2,1)S(1)}, u32[]{:S(2)}, u32[]{:S(2)}) collective-permute-start(bf16[592,128]{1,0:T(8,128)(2,1)S(1)} %shard_map.102), channel_id=1, source_target_pairs={{1,31},{3,29},{5,27},{7,25},{9,23},{11,21},{13,19},{15,17},{17,15}... | collective-permute-start | bytes 454664 | tf_op jit(solution)/shard_map/ppermute | solution.py:611
  8.9 0.0 copy-done.3
  8.9 0.0 copy-done.4
  8.9 0.0 copy-done.5
  8.9 0.0 copy-done.6
  8.9 0.0 copy-done.7
  8.9 0.0 copy-done.8
  8.9 0.0 copy-done.9
  8.9 0.0 copy-start
  9.0 1.6 %shard_map.104 = (bf16[2304,256]{1,0:T(8,128)(2,1)S(1)}, bf16[1536,256]{1,0:T(8,128)(2,1)S(1)}, f32[2,3,96,128]{3,2,1,0:T(8,128)S(1)}, bf16[2,384,112]{2,1,0:T(8,128)(2,1)S(1)}) custom-call(f32[49,2,96]{2,1,0:T(2,128)S(1)} %bitcast.5, f32[2,96]{1,0:T(2,128)S(1)} %copy-done.6, f32[2,96]{1,0:T(2,128)S(1)} %copy-done.7, f32[2,96]{1,0:T(2,128)S(1)} %copy-done.8, ...), custom_call_target="tpu_custom_call" | custom-call | flops 2000000000 | bytes 1048576 | tf_op jit(solution)/shard_map/pallas_call | solution.py:618
  10.6 0.0 copy-done
  10.6 2.0 %shard_map.105.after_ref.old_ref = f32[2304,128]{1,0:T(8,128)S(1)} custom-call(bf16[96,16,128]{2,1,0:T(8,128)(2,1)S(1)} %copy-done.1, bf16[2304,256]{1,0:T(8,128)(2,1)S(1)} %get-tuple-element.19.matrix_ref, f32[2,3,96,128]{3,2,1,0:T(8,128)S(1)} %get-tuple-element.20.rows_ref, bf16[2,384,112]{2,1,0:T(8,128)(2,1)S(1)} %get-tuple-element.21.expand_ref, ...), custom_call_target="tpu_custom_call" | custom-call | flops 4000000000 | bytes 1048576 | tf_op jit(solution)/shard_map/pallas_call | solution.py:645
  12.6 0.0 collective-permute-done.1.first_ref
  12.6 0.3 %shard_map.103 = (bf16[96,16,128]{2,1,0:T(8,128)(2,1)S(1)}, f32[16,128]{1,0:T(8,128)S(1)}, bf16[208,128]{1,0:T(8,128)(2,1)S(1)}) custom-call(bf16[96,16,128]{2,1,0:T(8,128)(2,1)S(1)} %copy-done.1, s32[16,128]{1,0:T(8,128)S(1)} %copy-done.2, bf16[592,128]{1,0:T(8,128)(2,1)S(1)} %collective-permute-done.1.first_ref), custom_call_target="tpu_custom_call" | custom-call | flops 1000000000 | bytes 1048576 | tf_op jit(solution)/shard_map/pallas_call | solution.py:657
  12.9 0.0 collective-permute-done.second_ref
  13.0 0.6 %shard_map.106 = (bf16[96,16,128]{2,1,0:T(8,128)(2,1)S(1)}, f32[16,128]{1,0:T(8,128)S(1)}, bf16[416,128]{1,0:T(8,128)(2,1)S(1)}, bf16[224,128]{1,0:T(8,128)(2,1)S(1)}) custom-call(bf16[592,128]{1,0:T(8,128)(2,1)S(1)} %collective-permute-done.second_ref, bf16[96,16,128]{2,1,0:T(8,128)(2,1)S(1)} %get-tuple-element.16.near_halo_ref, ...), custom_call_target="tpu_custom_call" | custom-call | tf_op jit(solution)/shard_map/pallas_call | solution.py:670
  13.6 1.7 %collective-permute-start.3 = (bf16[224,128]{1,0:T(8,128)(2,1)S(1)}, bf16[224,128]{1,0:T(8,128)(2,1)S(1)}, u32[]{:S(2)}, u32[]{:S(2)}) collective-permute-start(bf16[224,128]{1,0:T(8,128)(2,1)S(1)} %get-tuple-element.25.after_ref), channel_id=1, source_target_pairs={{2,4},{4,2},{6,8},{8,6},{10,12},{12,10},{14,16},{16,14},{18,20},{2... | collective-permute-start | bytes 172040 | tf_op jit(solution)/shard_map/ppermute | solution.py:702
  15.3 0.1 shard_map.107
  15.4 2.9 %collective-permute-start.2 = (bf16[224,128]{1,0:T(8,128)(2,1)S(1)}, bf16[224,128]{1,0:T(8,128)(2,1)S(1)}, u32[]{:S(2)}, u32[]{:S(2)}) collective-permute-start(bf16[224,128]{1,0:T(8,128)(2,1)S(1)} %shard_map.107), channel_id=1, source_target_pairs={{0,2},{2,0},{4,6},{6,4},{8,10},{10,8},{12,14},{14,12},{16,18},{18,... | collective-permute-start | bytes 172040 | tf_op jit(solution)/shard_map/ppermute | solution.py:697
  18.3 2.6 %shard_map.109.update_ref = f32[2304,128]{1,0:T(8,128)S(1)} custom-call(bf16[96,16,128]{2,1,0:T(8,128)(2,1)S(1)} %copy-done.1, bf16[96,16,128]{2,1,0:T(8,128)(2,1)S(1)} %get-tuple-element.22.halo_ref, bf16[2304,256]{1,0:T(8,128)(2,1)S(1)} %get-tuple-element.19.matrix_ref, ...), custom_call_target="tpu_custom_call", output_to_operand_aliasing={{}: (6, {})} | custom-call | flops 4000000000 | bytes 1048576 | tf_op jit(solution)/shard_map/pallas_call | solution.py:704
  20.9 0.0 collective-permute-done.2.core_ref
  20.9 0.0 collective-permute-done.3.cross_ref
  20.9 2.3 %shard_map.108.strips = f32[2304,128]{1,0:T(8,128)S(1)} custom-call(bf16[224,128]{1,0:T(8,128)(2,1)S(1)} %collective-permute-done.2.core_ref, bf16[224,128]{1,0:T(8,128)(2,1)S(1)} %collective-permute-done.3.cross_ref, bf16[416,128]{1,0:T(8,128)(2,1)S(1)} %get-tuple-element.24.ends_ref, bf16[2304,256]{1,0:T(8,128)(2,1)S(1)} %get-tuple-element.19.matrix_ref, ...), custom_call_target="tpu_custom_call" | custom-call | tf_op jit(solution)/shard_map/pallas_call | solution.py:715
  23.2 4.6 %shard_map.110 = bf16[96,16,128]{2,1,0:T(8,128)(2,1)} custom-call(bf16[96,16,128]{2,1,0:T(8,128)(2,1)S(1)} %copy-done.1, s32[16,128]{1,0:T(8,128)S(1)} %copy-done.2, bf16[96,16,128]{2,1,0:T(8,128)(2,1)S(1)} %get-tuple-element.22.halo_ref, f32[16,128]{1,0:T(8,128)S(1)} %get-tuple-element.23.halo_mask_ref, ...), custom_call_target="tpu_custom_call" | custom-call | tf_op jit(solution)/shard_map/pallas_call | solution.py:724
  (1 shorter events, 0.0 us)
Async XLA Ops:
  0.0 1.0 %copy-start.1 = (bf16[96,16,128]{2,1,0:T(8,128)(2,1)S(1)}, bf16[96,16,128]{2,1,0:T(8,128)(2,1)}, u32[]{:S(2)}) copy-start(bf16[96,16,128]{2,1,0:T(8,128)(2,1)} %field_ref.11) | copy-start | bytes 1179652
  0.0 1.0 %copy-start.2 = (s32[16,128]{1,0:T(8,128)S(1)}, s32[16,128]{1,0:T(8,128)}, u32[]{:S(2)}) copy-start(s32[16,128]{1,0:T(8,128)} %mask_ref.7) | copy-start | bytes 24580
  1.2 7.7 %copy-start.3 = (bf16[2,384,96]{1,2,0:T(8,128)(2,1)S(1)}, bf16[2,384,96]{1,2,0:T(8,128)(2,1)}, u32[]{:S(2)}) copy-start(bf16[2,384,96]{1,2,0:T(8,128)(2,1)} %param.16) | copy-start | bytes 442372
  1.2 7.7 %copy-start.4 = (f32[2,96,7,7]{1,0,3,2:T(2,128)S(1)}, f32[2,96,7,7]{1,0,3,2:T(2,128)}, u32[]{:S(2)}) copy-start(f32[2,96,7,7]{1,0,3,2:T(2,128)} %param.12) | copy-start | bytes 112900
  1.2 7.7 %copy-start.5 = (f32[2,384]{1,0:T(2,128)S(1)}, f32[2,384]{1,0:T(2,128)}, u32[]{:S(2)}) copy-start(f32[2,384]{1,0:T(2,128)} %expand_bias_ref.1) | copy-start | bytes 9220
  1.3 7.7 %copy-start.6 = (f32[2,96]{1,0:T(2,128)S(1)}, f32[2,96]{1,0:T(2,128)}, u32[]{:S(2)}) copy-start(f32[2,96]{1,0:T(2,128)} %bias_ref.1) | copy-start | bytes 2308
  1.3 7.7 %copy-start.7 = (f32[2,96]{1,0:T(2,128)S(1)}, f32[2,96]{1,0:T(2,128)}, u32[]{:S(2)}) copy-start(f32[2,96]{1,0:T(2,128)} %gain_ref.1) | copy-start | bytes 2308
  1.3 7.6 %copy-start.8 = (f32[2,96]{1,0:T(2,128)S(1)}, f32[2,96]{1,0:T(2,128)}, u32[]{:S(2)}) copy-start(f32[2,96]{1,0:T(2,128)} %norm_bias_ref.1) | copy-start | bytes 2308
  1.3 7.6 %copy-start.9 = (f32[2,96]{1,0:T(2,128)S(1)}, f32[2,96]{1,0:T(2,128)}, u32[]{:S(2)}) copy-start(f32[2,96]{1,0:T(2,128)} %reduce_bias_ref.1) | copy-start | bytes 2308
  1.3 11.3 %collective-permute-start.1 = (bf16[592,128]{1,0:T(8,128)(2,1)S(1)}, bf16[592,128]{1,0:T(8,128)(2,1)S(1)}, u32[]{:S(2)}, u32[]{:S(2)}) collective-permute-start(bf16[592,128]{1,0:T(8,128)(2,1)S(1)} %shard_map.101.after_ref), channel_id=1, source_target_pairs={{0,1},{1,0},{2,3},{3,2},{4,5},{5,4},{6,7},{7,6},{8,9},{9,8},{10,11... | collective-permute-start | bytes 454664 | tf_op jit(solution)/shard_map/ppermute | solution.py:615
  1.6 11.3 %collective-permute-start = (bf16[592,128]{1,0:T(8,128)(2,1)S(1)}, bf16[592,128]{1,0:T(8,128)(2,1)S(1)}, u32[]{:S(2)}, u32[]{:S(2)}) collective-permute-start(bf16[592,128]{1,0:T(8,128)(2,1)S(1)} %shard_map.102), channel_id=1, source_target_pairs={{1,31},{3,29},{5,27},{7,25},{9,23},{11,21},{13,19},{15,17},{17,15}... | collective-permute-start | bytes 454664 | tf_op jit(solution)/shard_map/ppermute | solution.py:611
  8.9 1.7 %copy-start = (bf16[2,96,384]{2,1,0:T(8,128)(2,1)S(1)}, bf16[2,96,384]{2,1,0:T(8,128)(2,1)}, u32[]{:S(2)}) copy-start(bf16[2,96,384]{2,1,0:T(8,128)(2,1)} %reduce_ref.7) | copy-start | bytes 442372
  13.6 7.3 %collective-permute-start.3 = (bf16[224,128]{1,0:T(8,128)(2,1)S(1)}, bf16[224,128]{1,0:T(8,128)(2,1)S(1)}, u32[]{:S(2)}, u32[]{:S(2)}) collective-permute-start(bf16[224,128]{1,0:T(8,128)(2,1)S(1)} %get-tuple-element.25.after_ref), channel_id=1, source_target_pairs={{2,4},{4,2},{6,8},{8,6},{10,12},{12,10},{14,16},{16,14},{18,20},{2... | collective-permute-start | bytes 172040 | tf_op jit(solution)/shard_map/ppermute | solution.py:702
  15.4 5.5 %collective-permute-start.2 = (bf16[224,128]{1,0:T(8,128)(2,1)S(1)}, bf16[224,128]{1,0:T(8,128)(2,1)S(1)}, u32[]{:S(2)}, u32[]{:S(2)}) collective-permute-start(bf16[224,128]{1,0:T(8,128)(2,1)S(1)} %shard_map.107), channel_id=1, source_target_pairs={{0,2},{2,0},{4,6},{6,4},{8,10},{10,8},{12,14},{14,12},{16,18},{18,... | collective-permute-start | bytes 172040 | tf_op jit(solution)/shard_map/ppermute | solution.py:697

commit v4 on v3

--- a/solution.py
+++ b/solution.py
@@ -97,7 +97,14 @@
     return slot // 2 * (channels // 4) + group * 2 + slot % 2
 
 
-def near_rows(field_ref, mask_ref, first_ref, halo_ref, mask_rows, ends_ref, wide):
+def over_wrap():
+    lon = lax.axis_index("lon")
+    return (lon == 0) | (lon == lax.axis_size("lon") - 1)
+
+
+def near_rows(
+    field_ref, mask_ref, first_ref, halo_ref, mask_rows, ends_ref, wrap_ref, wide, all_ends
+):
     channels, rows, width = field_ref.shape
     even = lax.rem(lax.axis_index("lat"), 2) == 0
     place_rows(first_ref, even, None, wide, mask_rows, channels)
@@ -108,6 +115,27 @@
         ends_ref[g * 16 : g * 16 + 16, :] = pack_ends(blocks)
     mask = mask_ref[...].astype(jnp.float32).astype(jnp.bfloat16)
     ends_ref[groups * 16 :, :] = pack_ends([mask])
+    wrap_ref[...] = jnp.zeros_like(wrap_ref)
+
+    @pl.when(over_wrap())
+    def _():
+        join_ends(ends_ref, halo_ref, mask_rows, all_ends)
+        pack_side(all_ends, wrap_ref, lax.rem(lax.axis_index("lon"), 2) == 1)
+
+
+def join_ends(own_ends_ref, halo_ref, mask_rows, ends_ref):
+    channels = halo_ref.shape[0]
+    groups = channels // 8
+    for g in range(groups + 1):
+        if g < groups:
+            blocks = [halo_ref[channel_of(channels, g, j)] for j in range(8)]
+        else:
+            blocks = [mask_rows[...].astype(jnp.bfloat16)]
+        own = jnp.zeros((16, halo_ref.shape[2]), jnp.bfloat16)
+        if own_ends_ref is not None:
+            own = own_ends_ref[g * 16 : g * 16 + 16, :]
+        ends_ref[g * 32 : g * 32 + 16, :] = own
+        ends_ref[g * 32 + 16 : g * 32 + 32, :] = pack_ends(blocks)
 
 
 def pack_side(ends_ref, out_ref, to_east):
@@ -126,7 +154,9 @@
 
 
 def far_rows(
+    mirrored,
     second_ref,
+    sent_ref,
     near_halo_ref,
     near_mask_ref,
     own_ends_ref,
@@ -135,6 +165,7 @@
     halo_mask_ref,
     ends_ref,
     cross_ref,
+    own_ref,
     wide,
     mask_rows,
 ):
@@ -142,21 +173,24 @@
     channels, _, width = halo_ref.shape
     lat = lax.axis_index("lat")
     odd = lax.rem(lat, 2) == 1
+    lon_odd = lax.rem(lax.axis_index("lon"), 2) == 1
     folded = lat == lax.axis_size("lat") - 1
+    own_ref[...] = jnp.zeros_like(own_ref)
+    if mirrored:
+
+        @pl.when(folded & over_wrap())
+        def _():
+            place_rows(sent_ref, odd, folded, wide, mask_rows, channels)
+            halo_ref[...] = wide[...].astype(jnp.bfloat16).reshape(channels, 16, width)
+            join_ends(None, halo_ref, mask_rows, ends_ref)
+            pack_side(ends_ref, own_ref, jnp.logical_not(lon_odd))
+
     place_rows(second_ref, odd, folded, wide, mask_rows, channels)
     far = wide[...].astype(jnp.bfloat16).reshape(channels, 16, width)
     halo_ref[...] = near_halo_ref[...] + far
-    halo_mask = near_mask_ref[...] + mask_rows[...]
-    halo_mask_ref[...] = halo_mask
-    groups = channels // 8
-    for g in range(groups + 1):
-        if g < groups:
-            blocks = [halo_ref[channel_of(channels, g, j)] for j in range(8)]
-        else:
-            blocks = [halo_mask.astype(jnp.bfloat16)]
-        ends_ref[g * 32 : g * 32 + 16, :] = own_ends_ref[g * 16 : g * 16 + 16, :]
-        ends_ref[g * 32 + 16 : g * 32 + 32, :] = pack_ends(blocks)
-    pack_side(ends_ref, cross_ref, lax.rem(lax.axis_index("lon"), 2) == 1)
+    halo_mask_ref[...] = near_mask_ref[...] + mask_rows[...]
+    join_ends(own_ends_ref, halo_ref, halo_mask_ref, ends_ref)
+    pack_side(ends_ref, cross_ref, lon_odd)
 
 
 def core_columns(ends_ref, after_ref, core_ref):
@@ -384,12 +418,12 @@
     mlp(rows_ref, expand_ref, reduce_ref, 0, blocks, normed, inner, put)
 
 
-def neighbours(core_ref, cross_ref, group, groups):
+def neighbours(core_ref, cross_refs, group, groups):
     width = core_ref.shape[1]
     half = groups // 2
     m, upper = (half, 0) if group == groups else (group % half, group // half)
     core = core_ref[m * 32 : m * 32 + 32, :]
-    cross = cross_ref[m * 32 : m * 32 + 32, :]
+    cross = sum(ref[m * 32 : m * 32 + 32, :] for ref in cross_refs)
     lon_even = lax.rem(lax.axis_index("lon"), 2) == 0
     east = jnp.where(lon_even, core, cross)
     west = jnp.where(lon_even, cross, core)
@@ -400,6 +434,8 @@
 def edge_columns(
     core_ref,
     cross_ref,
+    wrap_ref,
+    own_ref,
     ends_ref,
     matrix_ref,
     rows_ref,
@@ -419,7 +455,7 @@
     ones = jnp.ones((32, width), jnp.bfloat16)
     for g in range(groups):
         at = slice(g * 32, g * 32 + 32)
-        east, west = neighbours(core_ref, cross_ref, g, groups)
+        east, west = neighbours(core_ref, (cross_ref, wrap_ref, own_ref), g, groups)
         own = ends_ref[at, :]
         at_west = jnp.where(first_six, west, own)
         at_east = jnp.where(first_six, own, east)
@@ -472,6 +508,8 @@
     halo_mask_ref,
     core_ref,
     cross_ref,
+    wrap_ref,
+    own_ref,
     strips,
     update_ref,
     matrix_ref,
@@ -495,7 +533,7 @@
         return beside.astype(jnp.float32)[0:24, :]
 
     def received(g):
-        east, west = neighbours(core_ref, cross_ref, g, groups)
+        east, west = neighbours(core_ref, (cross_ref, wrap_ref, own_ref), g, groups)
         return jnp.where(first_six, west, east)
 
     main_mask = jnp.concatenate(
@@ -600,15 +638,19 @@
         cost_estimate=cost(4e9),
     )()
     first = pack(True, begun)
-    second = pack(False, first)
+    second_sent = pack(False, first)
+
+    alone = nlat == 2
+
+    def at(d, lat):
+        return d * nlat + lat
 
     pairs = []
     for d in range(nlon):
-        at = d * nlat
         for low in range(1, nlat - 1, 2):
-            pairs += [(at + low, at + low + 1), (at + low + 1, at + low)]
-        pairs.append((at + nlat - 1, (nlon - 1 - d) * nlat + nlat - 1))
-    second = lax.ppermute(second, ("lon", "lat"), pairs)
+            pairs += [(at(d, low), at(d, low + 1)), (at(d, low + 1), at(d, low))]
+        pairs.append((at(d, nlat - 1), at(nlon - 1 - d, nlat - 1)))
+    second = lax.ppermute(second_sent, ("lon", "lat"), pairs)
     pairs = []
     for low in range(0, nlat - 1, 2):
         pairs += [(low, low + 1), (low + 1, low)]
@@ -654,35 +696,47 @@
 
     groups = channels // 8 + 1
     sent_rows = (channels // 16 + 1) * 32
-    near_halo, near_mask, own_ends = pl.pallas_call(
+    near_halo, near_mask, own_ends, wrap = pl.pallas_call(
         near_rows,
         out_shape=[
             jax.ShapeDtypeStruct((channels, 16, width), bf16),
             jax.ShapeDtypeStruct((16, width), f32),
             jax.ShapeDtypeStruct((groups * 16, width), bf16),
+            jax.ShapeDtypeStruct((sent_rows, width), bf16),
         ],
         in_specs=vmem(3),
-        out_specs=vmem(3),
-        scratch_shapes=[pltpu.VMEM((channels * 16, width), f32)],
+        out_specs=vmem(4),
+        scratch_shapes=[
+            pltpu.VMEM((channels * 16, width), f32),
+            pltpu.VMEM((groups * 32, width), bf16),
+        ],
         compiler_params=params(),
         cost_estimate=cost(1e9),
     )(field, land_mask, first)
-    halo, halo_mask, ends, cross = pl.pallas_call(
-        far_rows,
+    if alone:
+        pairs = []
+        for lat in range(nlat):
+            pairs += [(lat, at(nlon - 1, lat)), (at(nlon - 1, lat), lat)]
+        wrap = lax.ppermute(wrap, ("lon", "lat"), pairs)
+    else:
+        wrap = jnp.zeros_like(wrap)
+    halo, halo_mask, ends, cross, own = pl.pallas_call(
+        functools.partial(far_rows, alone),
         out_shape=[
             jax.ShapeDtypeStruct((channels, 16, width), bf16),
             jax.ShapeDtypeStruct((16, width), f32),
             jax.ShapeDtypeStruct((groups * 32, width), bf16),
             jax.ShapeDtypeStruct((sent_rows, width), bf16),
+            jax.ShapeDtypeStruct((sent_rows, width), bf16),
         ],
-        in_specs=vmem(4) + [pl.BlockSpec(memory_space=pl.ANY)],
-        out_specs=vmem(4),
+        in_specs=vmem(5) + [pl.BlockSpec(memory_space=pl.ANY)],
+        out_specs=vmem(5),
         scratch_shapes=[
             pltpu.VMEM((channels * 16, width), f32),
             pltpu.VMEM((16, width), f32),
         ],
         compiler_params=params(),
-    )(second, near_halo, near_mask, own_ends, update)
+    )(second, second_sent, near_halo, near_mask, own_ends, update)
     core = pl.pallas_call(
         core_columns,
         out_shape=jax.ShapeDtypeStruct((sent_rows, width), bf16),
@@ -698,7 +752,8 @@
     pairs = []
     for low in range(1, nlon, 2):
         after = (low + 1) % nlon
-        pairs += [(low, after), (after, low)]
+        if after or not alone:
+            pairs += [(low, after), (after, low)]
     cross = lax.ppermute(cross, "lon", pairs)
 
     update = pl.pallas_call(
@@ -715,16 +770,16 @@
     strips = pl.pallas_call(
         edge_columns,
         out_shape=jax.ShapeDtypeStruct((channels * 24, width), f32),
-        in_specs=vmem(7),
+        in_specs=vmem(9),
         out_specs=pl.BlockSpec(memory_space=pltpu.VMEM),
         scratch_shapes=[pltpu.VMEM((channels * 24, width), f32)] + buffers(3),
         compiler_params=params(),
-    )(core, cross, ends, matrix_one, by_channel, expand, w_reduce)
+    )(core, cross, wrap, own, ends, matrix_one, by_channel, expand, w_reduce)
 
     return pl.pallas_call(
         second_layer,
         out_shape=jax.ShapeDtypeStruct((channels, rows, width), bf16),
-        in_specs=vmem(12),
+        in_specs=vmem(14),
         out_specs=pl.BlockSpec(memory_space=pltpu.VMEM),
         scratch_shapes=[
             pltpu.VMEM((channels, rows, width), bf16),
@@ -739,6 +794,8 @@
         halo_mask,
         core,
         cross,
+        wrap,
+        own,
         strips,
         update,
         matrix_two,

time: 28 us -> 28.7 us (1.025)
  the two profiles are of different devices: /device:TPU:3 before, /device:TPU:7 now
where the time goes in v4:
time: 28.7 us; the launch traced here: 28.5 us
  Pallas kernels  14.6 us (51%)
  starting transfers between devices  12.4 us (43%)
  local copies, waits for them, and re-layouts  1.04 us (4%)
    ppermute x1, starting transfers between devices, per_device(): second = lax.ppermute(second_sent, ('lon', 'lat'), pairs)  6.01 us
    ppermute x1, starting transfers between devices, per_device(): cross = lax.ppermute(cross, 'lon', pairs)  5.35 us
    pallas_call x1, Pallas kernels, per_device(): pl.pallas_call(second_layer, out_shape=jax.ShapeDtypeStruct((channels, ro...  4.59 us
    pallas_call x1, Pallas kernels, per_device(): pl.pallas_call(edge_rows, out_shape=jax.ShapeDtypeStruct((channels * 24,...  2.6 us
    pallas_call x1, Pallas kernels, per_device(): pl.pallas_call(edge_columns, out_shape=jax.ShapeDtypeStruct((channels * 2...  2.3 us
    pallas_call x1, Pallas kernels, per_device(): pl.pallas_call(inner_rows, out_shape=jax.ShapeDtypeStruct((channels * 24,...  1.96 us
    pallas_call x1, Pallas kernels, per_device(): pl.pallas_call(weights, out_shape=[jax.ShapeDtypeStruct((channels * 24, 2...  1.65 us
    unnamed x20, local copies, waits for them, and re-layouts  1.04 us
  transfers between devices with their start and end apart: 5, of which 1 were waited for; matrix products, arithmetic and copies ran while one was open for 0% of the time, Pallas kernels for 26%

profile of v4, /device:TPU:7, one launch (start us, length us, event | category | flops | bytes accessed | tf_op | source)
XLA Modules:
  0.0 28.5 jit_solution(7616733043998401919)
XLA Ops:
  0.0 0.0 copy-start.1
  0.0 0.0 copy-start.2
  0.0 1.0 %copy-done.1 = bf16[96,16,128]{2,1,0:T(8,128)(2,1)S(1)} copy-done((bf16[96,16,128]{2,1,0:T(8,128)(2,1)S(1)}, bf16[96,16,128]{2,1,0:T(8,128)(2,1)}, u32[]{:S(2)}) %copy-start.1) | copy-done | bytes 393240
  1.0 0.0 copy-done.2
  1.0 0.2 shard_map.101.after_ref
  1.2 0.0 copy-start.3
  1.2 0.0 copy-start.4
  1.2 0.0 copy-start.5
  1.3 0.0 copy-start.6
  1.3 0.0 copy-start.7
  1.3 0.0 copy-start.8
  1.3 0.0 copy-start.9
  1.3 0.3 %collective-permute-start.1 = (bf16[592,128]{1,0:T(8,128)(2,1)S(1)}, bf16[592,128]{1,0:T(8,128)(2,1)S(1)}, u32[]{:S(2)}, u32[]{:S(2)}) collective-permute-start(bf16[592,128]{1,0:T(8,128)(2,1)S(1)} %shard_map.101.after_ref), channel_id=1, source_target_pairs={{0,1},{1,0},{2,3},{3,2},{4,5},{5,4},{6,7},{7,6},{8,9},{9,8},{10,11... | collective-permute-start | bytes 454664 | tf_op jit(solution)/shard_map/ppermute | solution.py:657
  1.6 0.2 shard_map.102.sent_ref
  1.8 6.0 %collective-permute-start = (bf16[592,128]{1,0:T(8,128)(2,1)S(1)}, bf16[592,128]{1,0:T(8,128)(2,1)S(1)}, u32[]{:S(2)}, u32[]{:S(2)}) collective-permute-start(bf16[592,128]{1,0:T(8,128)(2,1)S(1)} %shard_map.102.sent_ref), channel_id=1, source_target_pairs={{1,31},{3,29},{5,27},{7,25},{9,23},{11,21},{13,19},{15,17},{17,15}... | collective-permute-start | bytes 454664 | tf_op jit(solution)/shard_map/ppermute | solution.py:653
  7.9 0.0 copy-done.3
  7.9 0.0 copy-done.4
  7.9 0.0 copy-done.5
  7.9 0.0 copy-done.6
  7.9 0.0 copy-done.7
  7.9 0.0 copy-done.8
  7.9 0.0 copy-done.9
  7.9 0.0 copy-start
  7.9 1.6 %shard_map.104 = (bf16[2304,256]{1,0:T(8,128)(2,1)S(1)}, bf16[1536,256]{1,0:T(8,128)(2,1)S(1)}, f32[2,3,96,128]{3,2,1,0:T(8,128)S(1)}, bf16[2,384,112]{2,1,0:T(8,128)(2,1)S(1)}) custom-call(f32[49,2,96]{2,1,0:T(2,128)S(1)} %bitcast.5, f32[2,96]{1,0:T(2,128)S(1)} %copy-done.6, f32[2,96]{1,0:T(2,128)S(1)} %copy-done.7, f32[2,96]{1,0:T(2,128)S(1)} %copy-done.8, ...), custom_call_target="tpu_custom_call" | custom-call | flops 2000000000 | bytes 1048576 | tf_op jit(solution)/shard_map/pallas_call | solution.py:660
  9.6 0.0 copy-done
  9.6 2.0 %shard_map.105.after_ref.old_ref = f32[2304,128]{1,0:T(8,128)S(1)} custom-call(bf16[96,16,128]{2,1,0:T(8,128)(2,1)S(1)} %copy-done.1, bf16[2304,256]{1,0:T(8,128)(2,1)S(1)} %get-tuple-element.21.matrix_ref, f32[2,3,96,128]{3,2,1,0:T(8,128)S(1)} %get-tuple-element.22.rows_ref, bf16[2,384,112]{2,1,0:T(8,128)(2,1)S(1)} %get-tuple-element.23.expand_ref, ...), custom_call_target="tpu_custom_call" | custom-call | flops 4000000000 | bytes 1048576 | tf_op jit(solution)/shard_map/pallas_call | solution.py:687
  11.6 0.0 collective-permute-done.1.first_ref
  11.6 0.3 %shard_map.103 = (bf16[96,16,128]{2,1,0:T(8,128)(2,1)S(1)}, f32[16,128]{1,0:T(8,128)S(1)}, bf16[208,128]{1,0:T(8,128)(2,1)S(1)}, bf16[224,128]{1,0:T(8,128)(2,1)S(1)}) custom-call(bf16[96,16,128]{2,1,0:T(8,128)(2,1)S(1)} %copy-done.1, s32[16,128]{1,0:T(8,128)S(1)} %copy-done.2, bf16[592,128]{1,0:T(8,128)(2,1)S(1)} %collective-permute-done.1.first_ref), custom_call_target="tpu_custom_call" | custom-call | flops 1000000000 | bytes 1048576 | tf_op jit(solution)/shard_map/pallas_call | solution.py:699
  11.9 0.7 %collective-permute-start.4 = (bf16[224,128]{1,0:T(8,128)(2,1)S(1)}, bf16[224,128]{1,0:T(8,128)(2,1)S(1)}, u32[]{:S(2)}, u32[]{:S(2)}) collective-permute-start(bf16[224,128]{1,0:T(8,128)(2,1)S(1)} %get-tuple-element.28), channel_id=1, source_target_pairs={{0,30},{30,0},{1,31},{31,1}} | collective-permute-start | bytes 172040 | tf_op jit(solution)/shard_map/ppermute | solution.py:720
  12.6 0.1 collective-permute-done.second_ref
  12.7 0.7 %shard_map.106 = (bf16[96,16,128]{2,1,0:T(8,128)(2,1)S(1)}, f32[16,128]{1,0:T(8,128)S(1)}, bf16[416,128]{1,0:T(8,128)(2,1)S(1)}, bf16[224,128]{1,0:T(8,128)(2,1)S(1)}, bf16[224,128]{1,0:T(8,128)(2,1)S(1)}) custom-call(bf16[592,128]{1,0:T(8,128)(2,1)S(1)} %collective-permute-done.second_ref, bf16[592,128]{1,0:T(8,128)(2,1)S(1)} %shard_map.102.sent_ref, ...), custom_call_target="tpu_custom_call" | custom-call | tf_op jit(solution)/shard_map/pallas_call | solution.py:723
  13.4 5.3 %collective-permute-start.3 = (bf16[224,128]{1,0:T(8,128)(2,1)S(1)}, bf16[224,128]{1,0:T(8,128)(2,1)S(1)}, u32[]{:S(2)}, u32[]{:S(2)}) collective-permute-start(bf16[224,128]{1,0:T(8,128)(2,1)S(1)} %get-tuple-element.27.after_ref), channel_id=1, source_target_pairs={{2,4},{4,2},{6,8},{8,6},{10,12},{12,10},{14,16},{16,14},{18,20},{2... | collective-permute-start | bytes 172040 | tf_op jit(solution)/shard_map/ppermute | solution.py:757
  18.8 0.1 shard_map.107
  18.9 0.1 collective-permute-start.2
  19.0 2.6 %shard_map.109.update_ref = f32[2304,128]{1,0:T(8,128)S(1)} custom-call(bf16[96,16,128]{2,1,0:T(8,128)(2,1)S(1)} %copy-done.1, bf16[96,16,128]{2,1,0:T(8,128)(2,1)S(1)} %get-tuple-element.24.halo_ref, bf16[2304,256]{1,0:T(8,128)(2,1)S(1)} %get-tuple-element.21.matrix_ref, ...), custom_call_target="tpu_custom_call", output_to_operand_aliasing={{}: (6, {})} | custom-call | flops 4000000000 | bytes 1048576 | tf_op jit(solution)/shard_map/pallas_call | solution.py:759
  21.6 0.0 collective-permute-done.4.wrap_ref
  21.6 0.0 collective-permute-done.2.core_ref
  21.6 0.0 collective-permute-done.3.cross_ref
  21.6 2.3 %shard_map.108.strips = f32[2304,128]{1,0:T(8,128)S(1)} custom-call(bf16[224,128]{1,0:T(8,128)(2,1)S(1)} %collective-permute-done.2.core_ref, bf16[224,128]{1,0:T(8,128)(2,1)S(1)} %collective-permute-done.3.cross_ref, bf16[224,128]{1,0:T(8,128)(2,1)S(1)} %collective-permute-done.4.wrap_ref, bf16[224,128]{1,0:T(8,128)(2,1)S(1)} %get-tuple-element.29.own_ref, ...), custom_call_target="tpu_custom_call" | custom-call | tf_op jit(solution)/shard_map/pallas_call | solution.py:770
  23.9 4.6 %shard_map.110 = bf16[96,16,128]{2,1,0:T(8,128)(2,1)} custom-call(bf16[96,16,128]{2,1,0:T(8,128)(2,1)S(1)} %copy-done.1, s32[16,128]{1,0:T(8,128)S(1)} %copy-done.2, bf16[96,16,128]{2,1,0:T(8,128)(2,1)S(1)} %get-tuple-element.24.halo_ref, f32[16,128]{1,0:T(8,128)S(1)} %get-tuple-element.25.halo_mask_ref, ...), custom_call_target="tpu_custom_call" | custom-call | tf_op jit(solution)/shard_map/pallas_call | solution.py:779
  (1 shorter events, 0.0 us)
Async XLA Ops:
  0.0 1.0 %copy-start.1 = (bf16[96,16,128]{2,1,0:T(8,128)(2,1)S(1)}, bf16[96,16,128]{2,1,0:T(8,128)(2,1)}, u32[]{:S(2)}) copy-start(bf16[96,16,128]{2,1,0:T(8,128)(2,1)} %field_ref.11) | copy-start | bytes 1179652
  0.0 1.0 %copy-start.2 = (s32[16,128]{1,0:T(8,128)S(1)}, s32[16,128]{1,0:T(8,128)}, u32[]{:S(2)}) copy-start(s32[16,128]{1,0:T(8,128)} %mask_ref.7) | copy-start | bytes 24580
  1.2 6.6 %copy-start.3 = (bf16[2,384,96]{1,2,0:T(8,128)(2,1)S(1)}, bf16[2,384,96]{1,2,0:T(8,128)(2,1)}, u32[]{:S(2)}) copy-start(bf16[2,384,96]{1,2,0:T(8,128)(2,1)} %param.16) | copy-start | bytes 442372
  1.2 6.6 %copy-start.4 = (f32[2,96,7,7]{1,0,3,2:T(2,128)S(1)}, f32[2,96,7,7]{1,0,3,2:T(2,128)}, u32[]{:S(2)}) copy-start(f32[2,96,7,7]{1,0,3,2:T(2,128)} %param.12) | copy-start | bytes 112900
  1.2 6.6 %copy-start.5 = (f32[2,384]{1,0:T(2,128)S(1)}, f32[2,384]{1,0:T(2,128)}, u32[]{:S(2)}) copy-start(f32[2,384]{1,0:T(2,128)} %expand_bias_ref.1) | copy-start | bytes 9220
  1.3 6.6 %copy-start.6 = (f32[2,96]{1,0:T(2,128)S(1)}, f32[2,96]{1,0:T(2,128)}, u32[]{:S(2)}) copy-start(f32[2,96]{1,0:T(2,128)} %bias_ref.1) | copy-start | bytes 2308
  1.3 6.6 %copy-start.7 = (f32[2,96]{1,0:T(2,128)S(1)}, f32[2,96]{1,0:T(2,128)}, u32[]{:S(2)}) copy-start(f32[2,96]{1,0:T(2,128)} %gain_ref.1) | copy-start | bytes 2308
  1.3 6.6 %copy-start.8 = (f32[2,96]{1,0:T(2,128)S(1)}, f32[2,96]{1,0:T(2,128)}, u32[]{:S(2)}) copy-start(f32[2,96]{1,0:T(2,128)} %norm_bias_ref.1) | copy-start | bytes 2308
  1.3 6.6 %copy-start.9 = (f32[2,96]{1,0:T(2,128)S(1)}, f32[2,96]{1,0:T(2,128)}, u32[]{:S(2)}) copy-start(f32[2,96]{1,0:T(2,128)} %reduce_bias_ref.1) | copy-start | bytes 2308
  1.3 10.3 %collective-permute-start.1 = (bf16[592,128]{1,0:T(8,128)(2,1)S(1)}, bf16[592,128]{1,0:T(8,128)(2,1)S(1)}, u32[]{:S(2)}, u32[]{:S(2)}) collective-permute-start(bf16[592,128]{1,0:T(8,128)(2,1)S(1)} %shard_map.101.after_ref), channel_id=1, source_target_pairs={{0,1},{1,0},{2,3},{3,2},{4,5},{5,4},{6,7},{7,6},{8,9},{9,8},{10,11... | collective-permute-start | bytes 454664 | tf_op jit(solution)/shard_map/ppermute | solution.py:657
  1.8 10.9 %collective-permute-start = (bf16[592,128]{1,0:T(8,128)(2,1)S(1)}, bf16[592,128]{1,0:T(8,128)(2,1)S(1)}, u32[]{:S(2)}, u32[]{:S(2)}) collective-permute-start(bf16[592,128]{1,0:T(8,128)(2,1)S(1)} %shard_map.102.sent_ref), channel_id=1, source_target_pairs={{1,31},{3,29},{5,27},{7,25},{9,23},{11,21},{13,19},{15,17},{17,15}... | collective-permute-start | bytes 454664 | tf_op jit(solution)/shard_map/ppermute | solution.py:653
  7.9 1.7 %copy-start = (bf16[2,96,384]{2,1,0:T(8,128)(2,1)S(1)}, bf16[2,96,384]{2,1,0:T(8,128)(2,1)}, u32[]{:S(2)}) copy-start(bf16[2,96,384]{2,1,0:T(8,128)(2,1)} %reduce_ref.7) | copy-start | bytes 442372
  11.9 9.6 %collective-permute-start.4 = (bf16[224,128]{1,0:T(8,128)(2,1)S(1)}, bf16[224,128]{1,0:T(8,128)(2,1)S(1)}, u32[]{:S(2)}, u32[]{:S(2)}) collective-permute-start(bf16[224,128]{1,0:T(8,128)(2,1)S(1)} %get-tuple-element.28), channel_id=1, source_target_pairs={{0,30},{30,0},{1,31},{31,1}} | collective-permute-start | bytes 172040 | tf_op jit(solution)/shard_map/ppermute | solution.py:720
  13.4 8.2 %collective-permute-start.3 = (bf16[224,128]{1,0:T(8,128)(2,1)S(1)}, bf16[224,128]{1,0:T(8,128)(2,1)S(1)}, u32[]{:S(2)}, u32[]{:S(2)}) collective-permute-start(bf16[224,128]{1,0:T(8,128)(2,1)S(1)} %get-tuple-element.27.after_ref), channel_id=1, source_target_pairs={{2,4},{4,2},{6,8},{8,6},{10,12},{12,10},{14,16},{16,14},{18,20},{2... | collective-permute-start | bytes 172040 | tf_op jit(solution)/shard_map/ppermute | solution.py:757
  18.9 2.7 %collective-permute-start.2 = (bf16[224,128]{1,0:T(8,128)(2,1)S(1)}, bf16[224,128]{1,0:T(8,128)(2,1)S(1)}, u32[]{:S(2)}, u32[]{:S(2)}) collective-permute-start(bf16[224,128]{1,0:T(8,128)(2,1)S(1)} %shard_map.107), channel_id=1, source_target_pairs={{0,2},{2,0},{4,6},{6,4},{8,10},{10,8},{12,14},{14,12},{16,18},{18,... | collective-permute-start | bytes 172040 | tf_op jit(solution)/shard_map/ppermute | solution.py:751

commit v5 on v4

--- a/solution.py
+++ b/solution.py
@@ -34,6 +34,7 @@
 
 def pack_rows(upper_if_even, field_ref, mask_ref, after_ref, out_ref, wide, wide_mask):
     del after_ref
+    kept = 1.0 if upper_if_even else (lax.axis_index("lat") > 0).astype(jnp.float32)
     channels, rows, width = field_ref.shape
     even = lax.rem(lax.axis_index("lat"), 2) == 0
     take_upper = even if upper_if_even else jnp.logical_not(even)
@@ -43,12 +44,12 @@
         lower = wide[pl.ds(k, channels, stride=rows), :]
         upper = wide[pl.ds(rows - HALO + k, channels, stride=rows), :]
         at = pl.ds(k * channels, channels)
-        out_ref[at, :] = jnp.where(take_upper, upper, lower).astype(jnp.bfloat16)
+        out_ref[at, :] = (kept * jnp.where(take_upper, upper, lower)).astype(jnp.bfloat16)
     pad = jnp.zeros((16 - HALO, width), jnp.float32)
     lower = jnp.concatenate([wide_mask[0:HALO, :], pad], axis=0)
     upper = jnp.concatenate([wide_mask[rows - HALO : rows, :], pad], axis=0)
     at = pl.ds(HALO * channels, 16)
-    out_ref[at, :] = jnp.where(take_upper, upper, lower).astype(jnp.bfloat16)
+    out_ref[at, :] = (kept * jnp.where(take_upper, upper, lower)).astype(jnp.bfloat16)
 
 
 def north_place(row):
@@ -191,6 +192,11 @@
     halo_mask_ref[...] = near_mask_ref[...] + mask_rows[...]
     join_ends(own_ends_ref, halo_ref, halo_mask_ref, ends_ref)
     pack_side(ends_ref, cross_ref, lon_odd)
+    if mirrored:
+
+        @pl.when(over_wrap())
+        def _():
+            cross_ref[...] = jnp.zeros_like(cross_ref)
 
 
 def core_columns(ends_ref, after_ref, core_ref):
@@ -544,7 +550,13 @@
     high = lane24 >= width - 3
     blank = jnp.zeros((8, width), jnp.float32)
     ones = jnp.ones((32, width), jnp.bfloat16)
-    away = {s: lane32 < s if s > 0 else lane32 >= width + s for s in range(-3, 4) if s}
+    lane16 = lanes((16, width))
+    away = {s: lane16 < s if s > 0 else lane16 >= width + s for s in range(-3, 4) if s}
+
+    def halves(block):
+        low_rows = block[:16, :].astype(jnp.bfloat16)
+        return low_rows, jnp.concatenate([block[16:, :], blank], axis=0).astype(jnp.bfloat16)
+
     for g in range(groups):
         both = received(g)
         for j in range(8):
@@ -553,19 +565,18 @@
             far = pltpu.roll(near, width - 2 * HALO, 1)
             change = update_ref[c * 24 : c * 24 + 24, :]
             change = jnp.where(low, near, jnp.where(high, far, change))
-            old = jnp.concatenate([field_ref[c], halo_ref[c]], axis=0).astype(jnp.float32)
-            main = main_mask * (old[:24, :] + change)
-            main = jnp.concatenate([main, blank], axis=0).astype(jnp.bfloat16)
-            main_ref[c] = main[:rows, :]
+            own = field_ref[c].astype(jnp.float32)
+            halo = halo_ref[c].astype(jnp.float32)[:8, :]
+            main = halves(main_mask * (jnp.concatenate([own, halo], axis=0) + change))
+            main_ref[c] = main[0]
             change = jnp.where(high, near, far)
-            beside = side_mask * (beside_of(both, j) + change)
-            beside = jnp.concatenate([beside, blank], axis=0).astype(jnp.bfloat16)
+            beside = halves(side_mask * (beside_of(both, j) + change))
             stack = []
             for s in range(-3, 4):
-                moved = main
-                if s:
-                    moved = pltpu.roll(jnp.where(away[s], beside, main), (-s) % width, 1)
-                stack.append(moved)
+                for part, other in zip(main, beside):
+                    if s:
+                        part = pltpu.roll(jnp.where(away[s], other, part), (-s) % width, 1)
+                    stack.append(part)
             stack = jnp.concatenate(stack + [ones], axis=0)
             matrix = matrix_ref[c * 16 : c * 16 + 16, :]
             result = jnp.dot(matrix, stack, preferred_element_type=jnp.float32)
@@ -650,6 +661,7 @@
         for low in range(1, nlat - 1, 2):
             pairs += [(at(d, low), at(d, low + 1)), (at(d, low + 1), at(d, low))]
         pairs.append((at(d, nlat - 1), at(nlon - 1 - d, nlat - 1)))
+        pairs.append((at(d, 0), at(d ^ 1, 0)))
     second = lax.ppermute(second_sent, ("lon", "lat"), pairs)
     pairs = []
     for low in range(0, nlat - 1, 2):
@@ -717,6 +729,7 @@
         pairs = []
         for lat in range(nlat):
             pairs += [(lat, at(nlon - 1, lat)), (at(nlon - 1, lat), lat)]
+            pairs += [(at(d, lat), at(d, 1 - lat)) for d in range(1, nlon - 1)]
         wrap = lax.ppermute(wrap, ("lon", "lat"), pairs)
     else:
         wrap = jnp.zeros_like(wrap)
@@ -750,11 +763,14 @@
         pairs += [(low, low + 1), (low + 1, low)]
     core = lax.ppermute(core, "lon", pairs)
     pairs = []
-    for low in range(1, nlon, 2):
-        after = (low + 1) % nlon
-        if after or not alone:
-            pairs += [(low, after), (after, low)]
-    cross = lax.ppermute(cross, "lon", pairs)
+    for lat in range(nlat):
+        for low in range(1, nlon, 2):
+            after = (low + 1) % nlon
+            if after or not alone:
+                pairs += [(at(low, lat), at(after, lat)), (at(after, lat), at(low, lat))]
+            else:
+                pairs += [(at(low, lat), at(low, 1 - lat)), (at(after, lat), at(after, 1 - lat))]
+    cross = lax.ppermute(cross, ("lon", "lat"), pairs)
 
     update = pl.pallas_call(
         edge_rows,

time: 28.7 us -> 25.8 us (0.90)
  the two profiles are of different devices: /device:TPU:7 before, /device:TPU:0 now
where the time goes in v5:
time: 25.8 us; the launch traced here: 25.7 us
  Pallas kernels  15.1 us (59%)
  starting transfers between devices  8.64 us (33%)
  local copies, waits for them, and re-layouts  1.05 us (4%)
  waiting for transfers between devices  0.64 us (2%)
    ppermute x1, starting transfers between devices, per_device(): wrap = lax.ppermute(wrap, ('lon', 'lat'), pairs)  4.7 us
    pallas_call x1, Pallas kernels, per_device(): pl.pallas_call(second_layer, out_shape=jax.ShapeDtypeStruct((channels, ro...  4.6 us
    ppermute x1, starting transfers between devices, per_device(): first = lax.ppermute(first, 'lat', pairs)  3 us
    pallas_call x1, Pallas kernels, per_device(): pl.pallas_call(edge_rows, out_shape=jax.ShapeDtypeStruct((channels * 24,...  2.59 us
    pallas_call x1, Pallas kernels, per_device(): pl.pallas_call(edge_columns, out_shape=jax.ShapeDtypeStruct((channels * 2...  2.3 us
    pallas_call x1, Pallas kernels, per_device(): pl.pallas_call(inner_rows, out_shape=jax.ShapeDtypeStruct((channels * 24,...  1.96 us
    pallas_call x1, Pallas kernels, per_device(): pl.pallas_call(weights, out_shape=[jax.ShapeDtypeStruct((channels * 24, 2...  1.65 us
    unnamed x20, local copies, waits for them, and re-layouts  1.05 us
  transfers between devices with their start and end apart: 5, of which 1 were waited for; matrix products, arithmetic and copies ran while one was open for 0% of the time, Pallas kernels for 31%

profile of v5, /device:TPU:0, one launch (start us, length us, event | category | flops | bytes accessed | tf_op | source)
XLA Modules:
  0.0 25.7 jit_solution(2230539079693473040)
XLA Ops:
  0.0 0.0 copy-start.1
  0.0 0.0 copy-start.2
  0.0 1.0 %copy-done.1 = bf16[96,16,128]{2,1,0:T(8,128)(2,1)S(1)} copy-done((bf16[96,16,128]{2,1,0:T(8,128)(2,1)S(1)}, bf16[96,16,128]{2,1,0:T(8,128)(2,1)}, u32[]{:S(2)}) %copy-start.1) | copy-done | bytes 393240
  1.0 0.0 copy-done.2
  1.0 0.2 shard_map.101.after_ref
  1.2 0.0 copy-start.3
  1.2 0.0 copy-start.4
  1.2 0.0 copy-start.5
  1.3 0.0 copy-start.6
  1.3 0.0 copy-start.7
  1.3 0.0 copy-start.8
  1.3 0.0 copy-start.9
  1.3 3.0 %collective-permute-start.1 = (bf16[592,128]{1,0:T(8,128)(2,1)S(1)}, bf16[592,128]{1,0:T(8,128)(2,1)S(1)}, u32[]{:S(2)}, u32[]{:S(2)}) collective-permute-start(bf16[592,128]{1,0:T(8,128)(2,1)S(1)} %shard_map.101.after_ref), channel_id=1, source_target_pairs={{0,1},{1,0},{2,3},{3,2},{4,5},{5,4},{6,7},{7,6},{8,9},{9,8},{10,11... | collective-permute-start | bytes 454664 | tf_op jit(solution)/shard_map/ppermute | solution.py:669
  4.3 0.2 shard_map.102.sent_ref
  4.5 0.1 collective-permute-start
  4.6 0.0 copy-done.3
  4.6 0.0 copy-done.4
  4.6 0.0 copy-done.5
  4.6 0.0 copy-done.6
  4.6 0.0 copy-done.7
  4.7 0.0 copy-done.8
  4.7 0.0 copy-done.9
  4.7 0.0 copy-start
  4.7 1.6 %shard_map.104 = (bf16[2304,256]{1,0:T(8,128)(2,1)S(1)}, bf16[1536,256]{1,0:T(8,128)(2,1)S(1)}, f32[2,3,96,128]{3,2,1,0:T(8,128)S(1)}, bf16[2,384,112]{2,1,0:T(8,128)(2,1)S(1)}) custom-call(f32[49,2,96]{2,1,0:T(2,128)S(1)} %bitcast.5, f32[2,96]{1,0:T(2,128)S(1)} %copy-done.6, f32[2,96]{1,0:T(2,128)S(1)} %copy-done.7, f32[2,96]{1,0:T(2,128)S(1)} %copy-done.8, ...), custom_call_target="tpu_custom_call" | custom-call | flops 2000000000 | bytes 1048576 | tf_op jit(solution)/shard_map/pallas_call | solution.py:672
  6.3 0.0 copy-done
  6.4 2.0 %shard_map.105.after_ref.old_ref = f32[2304,128]{1,0:T(8,128)S(1)} custom-call(bf16[96,16,128]{2,1,0:T(8,128)(2,1)S(1)} %copy-done.1, bf16[2304,256]{1,0:T(8,128)(2,1)S(1)} %get-tuple-element.21.matrix_ref, f32[2,3,96,128]{3,2,1,0:T(8,128)S(1)} %get-tuple-element.22.rows_ref, bf16[2,384,112]{2,1,0:T(8,128)(2,1)S(1)} %get-tuple-element.23.expand_ref, ...), custom_call_target="tpu_custom_call" | custom-call | flops 4000000000 | bytes 1048576 | tf_op jit(solution)/shard_map/pallas_call | solution.py:699
  8.3 0.0 collective-permute-done.1.first_ref
  8.3 0.6 %shard_map.103 = (bf16[96,16,128]{2,1,0:T(8,128)(2,1)S(1)}, f32[16,128]{1,0:T(8,128)S(1)}, bf16[208,128]{1,0:T(8,128)(2,1)S(1)}, bf16[224,128]{1,0:T(8,128)(2,1)S(1)}) custom-call(bf16[96,16,128]{2,1,0:T(8,128)(2,1)S(1)} %copy-done.1, s32[16,128]{1,0:T(8,128)S(1)} %copy-done.2, bf16[592,128]{1,0:T(8,128)(2,1)S(1)} %collective-permute-done.1.first_ref), custom_call_target="tpu_custom_call" | custom-call | flops 1000000000 | bytes 1048576 | tf_op jit(solution)/shard_map/pallas_call | solution.py:711
  9.0 4.7 %collective-permute-start.4 = (bf16[224,128]{1,0:T(8,128)(2,1)S(1)}, bf16[224,128]{1,0:T(8,128)(2,1)S(1)}, u32[]{:S(2)}, u32[]{:S(2)}) collective-permute-start(bf16[224,128]{1,0:T(8,128)(2,1)S(1)} %get-tuple-element.28), channel_id=1, source_target_pairs={{0,30},{30,0},{2,3},{4,5},{6,7},{8,9},{10,11},{12,13},{14,15},{16,... | collective-permute-start | bytes 172040 | tf_op jit(solution)/shard_map/ppermute | solution.py:733
  13.7 0.0 collective-permute-done.second_ref
  13.7 0.8 %shard_map.106 = (bf16[96,16,128]{2,1,0:T(8,128)(2,1)S(1)}, f32[16,128]{1,0:T(8,128)S(1)}, bf16[416,128]{1,0:T(8,128)(2,1)S(1)}, bf16[224,128]{1,0:T(8,128)(2,1)S(1)}, bf16[224,128]{1,0:T(8,128)(2,1)S(1)}) custom-call(bf16[592,128]{1,0:T(8,128)(2,1)S(1)} %collective-permute-done.second_ref, bf16[592,128]{1,0:T(8,128)(2,1)S(1)} %shard_map.102.sent_ref, ...), custom_call_target="tpu_custom_call" | custom-call | tf_op jit(solution)/shard_map/pallas_call | solution.py:736
  14.5 0.8 %collective-permute-start.3 = (bf16[224,128]{1,0:T(8,128)(2,1)S(1)}, bf16[224,128]{1,0:T(8,128)(2,1)S(1)}, u32[]{:S(2)}, u32[]{:S(2)}) collective-permute-start(bf16[224,128]{1,0:T(8,128)(2,1)S(1)} %get-tuple-element.27.after_ref), channel_id=1, source_target_pairs={{2,4},{4,2},{6,8},{8,6},{10,12},{12,10},{14,16},{16,14},{18,20},{2... | collective-permute-start | bytes 172040 | tf_op jit(solution)/shard_map/ppermute | solution.py:773
  15.3 0.1 shard_map.107
  15.4 0.1 collective-permute-start.2
  15.5 2.6 %shard_map.109.update_ref = f32[2304,128]{1,0:T(8,128)S(1)} custom-call(bf16[96,16,128]{2,1,0:T(8,128)(2,1)S(1)} %copy-done.1, bf16[96,16,128]{2,1,0:T(8,128)(2,1)S(1)} %get-tuple-element.24.halo_ref, bf16[2304,256]{1,0:T(8,128)(2,1)S(1)} %get-tuple-element.21.matrix_ref, ...), custom_call_target="tpu_custom_call", output_to_operand_aliasing={{}: (6, {})} | custom-call | flops 4000000000 | bytes 1048576 | tf_op jit(solution)/shard_map/pallas_call | solution.py:775
  18.1 0.0 collective-permute-done.4.wrap_ref
  18.1 0.0 collective-permute-done.2.core_ref
  18.1 0.6 %collective-permute-done.3.cross_ref = bf16[224,128]{1,0:T(8,128)(2,1)S(1)} collective-permute-done((bf16[224,128]{1,0:T(8,128)(2,1)S(1)}, bf16[224,128]{1,0:T(8,128)(2,1)S(1)}, u32[]{:S(2)}, u32[]{:S(2)}) %collective-permute-start.3) | collective-permute-done | bytes 57376 | tf_op jit(solution)/shard_map/ppermute | solution.py:773
  18.8 2.3 %shard_map.108.strips = f32[2304,128]{1,0:T(8,128)S(1)} custom-call(bf16[224,128]{1,0:T(8,128)(2,1)S(1)} %collective-permute-done.2.core_ref, bf16[224,128]{1,0:T(8,128)(2,1)S(1)} %collective-permute-done.3.cross_ref, bf16[224,128]{1,0:T(8,128)(2,1)S(1)} %collective-permute-done.4.wrap_ref, bf16[224,128]{1,0:T(8,128)(2,1)S(1)} %get-tuple-element.29.own_ref, ...), custom_call_target="tpu_custom_call" | custom-call | tf_op jit(solution)/shard_map/pallas_call | solution.py:786
  21.1 4.6 %shard_map.110 = bf16[96,16,128]{2,1,0:T(8,128)(2,1)} custom-call(bf16[96,16,128]{2,1,0:T(8,128)(2,1)S(1)} %copy-done.1, s32[16,128]{1,0:T(8,128)S(1)} %copy-done.2, bf16[96,16,128]{2,1,0:T(8,128)(2,1)S(1)} %get-tuple-element.24.halo_ref, f32[16,128]{1,0:T(8,128)S(1)} %get-tuple-element.25.halo_mask_ref, ...), custom_call_target="tpu_custom_call" | custom-call | tf_op jit(solution)/shard_map/pallas_call | solution.py:795
  (1 shorter events, 0.0 us)
Async XLA Ops:
  0.0 1.0 %copy-start.1 = (bf16[96,16,128]{2,1,0:T(8,128)(2,1)S(1)}, bf16[96,16,128]{2,1,0:T(8,128)(2,1)}, u32[]{:S(2)}) copy-start(bf16[96,16,128]{2,1,0:T(8,128)(2,1)} %field_ref.11) | copy-start | bytes 1179652
  0.0 1.0 %copy-start.2 = (s32[16,128]{1,0:T(8,128)S(1)}, s32[16,128]{1,0:T(8,128)}, u32[]{:S(2)}) copy-start(s32[16,128]{1,0:T(8,128)} %mask_ref.7) | copy-start | bytes 24580
  1.2 3.4 %copy-start.3 = (bf16[2,384,96]{1,2,0:T(8,128)(2,1)S(1)}, bf16[2,384,96]{1,2,0:T(8,128)(2,1)}, u32[]{:S(2)}) copy-start(bf16[2,384,96]{1,2,0:T(8,128)(2,1)} %param.16) | copy-start | bytes 442372
  1.2 3.4 %copy-start.4 = (f32[2,96,7,7]{1,0,3,2:T(2,128)S(1)}, f32[2,96,7,7]{1,0,3,2:T(2,128)}, u32[]{:S(2)}) copy-start(f32[2,96,7,7]{1,0,3,2:T(2,128)} %param.12) | copy-start | bytes 112900
  1.2 3.4 %copy-start.5 = (f32[2,384]{1,0:T(2,128)S(1)}, f32[2,384]{1,0:T(2,128)}, u32[]{:S(2)}) copy-start(f32[2,384]{1,0:T(2,128)} %expand_bias_ref.1) | copy-start | bytes 9220
  1.3 3.4 %copy-start.6 = (f32[2,96]{1,0:T(2,128)S(1)}, f32[2,96]{1,0:T(2,128)}, u32[]{:S(2)}) copy-start(f32[2,96]{1,0:T(2,128)} %bias_ref.1) | copy-start | bytes 2308
  1.3 3.4 %copy-start.7 = (f32[2,96]{1,0:T(2,128)S(1)}, f32[2,96]{1,0:T(2,128)}, u32[]{:S(2)}) copy-start(f32[2,96]{1,0:T(2,128)} %gain_ref.1) | copy-start | bytes 2308
  1.3 3.4 %copy-start.8 = (f32[2,96]{1,0:T(2,128)S(1)}, f32[2,96]{1,0:T(2,128)}, u32[]{:S(2)}) copy-start(f32[2,96]{1,0:T(2,128)} %norm_bias_ref.1) | copy-start | bytes 2308
  1.3 3.4 %copy-start.9 = (f32[2,96]{1,0:T(2,128)S(1)}, f32[2,96]{1,0:T(2,128)}, u32[]{:S(2)}) copy-start(f32[2,96]{1,0:T(2,128)} %reduce_bias_ref.1) | copy-start | bytes 2308
  1.3 7.0 %collective-permute-start.1 = (bf16[592,128]{1,0:T(8,128)(2,1)S(1)}, bf16[592,128]{1,0:T(8,128)(2,1)S(1)}, u32[]{:S(2)}, u32[]{:S(2)}) collective-permute-start(bf16[592,128]{1,0:T(8,128)(2,1)S(1)} %shard_map.101.after_ref), channel_id=1, source_target_pairs={{0,1},{1,0},{2,3},{3,2},{4,5},{5,4},{6,7},{7,6},{8,9},{9,8},{10,11... | collective-permute-start | bytes 454664 | tf_op jit(solution)/shard_map/ppermute | solution.py:669
  4.5 9.1 %collective-permute-start = (bf16[592,128]{1,0:T(8,128)(2,1)S(1)}, bf16[592,128]{1,0:T(8,128)(2,1)S(1)}, u32[]{:S(2)}, u32[]{:S(2)}) collective-permute-start(bf16[592,128]{1,0:T(8,128)(2,1)S(1)} %shard_map.102.sent_ref), channel_id=1, source_target_pairs={{1,31},{0,2},{3,29},{2,0},{5,27},{4,6},{7,25},{6,4},{9,23},{8,10},... | collective-permute-start | bytes 454664 | tf_op jit(solution)/shard_map/ppermute | solution.py:665
  4.7 1.7 %copy-start = (bf16[2,96,384]{2,1,0:T(8,128)(2,1)S(1)}, bf16[2,96,384]{2,1,0:T(8,128)(2,1)}, u32[]{:S(2)}) copy-start(bf16[2,96,384]{2,1,0:T(8,128)(2,1)} %reduce_ref.7) | copy-start | bytes 442372
  9.0 9.2 %collective-permute-start.4 = (bf16[224,128]{1,0:T(8,128)(2,1)S(1)}, bf16[224,128]{1,0:T(8,128)(2,1)S(1)}, u32[]{:S(2)}, u32[]{:S(2)}) collective-permute-start(bf16[224,128]{1,0:T(8,128)(2,1)S(1)} %get-tuple-element.28), channel_id=1, source_target_pairs={{0,30},{30,0},{2,3},{4,5},{6,7},{8,9},{10,11},{12,13},{14,15},{16,... | collective-permute-start | bytes 172040 | tf_op jit(solution)/shard_map/ppermute | solution.py:733
  14.5 4.2 %collective-permute-start.3 = (bf16[224,128]{1,0:T(8,128)(2,1)S(1)}, bf16[224,128]{1,0:T(8,128)(2,1)S(1)}, u32[]{:S(2)}, u32[]{:S(2)}) collective-permute-start(bf16[224,128]{1,0:T(8,128)(2,1)S(1)} %get-tuple-element.27.after_ref), channel_id=1, source_target_pairs={{2,4},{4,2},{6,8},{8,6},{10,12},{12,10},{14,16},{16,14},{18,20},{2... | collective-permute-start | bytes 172040 | tf_op jit(solution)/shard_map/ppermute | solution.py:773
  15.4 2.7 %collective-permute-start.2 = (bf16[224,128]{1,0:T(8,128)(2,1)S(1)}, bf16[224,128]{1,0:T(8,128)(2,1)S(1)}, u32[]{:S(2)}, u32[]{:S(2)}) collective-permute-start(bf16[224,128]{1,0:T(8,128)(2,1)S(1)} %shard_map.107), channel_id=1, source_target_pairs={{0,2},{2,0},{4,6},{6,4},{8,10},{10,8},{12,14},{14,12},{16,18},{18,... | collective-permute-start | bytes 172040 | tf_op jit(solution)/shard_map/ppermute | solution.py:764

commit v6 on v5

--- a/solution.py
+++ b/solution.py
@@ -10,6 +10,10 @@
 
 HALO = 6
 VMEM_LIMIT = 20 * 1024 * 1024
+
+
+def pitch(channels):
+    return channels + 8
 
 
 def params():
@@ -366,14 +370,15 @@
     def step(c, carry):
         matrix = matrix_ref[pl.ds(pl.multiple_of(c * stride + first, 8), count), :]
         result = jnp.dot(matrix, stack_of(c, ones), preferred_element_type=jnp.float32)
-        conv[pl.ds(c, count, stride=channels), :] = result
+        conv[pl.ds(c, count, stride=pitch(channels)), :] = result
         return carry
 
     lax.fori_loop(0, channels, step, 0, unroll=channels)
 
 
 def conv_row(conv, channels, i):
-    return lambda: conv[i * channels : (i + 1) * channels, :]
+    start = i * pitch(channels)
+    return lambda: conv[start : start + channels, :]
 
 
 def inner_rows(
@@ -476,7 +481,7 @@
             stack = columns_stack(block, ones)
             result = jnp.dot(matrix, stack, preferred_element_type=jnp.float32)
             for n, c in enumerate(some):
-                conv[pl.ds(c, 24, stride=channels), :] = result[n * 24 : n * 24 + 24, :]
+                conv[pl.ds(c, 24, stride=pitch(channels)), :] = result[n * 24 : n * 24 + 24, :]
 
     order = {place_of(row): i for i, row in enumerate(EDGE + INNER)}
     lane = lanes((quarter, width))
@@ -491,7 +496,7 @@
             packed = jnp.zeros((quarter, width), jnp.float32)
             for q, start in enumerate(starts):
                 if p * 8 + q in order:
-                    row = order[p * 8 + q] * channels + n * quarter
+                    row = order[p * 8 + q] * pitch(channels) + n * quarter
                     block = conv[row : row + quarter, :]
                     block = pltpu.roll(block, (start - 32 * n) % width, 1)
                     packed = jnp.where(inside[q], block, packed)
@@ -580,7 +585,7 @@
             stack = jnp.concatenate(stack + [ones], axis=0)
             matrix = matrix_ref[c * 16 : c * 16 + 16, :]
             result = jnp.dot(matrix, stack, preferred_element_type=jnp.float32)
-            conv[pl.ds(c, 16, stride=channels), :] = result
+            conv[pl.ds(c, 16, stride=pitch(channels)), :] = result
 
     mask = mask_ref[...].astype(jnp.float32)
     changes = []
@@ -701,7 +706,7 @@
         out_shape=jax.ShapeDtypeStruct((channels * 24, width), f32),
         in_specs=vmem(5),
         out_specs=pl.BlockSpec(memory_space=pltpu.VMEM),
-        scratch_shapes=[pltpu.VMEM((channels * 16, width), f32)] + buffers(len(INNER)),
+        scratch_shapes=[pltpu.VMEM((pitch(channels) * 16, width), f32)] + buffers(len(INNER)),
         compiler_params=params(),
         cost_estimate=cost(4e9),
     )(field, matrix_one, by_channel, expand, w_reduce)
@@ -777,7 +782,7 @@
         out_shape=jax.ShapeDtypeStruct((channels * 24, width), f32),
         in_specs=vmem(7),
         out_specs=pl.BlockSpec(memory_space=pltpu.VMEM),
-        scratch_shapes=[pltpu.VMEM((channels * 16, width), f32)] + buffers(len(EDGE)),
+        scratch_shapes=[pltpu.VMEM((pitch(channels) * 16, width), f32)] + buffers(len(EDGE)),
         input_output_aliases={6: 0},
         compiler_params=params(),
         cost_estimate=cost(4e9),
@@ -788,7 +793,7 @@
         out_shape=jax.ShapeDtypeStruct((channels * 24, width), f32),
         in_specs=vmem(9),
         out_specs=pl.BlockSpec(memory_space=pltpu.VMEM),
-        scratch_shapes=[pltpu.VMEM((channels * 24, width), f32)] + buffers(3),
+        scratch_shapes=[pltpu.VMEM((pitch(channels) * 24, width), f32)] + buffers(3),
         compiler_params=params(),
     )(core, cross, wrap, own, ends, matrix_one, by_channel, expand, w_reduce)
 
@@ -799,7 +804,7 @@
         out_specs=pl.BlockSpec(memory_space=pltpu.VMEM),
         scratch_shapes=[
             pltpu.VMEM((channels, rows, width), bf16),
-            pltpu.VMEM((channels * 16, width), f32),
+            pltpu.VMEM((pitch(channels) * 16, width), f32),
         ]
         + buffers(rows),
         compiler_params=params(),

time: 25.8 us -> 25.1 us (0.973)
  Pallas kernels: 15.1 us -> 14.3 us
    pallas_call x1, Pallas kernels: 2.3 us -> 1.88 us  [per_device(): pl.pallas_call(edge_columns, out_shape=jax.ShapeDtypeStruct((channels * 2...]
  transfers between devices with their start and end apart: 5 -> 5, of which waited for: 1 -> 1; matrix products, arithmetic and copies ran while one was open for 0% -> 0% of each run, Pallas kernels for 31% -> 32%
where the time goes in v6:
time: 25.1 us; the launch traced here: 25 us
  Pallas kernels  14.3 us (57%)
  starting transfers between devices  8.69 us (35%)
  local copies, waits for them, and re-layouts  1.05 us (4%)
  waiting for transfers between devices  0.65 us (3%)
    ppermute x1, starting transfers between devices, per_device(): wrap = lax.ppermute(wrap, ('lon', 'lat'), pairs)  4.7 us
    pallas_call x1, Pallas kernels, per_device(): pl.pallas_call(second_layer, out_shape=jax.ShapeDtypeStruct((channels, ro...  4.35 us
    ppermute x1, starting transfers between devices, per_device(): first = lax.ppermute(first, 'lat', pairs)  3 us
    pallas_call x1, Pallas kernels, per_device(): pl.pallas_call(edge_rows, out_shape=jax.ShapeDtypeStruct((channels * 24,...  2.53 us
    pallas_call x1, Pallas kernels, per_device(): pl.pallas_call(inner_rows, out_shape=jax.ShapeDtypeStruct((channels * 24,...  1.93 us
    pallas_call x1, Pallas kernels, per_device(): pl.pallas_call(edge_columns, out_shape=jax.ShapeDtypeStruct((channels * 2...  1.88 us
    pallas_call x1, Pallas kernels, per_device(): pl.pallas_call(weights, out_shape=[jax.ShapeDtypeStruct((channels * 24, 2...  1.65 us
    unnamed x20, local copies, waits for them, and re-layouts  1.05 us
  transfers between devices with their start and end apart: 5, of which 1 were waited for; matrix products, arithmetic and copies ran while one was open for 0% of the time, Pallas kernels for 32%

profile of v6, /device:TPU:0, one launch (start us, length us, event | category | flops | bytes accessed | tf_op | source)
XLA Modules:
  0.0 25.0 jit_solution(8257223604132703458)
XLA Ops:
  0.0 0.0 copy-start.1
  0.0 0.0 copy-start.2
  0.0 1.0 %copy-done.1 = bf16[96,16,128]{2,1,0:T(8,128)(2,1)S(1)} copy-done((bf16[96,16,128]{2,1,0:T(8,128)(2,1)S(1)}, bf16[96,16,128]{2,1,0:T(8,128)(2,1)}, u32[]{:S(2)}) %copy-start.1) | copy-done | bytes 393240
  1.0 0.0 copy-done.2
  1.0 0.2 shard_map.101.after_ref
  1.2 0.0 copy-start.3
  1.2 0.0 copy-start.4
  1.2 0.0 copy-start.5
  1.3 0.0 copy-start.6
  1.3 0.0 copy-start.7
  1.3 0.0 copy-start.8
  1.3 0.0 copy-start.9
  1.3 3.0 %collective-permute-start.1 = (bf16[592,128]{1,0:T(8,128)(2,1)S(1)}, bf16[592,128]{1,0:T(8,128)(2,1)S(1)}, u32[]{:S(2)}, u32[]{:S(2)}) collective-permute-start(bf16[592,128]{1,0:T(8,128)(2,1)S(1)} %shard_map.101.after_ref), channel_id=1, source_target_pairs={{0,1},{1,0},{2,3},{3,2},{4,5},{5,4},{6,7},{7,6},{8,9},{9,8},{10,11... | collective-permute-start | bytes 454664 | tf_op jit(solution)/shard_map/ppermute | solution.py:674
  4.3 0.2 shard_map.102.sent_ref
  4.5 0.1 collective-permute-start
  4.6 0.0 copy-done.3
  4.6 0.0 copy-done.4
  4.6 0.0 copy-done.5
  4.6 0.0 copy-done.6
  4.6 0.0 copy-done.7
  4.7 0.0 copy-done.8
  4.7 0.0 copy-done.9
  4.7 0.0 copy-start
  4.7 1.6 %shard_map.104 = (bf16[2304,256]{1,0:T(8,128)(2,1)S(1)}, bf16[1536,256]{1,0:T(8,128)(2,1)S(1)}, f32[2,3,96,128]{3,2,1,0:T(8,128)S(1)}, bf16[2,384,112]{2,1,0:T(8,128)(2,1)S(1)}) custom-call(f32[49,2,96]{2,1,0:T(2,128)S(1)} %bitcast.5, f32[2,96]{1,0:T(2,128)S(1)} %copy-done.6, f32[2,96]{1,0:T(2,128)S(1)} %copy-done.7, f32[2,96]{1,0:T(2,128)S(1)} %copy-done.8, ...), custom_call_target="tpu_custom_call" | custom-call | flops 2000000000 | bytes 1048576 | tf_op jit(solution)/shard_map/pallas_call | solution.py:677
  6.3 0.0 copy-done
  6.4 1.9 %shard_map.105.after_ref.old_ref = f32[2304,128]{1,0:T(8,128)S(1)} custom-call(bf16[96,16,128]{2,1,0:T(8,128)(2,1)S(1)} %copy-done.1, bf16[2304,256]{1,0:T(8,128)(2,1)S(1)} %get-tuple-element.21.matrix_ref, f32[2,3,96,128]{3,2,1,0:T(8,128)S(1)} %get-tuple-element.22.rows_ref, bf16[2,384,112]{2,1,0:T(8,128)(2,1)S(1)} %get-tuple-element.23.expand_ref, ...), custom_call_target="tpu_custom_call" | custom-call | flops 4000000000 | bytes 1048576 | tf_op jit(solution)/shard_map/pallas_call | solution.py:704
  8.3 0.0 collective-permute-done.1.first_ref
  8.3 0.6 %shard_map.103 = (bf16[96,16,128]{2,1,0:T(8,128)(2,1)S(1)}, f32[16,128]{1,0:T(8,128)S(1)}, bf16[208,128]{1,0:T(8,128)(2,1)S(1)}, bf16[224,128]{1,0:T(8,128)(2,1)S(1)}) custom-call(bf16[96,16,128]{2,1,0:T(8,128)(2,1)S(1)} %copy-done.1, s32[16,128]{1,0:T(8,128)S(1)} %copy-done.2, bf16[592,128]{1,0:T(8,128)(2,1)S(1)} %collective-permute-done.1.first_ref), custom_call_target="tpu_custom_call" | custom-call | flops 1000000000 | bytes 1048576 | tf_op jit(solution)/shard_map/pallas_call | solution.py:716
  8.9 4.7 %collective-permute-start.4 = (bf16[224,128]{1,0:T(8,128)(2,1)S(1)}, bf16[224,128]{1,0:T(8,128)(2,1)S(1)}, u32[]{:S(2)}, u32[]{:S(2)}) collective-permute-start(bf16[224,128]{1,0:T(8,128)(2,1)S(1)} %get-tuple-element.28), channel_id=1, source_target_pairs={{0,30},{30,0},{2,3},{4,5},{6,7},{8,9},{10,11},{12,13},{14,15},{16,... | collective-permute-start | bytes 172040 | tf_op jit(solution)/shard_map/ppermute | solution.py:738
  13.6 0.0 collective-permute-done.second_ref
  13.6 0.8 %shard_map.106 = (bf16[96,16,128]{2,1,0:T(8,128)(2,1)S(1)}, f32[16,128]{1,0:T(8,128)S(1)}, bf16[416,128]{1,0:T(8,128)(2,1)S(1)}, bf16[224,128]{1,0:T(8,128)(2,1)S(1)}, bf16[224,128]{1,0:T(8,128)(2,1)S(1)}) custom-call(bf16[592,128]{1,0:T(8,128)(2,1)S(1)} %collective-permute-done.second_ref, bf16[592,128]{1,0:T(8,128)(2,1)S(1)} %shard_map.102.sent_ref, ...), custom_call_target="tpu_custom_call" | custom-call | tf_op jit(solution)/shard_map/pallas_call | solution.py:741
  14.5 0.8 %collective-permute-start.3 = (bf16[224,128]{1,0:T(8,128)(2,1)S(1)}, bf16[224,128]{1,0:T(8,128)(2,1)S(1)}, u32[]{:S(2)}, u32[]{:S(2)}) collective-permute-start(bf16[224,128]{1,0:T(8,128)(2,1)S(1)} %get-tuple-element.27.after_ref), channel_id=1, source_target_pairs={{2,4},{4,2},{6,8},{8,6},{10,12},{12,10},{14,16},{16,14},{18,20},{2... | collective-permute-start | bytes 172040 | tf_op jit(solution)/shard_map/ppermute | solution.py:778
  15.3 0.1 shard_map.107
  15.4 0.1 collective-permute-start.2
  15.5 2.5 %shard_map.109.update_ref = f32[2304,128]{1,0:T(8,128)S(1)} custom-call(bf16[96,16,128]{2,1,0:T(8,128)(2,1)S(1)} %copy-done.1, bf16[96,16,128]{2,1,0:T(8,128)(2,1)S(1)} %get-tuple-element.24.halo_ref, bf16[2304,256]{1,0:T(8,128)(2,1)S(1)} %get-tuple-element.21.matrix_ref, ...), custom_call_target="tpu_custom_call", output_to_operand_aliasing={{}: (6, {})} | custom-call | flops 4000000000 | bytes 1048576 | tf_op jit(solution)/shard_map/pallas_call | solution.py:780
  18.0 0.0 collective-permute-done.4.wrap_ref
  18.1 0.0 collective-permute-done.2.core_ref
  18.1 0.6 %collective-permute-done.3.cross_ref = bf16[224,128]{1,0:T(8,128)(2,1)S(1)} collective-permute-done((bf16[224,128]{1,0:T(8,128)(2,1)S(1)}, bf16[224,128]{1,0:T(8,128)(2,1)S(1)}, u32[]{:S(2)}, u32[]{:S(2)}) %collective-permute-start.3) | collective-permute-done | bytes 57376 | tf_op jit(solution)/shard_map/ppermute | solution.py:778
  18.7 1.9 %shard_map.108.strips = f32[2304,128]{1,0:T(8,128)S(1)} custom-call(bf16[224,128]{1,0:T(8,128)(2,1)S(1)} %collective-permute-done.2.core_ref, bf16[224,128]{1,0:T(8,128)(2,1)S(1)} %collective-permute-done.3.cross_ref, bf16[224,128]{1,0:T(8,128)(2,1)S(1)} %collective-permute-done.4.wrap_ref, bf16[224,128]{1,0:T(8,128)(2,1)S(1)} %get-tuple-element.29.own_ref, ...), custom_call_target="tpu_custom_call" | custom-call | tf_op jit(solution)/shard_map/pallas_call | solution.py:791
  20.6 4.3 %shard_map.110 = bf16[96,16,128]{2,1,0:T(8,128)(2,1)} custom-call(bf16[96,16,128]{2,1,0:T(8,128)(2,1)S(1)} %copy-done.1, s32[16,128]{1,0:T(8,128)S(1)} %copy-done.2, bf16[96,16,128]{2,1,0:T(8,128)(2,1)S(1)} %get-tuple-element.24.halo_ref, f32[16,128]{1,0:T(8,128)S(1)} %get-tuple-element.25.halo_mask_ref, ...), custom_call_target="tpu_custom_call" | custom-call | tf_op jit(solution)/shard_map/pallas_call | solution.py:800
  (1 shorter events, 0.0 us)
Async XLA Ops:
  0.0 1.0 %copy-start.1 = (bf16[96,16,128]{2,1,0:T(8,128)(2,1)S(1)}, bf16[96,16,128]{2,1,0:T(8,128)(2,1)}, u32[]{:S(2)}) copy-start(bf16[96,16,128]{2,1,0:T(8,128)(2,1)} %field_ref.11) | copy-start | bytes 1179652
  0.0 1.0 %copy-start.2 = (s32[16,128]{1,0:T(8,128)S(1)}, s32[16,128]{1,0:T(8,128)}, u32[]{:S(2)}) copy-start(s32[16,128]{1,0:T(8,128)} %mask_ref.7) | copy-start | bytes 24580
  1.2 3.4 %copy-start.3 = (bf16[2,384,96]{1,2,0:T(8,128)(2,1)S(1)}, bf16[2,384,96]{1,2,0:T(8,128)(2,1)}, u32[]{:S(2)}) copy-start(bf16[2,384,96]{1,2,0:T(8,128)(2,1)} %param.16) | copy-start | bytes 442372
  1.2 3.4 %copy-start.4 = (f32[2,96,7,7]{1,0,3,2:T(2,128)S(1)}, f32[2,96,7,7]{1,0,3,2:T(2,128)}, u32[]{:S(2)}) copy-start(f32[2,96,7,7]{1,0,3,2:T(2,128)} %param.12) | copy-start | bytes 112900
  1.2 3.4 %copy-start.5 = (f32[2,384]{1,0:T(2,128)S(1)}, f32[2,384]{1,0:T(2,128)}, u32[]{:S(2)}) copy-start(f32[2,384]{1,0:T(2,128)} %expand_bias_ref.1) | copy-start | bytes 9220
  1.3 3.4 %copy-start.6 = (f32[2,96]{1,0:T(2,128)S(1)}, f32[2,96]{1,0:T(2,128)}, u32[]{:S(2)}) copy-start(f32[2,96]{1,0:T(2,128)} %bias_ref.1) | copy-start | bytes 2308
  1.3 3.4 %copy-start.7 = (f32[2,96]{1,0:T(2,128)S(1)}, f32[2,96]{1,0:T(2,128)}, u32[]{:S(2)}) copy-start(f32[2,96]{1,0:T(2,128)} %gain_ref.1) | copy-start | bytes 2308
  1.3 3.4 %copy-start.8 = (f32[2,96]{1,0:T(2,128)S(1)}, f32[2,96]{1,0:T(2,128)}, u32[]{:S(2)}) copy-start(f32[2,96]{1,0:T(2,128)} %norm_bias_ref.1) | copy-start | bytes 2308
  1.3 3.4 %copy-start.9 = (f32[2,96]{1,0:T(2,128)S(1)}, f32[2,96]{1,0:T(2,128)}, u32[]{:S(2)}) copy-start(f32[2,96]{1,0:T(2,128)} %reduce_bias_ref.1) | copy-start | bytes 2308
  1.3 7.0 %collective-permute-start.1 = (bf16[592,128]{1,0:T(8,128)(2,1)S(1)}, bf16[592,128]{1,0:T(8,128)(2,1)S(1)}, u32[]{:S(2)}, u32[]{:S(2)}) collective-permute-start(bf16[592,128]{1,0:T(8,128)(2,1)S(1)} %shard_map.101.after_ref), channel_id=1, source_target_pairs={{0,1},{1,0},{2,3},{3,2},{4,5},{5,4},{6,7},{7,6},{8,9},{9,8},{10,11... | collective-permute-start | bytes 454664 | tf_op jit(solution)/shard_map/ppermute | solution.py:674
  4.5 9.1 %collective-permute-start = (bf16[592,128]{1,0:T(8,128)(2,1)S(1)}, bf16[592,128]{1,0:T(8,128)(2,1)S(1)}, u32[]{:S(2)}, u32[]{:S(2)}) collective-permute-start(bf16[592,128]{1,0:T(8,128)(2,1)S(1)} %shard_map.102.sent_ref), channel_id=1, source_target_pairs={{1,31},{0,2},{3,29},{2,0},{5,27},{4,6},{7,25},{6,4},{9,23},{8,10},... | collective-permute-start | bytes 454664 | tf_op jit(solution)/shard_map/ppermute | solution.py:670
  4.7 1.7 %copy-start = (bf16[2,96,384]{2,1,0:T(8,128)(2,1)S(1)}, bf16[2,96,384]{2,1,0:T(8,128)(2,1)}, u32[]{:S(2)}) copy-start(bf16[2,96,384]{2,1,0:T(8,128)(2,1)} %reduce_ref.7) | copy-start | bytes 442372
  8.9 9.1 %collective-permute-start.4 = (bf16[224,128]{1,0:T(8,128)(2,1)S(1)}, bf16[224,128]{1,0:T(8,128)(2,1)S(1)}, u32[]{:S(2)}, u32[]{:S(2)}) collective-permute-start(bf16[224,128]{1,0:T(8,128)(2,1)S(1)} %get-tuple-element.28), channel_id=1, source_target_pairs={{0,30},{30,0},{2,3},{4,5},{6,7},{8,9},{10,11},{12,13},{14,15},{16,... | collective-permute-start | bytes 172040 | tf_op jit(solution)/shard_map/ppermute | solution.py:738
  14.5 4.2 %collective-permute-start.3 = (bf16[224,128]{1,0:T(8,128)(2,1)S(1)}, bf16[224,128]{1,0:T(8,128)(2,1)S(1)}, u32[]{:S(2)}, u32[]{:S(2)}) collective-permute-start(bf16[224,128]{1,0:T(8,128)(2,1)S(1)} %get-tuple-element.27.after_ref), channel_id=1, source_target_pairs={{2,4},{4,2},{6,8},{8,6},{10,12},{12,10},{14,16},{16,14},{18,20},{2... | collective-permute-start | bytes 172040 | tf_op jit(solution)/shard_map/ppermute | solution.py:778
  15.4 2.6 %collective-permute-start.2 = (bf16[224,128]{1,0:T(8,128)(2,1)S(1)}, bf16[224,128]{1,0:T(8,128)(2,1)S(1)}, u32[]{:S(2)}, u32[]{:S(2)}) collective-permute-start(bf16[224,128]{1,0:T(8,128)(2,1)S(1)} %shard_map.107), channel_id=1, source_target_pairs={{0,2},{2,0},{4,6},{6,4},{8,10},{10,8},{12,14},{14,12},{16,18},{18,... | collective-permute-start | bytes 172040 | tf_op jit(solution)/shard_map/ppermute | solution.py:769

commit v7 on v6

--- a/solution.py
+++ b/solution.py
@@ -9,6 +9,7 @@
 
 
 HALO = 6
+APART = 24
 VMEM_LIMIT = 20 * 1024 * 1024
 
 
@@ -42,11 +43,12 @@
     channels, rows, width = field_ref.shape
     even = lax.rem(lax.axis_index("lat"), 2) == 0
     take_upper = even if upper_if_even else jnp.logical_not(even)
-    wide[...] = field_ref[...].astype(jnp.float32).reshape(channels * rows, width)
+    for c in range(channels):
+        wide[c * APART : c * APART + rows, :] = field_ref[c].astype(jnp.float32)
     wide_mask[...] = mask_ref[...].astype(jnp.float32)
     for k in range(HALO):
-        lower = wide[pl.ds(k, channels, stride=rows), :]
-        upper = wide[pl.ds(rows - HALO + k, channels, stride=rows), :]
+        lower = wide[pl.ds(k, channels, stride=APART), :]
+        upper = wide[pl.ds(rows - HALO + k, channels, stride=APART), :]
         at = pl.ds(k * channels, channels)
         out_ref[at, :] = (kept * jnp.where(take_upper, upper, lower)).astype(jnp.bfloat16)
     pad = jnp.zeros((16 - HALO, width), jnp.float32)
@@ -85,8 +87,13 @@
     for k in range(HALO):
         row = k if turned is None else jnp.where(turned, HALO - 1 - k, k)
         place = jnp.where(is_north, north_place(row), south_place(k))
-        wide[pl.ds(place, channels, stride=16), :] = rows_at(k * channels, channels)
+        wide[pl.ds(place, channels, stride=APART), :] = rows_at(k * channels, channels)
         mask_rows[pl.ds(place, 1), :] = masks[k : k + 1, :]
+
+
+def placed(wide, channels):
+    blocks = wide[...].reshape(channels, APART, wide.shape[1])
+    return blocks[:, :16, :].astype(jnp.bfloat16)
 
 
 def pack_ends(blocks):
@@ -113,7 +120,7 @@
     channels, rows, width = field_ref.shape
     even = lax.rem(lax.axis_index("lat"), 2) == 0
     place_rows(first_ref, even, None, wide, mask_rows, channels)
-    halo_ref[...] = wide[...].astype(jnp.bfloat16).reshape(channels, 16, width)
+    halo_ref[...] = placed(wide, channels)
     groups = channels // 8
     for g in range(groups):
         blocks = [field_ref[channel_of(channels, g, j)] for j in range(8)]
@@ -186,12 +193,12 @@
         @pl.when(folded & over_wrap())
         def _():
             place_rows(sent_ref, odd, folded, wide, mask_rows, channels)
-            halo_ref[...] = wide[...].astype(jnp.bfloat16).reshape(channels, 16, width)
+            halo_ref[...] = placed(wide, channels)
             join_ends(None, halo_ref, mask_rows, ends_ref)
             pack_side(ends_ref, own_ref, jnp.logical_not(lon_odd))
 
     place_rows(second_ref, odd, folded, wide, mask_rows, channels)
-    far = wide[...].astype(jnp.bfloat16).reshape(channels, 16, width)
+    far = placed(wide, channels)
     halo_ref[...] = near_halo_ref[...] + far
     halo_mask_ref[...] = near_mask_ref[...] + mask_rows[...]
     join_ends(own_ends_ref, halo_ref, halo_mask_ref, ends_ref)
@@ -530,6 +537,7 @@
     out_ref,
     main_ref,
     conv,
+    changes,
     normed,
     inner,
 ):
@@ -587,24 +595,15 @@
             result = jnp.dot(matrix, stack, preferred_element_type=jnp.float32)
             conv[pl.ds(c, 16, stride=pitch(channels)), :] = result
 
-    mask = mask_ref[...].astype(jnp.float32)
-    changes = []
-
     def put(n, change):
-        changes.append(change)
-        if n < rows - 1:
-            return
-        for c in range(0, channels, 8):
-            parts = []
-            for half in range(0, rows, 8):
-                part = [changes[i][c : c + 8, :] for i in range(half, half + 8)]
-                parts.append(jnp.swapaxes(jnp.stack(part, axis=0), 0, 1))
-            change = jnp.concatenate(parts, axis=1)
-            old = main_ref[c : c + 8].astype(jnp.float32)
-            out_ref[c : c + 8] = (mask[None] * (old + change)).astype(jnp.bfloat16)
+        changes[pl.ds(n, channels, stride=APART), :] = change
 
     blocks = [conv_row(conv, channels, i) for i in range(rows)]
     mlp(rows_ref, expand_ref, reduce_ref, 1, blocks, normed, inner, put)
+    mask = main_mask[:rows, :]
+    for c in range(channels):
+        change = changes[c * APART : c * APART + rows, :]
+        out_ref[c] = (mask * (main_ref[c].astype(jnp.float32) + change)).astype(jnp.bfloat16)
 
 
 def per_device(
@@ -639,7 +638,7 @@
             in_specs=vmem(2) + [pl.BlockSpec(memory_space=pl.ANY)],
             out_specs=pl.BlockSpec(memory_space=pltpu.VMEM),
             scratch_shapes=[
-                pltpu.VMEM((channels * rows, width), f32),
+                pltpu.VMEM((channels * APART, width), f32),
                 pltpu.VMEM((rows, width), f32),
             ],
             compiler_params=params(),
@@ -724,7 +723,7 @@
         in_specs=vmem(3),
         out_specs=vmem(4),
         scratch_shapes=[
-            pltpu.VMEM((channels * 16, width), f32),
+            pltpu.VMEM((channels * APART, width), f32),
             pltpu.VMEM((groups * 32, width), bf16),
         ],
         compiler_params=params(),
@@ -750,7 +749,7 @@
         in_specs=vmem(5) + [pl.BlockSpec(memory_space=pl.ANY)],
         out_specs=vmem(5),
         scratch_shapes=[
-            pltpu.VMEM((channels * 16, width), f32),
+            pltpu.VMEM((channels * APART, width), f32),
             pltpu.VMEM((16, width), f32),
         ],
         compiler_params=params(),
@@ -805,6 +804,7 @@
         scratch_shapes=[
             pltpu.VMEM((channels, rows, width), bf16),
             pltpu.VMEM((pitch(channels) * 16, width), f32),
+            pltpu.VMEM((channels * APART, width), f32),
         ]
         + buffers(rows),
         compiler_params=params(),

time: 25.1 us -> 24.8 us (0.988)
  Pallas kernels: 14.3 us -> 14 us
  transfers between devices with their start and end apart: 5 -> 5, of which waited for: 1 -> 1; matrix products, arithmetic and copies ran while one was open for 0% -> 0% of each run, Pallas kernels for 32% -> 31%
where the time goes in v7:
time: 24.8 us; the launch traced here: 24.6 us
  Pallas kernels  14 us (56%)
  starting transfers between devices  8.7 us (35%)
  local copies, waits for them, and re-layouts  1.05 us (4%)
  waiting for transfers between devices  0.65 us (3%)
    ppermute x1, starting transfers between devices, per_device(): wrap = lax.ppermute(wrap, ('lon', 'lat'), pairs)  4.66 us
    pallas_call x1, Pallas kernels, per_device(): pl.pallas_call(second_layer, out_shape=jax.ShapeDtypeStruct((channels, ro...  4.34 us
    ppermute x1, starting transfers between devices, per_device(): first = lax.ppermute(first, 'lat', pairs)  3 us
    pallas_call x1, Pallas kernels, per_device(): pl.pallas_call(edge_rows, out_shape=jax.ShapeDtypeStruct((channels * 24,...  2.53 us
    pallas_call x1, Pallas kernels, per_device(): pl.pallas_call(inner_rows, out_shape=jax.ShapeDtypeStruct((channels * 24,...  1.93 us
    pallas_call x1, Pallas kernels, per_device(): pl.pallas_call(edge_columns, out_shape=jax.ShapeDtypeStruct((channels * 2...  1.88 us
    pallas_call x1, Pallas kernels, per_device(): pl.pallas_call(weights, out_shape=[jax.ShapeDtypeStruct((channels * 24, 2...  1.64 us
    unnamed x20, local copies, waits for them, and re-layouts  1.05 us
  transfers between devices with their start and end apart: 5, of which 1 were waited for; matrix products, arithmetic and copies ran while one was open for 0% of the time, Pallas kernels for 31%

profile of v7, /device:TPU:0, one launch (start us, length us, event | category | flops | bytes accessed | tf_op | source)
XLA Modules:
  0.0 24.6 jit_solution(465430581924134810)
XLA Ops:
  0.0 0.0 copy-start.1
  0.0 0.0 copy-start.2
  0.0 1.0 %copy-done.1 = bf16[96,16,128]{2,1,0:T(8,128)(2,1)S(1)} copy-done((bf16[96,16,128]{2,1,0:T(8,128)(2,1)S(1)}, bf16[96,16,128]{2,1,0:T(8,128)(2,1)}, u32[]{:S(2)}) %copy-start.1) | copy-done | bytes 393240
  1.0 0.0 copy-done.2
  1.0 0.1 shard_map.101.after_ref
  1.1 0.0 copy-start.3
  1.1 0.0 copy-start.4
  1.2 0.0 copy-start.5
  1.2 0.0 copy-start.6
  1.2 0.0 copy-start.7
  1.2 0.0 copy-start.8
  1.2 0.0 copy-start.9
  1.2 3.0 %collective-permute-start.1 = (bf16[592,128]{1,0:T(8,128)(2,1)S(1)}, bf16[592,128]{1,0:T(8,128)(2,1)S(1)}, u32[]{:S(2)}, u32[]{:S(2)}) collective-permute-start(bf16[592,128]{1,0:T(8,128)(2,1)S(1)} %shard_map.101.after_ref), channel_id=1, source_target_pairs={{0,1},{1,0},{2,3},{3,2},{4,5},{5,4},{6,7},{7,6},{8,9},{9,8},{10,11... | collective-permute-start | bytes 454664 | tf_op jit(solution)/shard_map/ppermute | solution.py:673
  4.2 0.1 shard_map.102.sent_ref
  4.4 0.1 collective-permute-start
  4.4 0.0 copy-done.3
  4.4 0.0 copy-done.4
  4.5 0.0 copy-done.5
  4.5 0.0 copy-done.6
  4.5 0.0 copy-done.7
  4.5 0.0 copy-done.8
  4.5 0.0 copy-done.9
  4.5 0.0 copy-start
  4.5 1.6 %shard_map.104 = (bf16[2304,256]{1,0:T(8,128)(2,1)S(1)}, bf16[1536,256]{1,0:T(8,128)(2,1)S(1)}, f32[2,3,96,128]{3,2,1,0:T(8,128)S(1)}, bf16[2,384,112]{2,1,0:T(8,128)(2,1)S(1)}) custom-call(f32[49,2,96]{2,1,0:T(2,128)S(1)} %bitcast.5, f32[2,96]{1,0:T(2,128)S(1)} %copy-done.6, f32[2,96]{1,0:T(2,128)S(1)} %copy-done.7, f32[2,96]{1,0:T(2,128)S(1)} %copy-done.8, ...), custom_call_target="tpu_custom_call" | custom-call | flops 2000000000 | bytes 1048576 | tf_op jit(solution)/shard_map/pallas_call | solution.py:676
  6.2 0.0 copy-done
  6.2 1.9 %shard_map.105.after_ref.old_ref = f32[2304,128]{1,0:T(8,128)S(1)} custom-call(bf16[96,16,128]{2,1,0:T(8,128)(2,1)S(1)} %copy-done.1, bf16[2304,256]{1,0:T(8,128)(2,1)S(1)} %get-tuple-element.21.matrix_ref, f32[2,3,96,128]{3,2,1,0:T(8,128)S(1)} %get-tuple-element.22.rows_ref, bf16[2,384,112]{2,1,0:T(8,128)(2,1)S(1)} %get-tuple-element.23.expand_ref, ...), custom_call_target="tpu_custom_call" | custom-call | flops 4000000000 | bytes 1048576 | tf_op jit(solution)/shard_map/pallas_call | solution.py:703
  8.1 0.1 collective-permute-done.1.first_ref
  8.2 0.5 %shard_map.103 = (bf16[96,16,128]{2,1,0:T(8,128)(2,1)S(1)}, f32[16,128]{1,0:T(8,128)S(1)}, bf16[208,128]{1,0:T(8,128)(2,1)S(1)}, bf16[224,128]{1,0:T(8,128)(2,1)S(1)}) custom-call(bf16[96,16,128]{2,1,0:T(8,128)(2,1)S(1)} %copy-done.1, s32[16,128]{1,0:T(8,128)S(1)} %copy-done.2, bf16[592,128]{1,0:T(8,128)(2,1)S(1)} %collective-permute-done.1.first_ref), custom_call_target="tpu_custom_call" | custom-call | flops 1000000000 | bytes 1048576 | tf_op jit(solution)/shard_map/pallas_call | solution.py:715
  8.7 4.7 %collective-permute-start.4 = (bf16[224,128]{1,0:T(8,128)(2,1)S(1)}, bf16[224,128]{1,0:T(8,128)(2,1)S(1)}, u32[]{:S(2)}, u32[]{:S(2)}) collective-permute-start(bf16[224,128]{1,0:T(8,128)(2,1)S(1)} %get-tuple-element.28), channel_id=1, source_target_pairs={{0,30},{30,0},{2,3},{4,5},{6,7},{8,9},{10,11},{12,13},{14,15},{16,... | collective-permute-start | bytes 172040 | tf_op jit(solution)/shard_map/ppermute | solution.py:737
  13.4 0.0 collective-permute-done.second_ref
  13.4 0.8 %shard_map.106 = (bf16[96,16,128]{2,1,0:T(8,128)(2,1)S(1)}, f32[16,128]{1,0:T(8,128)S(1)}, bf16[416,128]{1,0:T(8,128)(2,1)S(1)}, bf16[224,128]{1,0:T(8,128)(2,1)S(1)}, bf16[224,128]{1,0:T(8,128)(2,1)S(1)}) custom-call(bf16[592,128]{1,0:T(8,128)(2,1)S(1)} %collective-permute-done.second_ref, bf16[592,128]{1,0:T(8,128)(2,1)S(1)} %shard_map.102.sent_ref, ...), custom_call_target="tpu_custom_call" | custom-call | tf_op jit(solution)/shard_map/pallas_call | solution.py:740
  14.2 0.9 %collective-permute-start.3 = (bf16[224,128]{1,0:T(8,128)(2,1)S(1)}, bf16[224,128]{1,0:T(8,128)(2,1)S(1)}, u32[]{:S(2)}, u32[]{:S(2)}) collective-permute-start(bf16[224,128]{1,0:T(8,128)(2,1)S(1)} %get-tuple-element.27.after_ref), channel_id=1, source_target_pairs={{2,4},{4,2},{6,8},{8,6},{10,12},{12,10},{14,16},{16,14},{18,20},{2... | collective-permute-start | bytes 172040 | tf_op jit(solution)/shard_map/ppermute | solution.py:777
  15.1 0.1 shard_map.107
  15.2 0.1 collective-permute-start.2
  15.2 2.5 %shard_map.109.update_ref = f32[2304,128]{1,0:T(8,128)S(1)} custom-call(bf16[96,16,128]{2,1,0:T(8,128)(2,1)S(1)} %copy-done.1, bf16[96,16,128]{2,1,0:T(8,128)(2,1)S(1)} %get-tuple-element.24.halo_ref, bf16[2304,256]{1,0:T(8,128)(2,1)S(1)} %get-tuple-element.21.matrix_ref, ...), custom_call_target="tpu_custom_call", output_to_operand_aliasing={{}: (6, {})} | custom-call | flops 4000000000 | bytes 1048576 | tf_op jit(solution)/shard_map/pallas_call | solution.py:779
  17.8 0.0 collective-permute-done.4.wrap_ref
  17.8 0.0 collective-permute-done.2.core_ref
  17.8 0.6 %collective-permute-done.3.cross_ref = bf16[224,128]{1,0:T(8,128)(2,1)S(1)} collective-permute-done((bf16[224,128]{1,0:T(8,128)(2,1)S(1)}, bf16[224,128]{1,0:T(8,128)(2,1)S(1)}, u32[]{:S(2)}, u32[]{:S(2)}) %collective-permute-start.3) | collective-permute-done | bytes 57376 | tf_op jit(solution)/shard_map/ppermute | solution.py:777
  18.4 1.9 %shard_map.108.strips = f32[2304,128]{1,0:T(8,128)S(1)} custom-call(bf16[224,128]{1,0:T(8,128)(2,1)S(1)} %collective-permute-done.2.core_ref, bf16[224,128]{1,0:T(8,128)(2,1)S(1)} %collective-permute-done.3.cross_ref, bf16[224,128]{1,0:T(8,128)(2,1)S(1)} %collective-permute-done.4.wrap_ref, bf16[224,128]{1,0:T(8,128)(2,1)S(1)} %get-tuple-element.29.own_ref, ...), custom_call_target="tpu_custom_call" | custom-call | tf_op jit(solution)/shard_map/pallas_call | solution.py:790
  20.3 4.3 %shard_map.110 = bf16[96,16,128]{2,1,0:T(8,128)(2,1)} custom-call(bf16[96,16,128]{2,1,0:T(8,128)(2,1)S(1)} %copy-done.1, s32[16,128]{1,0:T(8,128)S(1)} %copy-done.2, bf16[96,16,128]{2,1,0:T(8,128)(2,1)S(1)} %get-tuple-element.24.halo_ref, f32[16,128]{1,0:T(8,128)S(1)} %get-tuple-element.25.halo_mask_ref, ...), custom_call_target="tpu_custom_call" | custom-call | tf_op jit(solution)/shard_map/pallas_call | solution.py:799
  (1 shorter events, 0.0 us)
Async XLA Ops:
  0.0 1.0 %copy-start.1 = (bf16[96,16,128]{2,1,0:T(8,128)(2,1)S(1)}, bf16[96,16,128]{2,1,0:T(8,128)(2,1)}, u32[]{:S(2)}) copy-start(bf16[96,16,128]{2,1,0:T(8,128)(2,1)} %field_ref.11) | copy-start | bytes 1179652
  0.0 1.0 %copy-start.2 = (s32[16,128]{1,0:T(8,128)S(1)}, s32[16,128]{1,0:T(8,128)}, u32[]{:S(2)}) copy-start(s32[16,128]{1,0:T(8,128)} %mask_ref.7) | copy-start | bytes 24580
  1.1 3.3 %copy-start.3 = (bf16[2,384,96]{1,2,0:T(8,128)(2,1)S(1)}, bf16[2,384,96]{1,2,0:T(8,128)(2,1)}, u32[]{:S(2)}) copy-start(bf16[2,384,96]{1,2,0:T(8,128)(2,1)} %param.16) | copy-start | bytes 442372
  1.1 3.3 %copy-start.4 = (f32[2,96,7,7]{1,0,3,2:T(2,128)S(1)}, f32[2,96,7,7]{1,0,3,2:T(2,128)}, u32[]{:S(2)}) copy-start(f32[2,96,7,7]{1,0,3,2:T(2,128)} %param.12) | copy-start | bytes 112900
  1.2 3.3 %copy-start.5 = (f32[2,384]{1,0:T(2,128)S(1)}, f32[2,384]{1,0:T(2,128)}, u32[]{:S(2)}) copy-start(f32[2,384]{1,0:T(2,128)} %expand_bias_ref.1) | copy-start | bytes 9220
  1.2 3.3 %copy-start.6 = (f32[2,96]{1,0:T(2,128)S(1)}, f32[2,96]{1,0:T(2,128)}, u32[]{:S(2)}) copy-start(f32[2,96]{1,0:T(2,128)} %bias_ref.1) | copy-start | bytes 2308
  1.2 3.3 %copy-start.7 = (f32[2,96]{1,0:T(2,128)S(1)}, f32[2,96]{1,0:T(2,128)}, u32[]{:S(2)}) copy-start(f32[2,96]{1,0:T(2,128)} %gain_ref.1) | copy-start | bytes 2308
  1.2 3.3 %copy-start.8 = (f32[2,96]{1,0:T(2,128)S(1)}, f32[2,96]{1,0:T(2,128)}, u32[]{:S(2)}) copy-start(f32[2,96]{1,0:T(2,128)} %norm_bias_ref.1) | copy-start | bytes 2308
  1.2 3.3 %copy-start.9 = (f32[2,96]{1,0:T(2,128)S(1)}, f32[2,96]{1,0:T(2,128)}, u32[]{:S(2)}) copy-start(f32[2,96]{1,0:T(2,128)} %reduce_bias_ref.1) | copy-start | bytes 2308
  1.2 6.9 %collective-permute-start.1 = (bf16[592,128]{1,0:T(8,128)(2,1)S(1)}, bf16[592,128]{1,0:T(8,128)(2,1)S(1)}, u32[]{:S(2)}, u32[]{:S(2)}) collective-permute-start(bf16[592,128]{1,0:T(8,128)(2,1)S(1)} %shard_map.101.after_ref), channel_id=1, source_target_pairs={{0,1},{1,0},{2,3},{3,2},{4,5},{5,4},{6,7},{7,6},{8,9},{9,8},{10,11... | collective-permute-start | bytes 454664 | tf_op jit(solution)/shard_map/ppermute | solution.py:673
  4.4 9.0 %collective-permute-start = (bf16[592,128]{1,0:T(8,128)(2,1)S(1)}, bf16[592,128]{1,0:T(8,128)(2,1)S(1)}, u32[]{:S(2)}, u32[]{:S(2)}) collective-permute-start(bf16[592,128]{1,0:T(8,128)(2,1)S(1)} %shard_map.102.sent_ref), channel_id=1, source_target_pairs={{1,31},{0,2},{3,29},{2,0},{5,27},{4,6},{7,25},{6,4},{9,23},{8,10},... | collective-permute-start | bytes 454664 | tf_op jit(solution)/shard_map/ppermute | solution.py:669
  4.5 1.7 %copy-start = (bf16[2,96,384]{2,1,0:T(8,128)(2,1)S(1)}, bf16[2,96,384]{2,1,0:T(8,128)(2,1)}, u32[]{:S(2)}) copy-start(bf16[2,96,384]{2,1,0:T(8,128)(2,1)} %reduce_ref.7) | copy-start | bytes 442372
  8.7 9.1 %collective-permute-start.4 = (bf16[224,128]{1,0:T(8,128)(2,1)S(1)}, bf16[224,128]{1,0:T(8,128)(2,1)S(1)}, u32[]{:S(2)}, u32[]{:S(2)}) collective-permute-start(bf16[224,128]{1,0:T(8,128)(2,1)S(1)} %get-tuple-element.28), channel_id=1, source_target_pairs={{0,30},{30,0},{2,3},{4,5},{6,7},{8,9},{10,11},{12,13},{14,15},{16,... | collective-permute-start | bytes 172040 | tf_op jit(solution)/shard_map/ppermute | solution.py:737
  14.2 4.2 %collective-permute-start.3 = (bf16[224,128]{1,0:T(8,128)(2,1)S(1)}, bf16[224,128]{1,0:T(8,128)(2,1)S(1)}, u32[]{:S(2)}, u32[]{:S(2)}) collective-permute-start(bf16[224,128]{1,0:T(8,128)(2,1)S(1)} %get-tuple-element.27.after_ref), channel_id=1, source_target_pairs={{2,4},{4,2},{6,8},{8,6},{10,12},{12,10},{14,16},{16,14},{18,20},{2... | collective-permute-start | bytes 172040 | tf_op jit(solution)/shard_map/ppermute | solution.py:777
  15.2 2.6 %collective-permute-start.2 = (bf16[224,128]{1,0:T(8,128)(2,1)S(1)}, bf16[224,128]{1,0:T(8,128)(2,1)S(1)}, u32[]{:S(2)}, u32[]{:S(2)}) collective-permute-start(bf16[224,128]{1,0:T(8,128)(2,1)S(1)} %shard_map.107), channel_id=1, source_target_pairs={{0,2},{2,0},{4,6},{6,4},{8,10},{10,8},{12,14},{14,12},{16,18},{18,... | collective-permute-start | bytes 172040 | tf_op jit(solution)/shard_map/ppermute | solution.py:768

commit v8 on v7

--- a/solution.py
+++ b/solution.py
@@ -166,9 +166,8 @@
 
 
 def far_rows(
-    mirrored,
+    alone,
     second_ref,
-    sent_ref,
     near_halo_ref,
     near_mask_ref,
     own_ends_ref,
@@ -177,37 +176,42 @@
     halo_mask_ref,
     ends_ref,
     cross_ref,
-    own_ref,
     wide,
     mask_rows,
 ):
     del after_ref
-    channels, _, width = halo_ref.shape
+    channels = halo_ref.shape[0]
     lat = lax.axis_index("lat")
     odd = lax.rem(lat, 2) == 1
     lon_odd = lax.rem(lax.axis_index("lon"), 2) == 1
     folded = lat == lax.axis_size("lat") - 1
-    own_ref[...] = jnp.zeros_like(own_ref)
-    if mirrored:
-
-        @pl.when(folded & over_wrap())
-        def _():
-            place_rows(sent_ref, odd, folded, wide, mask_rows, channels)
-            halo_ref[...] = placed(wide, channels)
-            join_ends(None, halo_ref, mask_rows, ends_ref)
-            pack_side(ends_ref, own_ref, jnp.logical_not(lon_odd))
-
     place_rows(second_ref, odd, folded, wide, mask_rows, channels)
-    far = placed(wide, channels)
-    halo_ref[...] = near_halo_ref[...] + far
+    halo_ref[...] = near_halo_ref[...] + placed(wide, channels)
     halo_mask_ref[...] = near_mask_ref[...] + mask_rows[...]
     join_ends(own_ends_ref, halo_ref, halo_mask_ref, ends_ref)
     pack_side(ends_ref, cross_ref, lon_odd)
-    if mirrored:
+    if alone:
 
         @pl.when(over_wrap())
         def _():
             cross_ref[...] = jnp.zeros_like(cross_ref)
+
+
+def mirrored_columns(alone, sent_ref, after_ref, own_ref, wide, mask_rows, halo, ends):
+    del after_ref
+    channels = halo.shape[0]
+    lat = lax.axis_index("lat")
+    folded = lat == lax.axis_size("lat") - 1
+    own_ref[...] = jnp.zeros_like(own_ref)
+    if alone:
+
+        @pl.when(folded & over_wrap())
+        def _():
+            odd = lax.rem(lat, 2) == 1
+            place_rows(sent_ref, odd, folded, wide, mask_rows, channels)
+            halo[...] = placed(wide, channels)
+            join_ends(None, halo, mask_rows, ends)
+            pack_side(ends, own_ref, lax.rem(lax.axis_index("lon"), 2) == 0)
 
 
 def core_columns(ends_ref, after_ref, core_ref):
@@ -737,23 +741,22 @@
         wrap = lax.ppermute(wrap, ("lon", "lat"), pairs)
     else:
         wrap = jnp.zeros_like(wrap)
-    halo, halo_mask, ends, cross, own = pl.pallas_call(
+    halo, halo_mask, ends, cross = pl.pallas_call(
         functools.partial(far_rows, alone),
         out_shape=[
             jax.ShapeDtypeStruct((channels, 16, width), bf16),
             jax.ShapeDtypeStruct((16, width), f32),
             jax.ShapeDtypeStruct((groups * 32, width), bf16),
             jax.ShapeDtypeStruct((sent_rows, width), bf16),
-            jax.ShapeDtypeStruct((sent_rows, width), bf16),
         ],
-        in_specs=vmem(5) + [pl.BlockSpec(memory_space=pl.ANY)],
-        out_specs=vmem(5),
+        in_specs=vmem(4) + [pl.BlockSpec(memory_space=pl.ANY)],
+        out_specs=vmem(4),
         scratch_shapes=[
             pltpu.VMEM((channels * APART, width), f32),
             pltpu.VMEM((16, width), f32),
         ],
         compiler_params=params(),
-    )(second, second_sent, near_halo, near_mask, own_ends, update)
+    )(second, near_halo, near_mask, own_ends, update)
     core = pl.pallas_call(
         core_columns,
         out_shape=jax.ShapeDtypeStruct((sent_rows, width), bf16),
@@ -761,6 +764,20 @@
         out_specs=pl.BlockSpec(memory_space=pltpu.VMEM),
         compiler_params=params(),
     )(ends, cross)
+
+    own = pl.pallas_call(
+        functools.partial(mirrored_columns, alone),
+        out_shape=jax.ShapeDtypeStruct((sent_rows, width), bf16),
+        in_specs=vmem(1) + [pl.BlockSpec(memory_space=pl.ANY)],
+        out_specs=pl.BlockSpec(memory_space=pltpu.VMEM),
+        scratch_shapes=[
+            pltpu.VMEM((channels * APART, width), f32),
+            pltpu.VMEM((16, width), f32),
+            pltpu.VMEM((channels, 16, width), bf16),
+            pltpu.VMEM((groups * 32, width), bf16),
+        ],
+        compiler_params=params(),
+    )(second_sent, core)
 
     pairs = []
     for low in range(0, nlon, 2):

time: 24.8 us -> 24.6 us (level)
  starting transfers between devices: 8.7 us -> 8.14 us
  waiting for transfers between devices: 0.65 us -> 1 us
    ppermute x1, starting transfers between devices: 0.9 us -> 0.33 us  [per_device(): cross = lax.ppermute(cross, ('lon', 'lat'), pairs)]
    ppermute x1, waiting for transfers between devices: 0.59 us -> 0.94 us  [per_device(): cross = lax.ppermute(cross, ('lon', 'lat'), pairs)]
where the time goes in v8:
time: 24.6 us; the launch traced here: 24.4 us
  Pallas kernels  14 us (57%)
  starting transfers between devices  8.14 us (33%)
  local copies, waits for them, and re-layouts  1.05 us (4%)
  waiting for transfers between devices  1 us (4%)
    ppermute x1, starting transfers between devices, per_device(): wrap = lax.ppermute(wrap, ('lon', 'lat'), pairs)  4.66 us
    pallas_call x1, Pallas kernels, per_device(): pl.pallas_call(second_layer, out_shape=jax.ShapeDtypeStruct((channels, ro...  4.33 us
    ppermute x1, starting transfers between devices, per_device(): first = lax.ppermute(first, 'lat', pairs)  3 us
    pallas_call x1, Pallas kernels, per_device(): pl.pallas_call(edge_rows, out_shape=jax.ShapeDtypeStruct((channels * 24,...  2.54 us
    pallas_call x1, Pallas kernels, per_device(): pl.pallas_call(inner_rows, out_shape=jax.ShapeDtypeStruct((channels * 24,...  1.93 us
    pallas_call x1, Pallas kernels, per_device(): pl.pallas_call(edge_columns, out_shape=jax.ShapeDtypeStruct((channels * 2...  1.88 us
    pallas_call x1, Pallas kernels, per_device(): pl.pallas_call(weights, out_shape=[jax.ShapeDtypeStruct((channels * 24, 2...  1.64 us
    unnamed x20, local copies, waits for them, and re-layouts  1.05 us
  transfers between devices with their start and end apart: 5, of which 1 were waited for; matrix products, arithmetic and copies ran while one was open for 0% of the time, Pallas kernels for 31%

profile of v8, /device:TPU:0, one launch (start us, length us, event | category | flops | bytes accessed | tf_op | source)
XLA Modules:
  0.0 24.4 jit_solution(79717301913886982)
XLA Ops:
  0.0 0.0 copy-start.1
  0.0 0.0 copy-start.2
  0.0 1.0 %copy-done.1 = bf16[96,16,128]{2,1,0:T(8,128)(2,1)S(1)} copy-done((bf16[96,16,128]{2,1,0:T(8,128)(2,1)S(1)}, bf16[96,16,128]{2,1,0:T(8,128)(2,1)}, u32[]{:S(2)}) %copy-start.1) | copy-done | bytes 393240
  1.0 0.0 copy-done.2
  1.0 0.1 shard_map.101.after_ref
  1.1 0.0 copy-start.3
  1.1 0.0 copy-start.4
  1.2 0.0 copy-start.5
  1.2 0.0 copy-start.6
  1.2 0.0 copy-start.7
  1.2 0.0 copy-start.8
  1.2 0.0 copy-start.9
  1.2 3.0 %collective-permute-start.1 = (bf16[592,128]{1,0:T(8,128)(2,1)S(1)}, bf16[592,128]{1,0:T(8,128)(2,1)S(1)}, u32[]{:S(2)}, u32[]{:S(2)}) collective-permute-start(bf16[592,128]{1,0:T(8,128)(2,1)S(1)} %shard_map.101.after_ref), channel_id=1, source_target_pairs={{0,1},{1,0},{2,3},{3,2},{4,5},{5,4},{6,7},{7,6},{8,9},{9,8},{10,11... | collective-permute-start | bytes 454664 | tf_op jit(solution)/shard_map/ppermute | solution.py:677
  4.2 0.1 shard_map.102.sent_ref
  4.4 0.1 collective-permute-start
  4.4 0.0 copy-done.3
  4.4 0.0 copy-done.4
  4.5 0.0 copy-done.5
  4.5 0.0 copy-done.6
  4.5 0.0 copy-done.7
  4.5 0.0 copy-done.8
  4.5 0.0 copy-done.9
  4.5 0.0 copy-start
  4.5 1.6 %shard_map.104 = (bf16[2304,256]{1,0:T(8,128)(2,1)S(1)}, bf16[1536,256]{1,0:T(8,128)(2,1)S(1)}, f32[2,3,96,128]{3,2,1,0:T(8,128)S(1)}, bf16[2,384,112]{2,1,0:T(8,128)(2,1)S(1)}) custom-call(f32[49,2,96]{2,1,0:T(2,128)S(1)} %bitcast.5, f32[2,96]{1,0:T(2,128)S(1)} %copy-done.6, f32[2,96]{1,0:T(2,128)S(1)} %copy-done.7, f32[2,96]{1,0:T(2,128)S(1)} %copy-done.8, ...), custom_call_target="tpu_custom_call" | custom-call | flops 2000000000 | bytes 1048576 | tf_op jit(solution)/shard_map/pallas_call | solution.py:680
  6.2 0.0 copy-done
  6.2 1.9 %shard_map.105.after_ref.old_ref = f32[2304,128]{1,0:T(8,128)S(1)} custom-call(bf16[96,16,128]{2,1,0:T(8,128)(2,1)S(1)} %copy-done.1, bf16[2304,256]{1,0:T(8,128)(2,1)S(1)} %get-tuple-element.20.matrix_ref, f32[2,3,96,128]{3,2,1,0:T(8,128)S(1)} %get-tuple-element.21.rows_ref, bf16[2,384,112]{2,1,0:T(8,128)(2,1)S(1)} %get-tuple-element.22.expand_ref, ...), custom_call_target="tpu_custom_call" | custom-call | flops 4000000000 | bytes 1048576 | tf_op jit(solution)/shard_map/pallas_call | solution.py:707
  8.1 0.1 collective-permute-done.1.first_ref
  8.2 0.5 %shard_map.103 = (bf16[96,16,128]{2,1,0:T(8,128)(2,1)S(1)}, f32[16,128]{1,0:T(8,128)S(1)}, bf16[208,128]{1,0:T(8,128)(2,1)S(1)}, bf16[224,128]{1,0:T(8,128)(2,1)S(1)}) custom-call(bf16[96,16,128]{2,1,0:T(8,128)(2,1)S(1)} %copy-done.1, s32[16,128]{1,0:T(8,128)S(1)} %copy-done.2, bf16[592,128]{1,0:T(8,128)(2,1)S(1)} %collective-permute-done.1.first_ref), custom_call_target="tpu_custom_call" | custom-call | flops 1000000000 | bytes 1048576 | tf_op jit(solution)/shard_map/pallas_call | solution.py:719
  8.7 4.7 %collective-permute-start.4 = (bf16[224,128]{1,0:T(8,128)(2,1)S(1)}, bf16[224,128]{1,0:T(8,128)(2,1)S(1)}, u32[]{:S(2)}, u32[]{:S(2)}) collective-permute-start(bf16[224,128]{1,0:T(8,128)(2,1)S(1)} %get-tuple-element.27), channel_id=1, source_target_pairs={{0,30},{30,0},{2,3},{4,5},{6,7},{8,9},{10,11},{12,13},{14,15},{16,... | collective-permute-start | bytes 172040 | tf_op jit(solution)/shard_map/ppermute | solution.py:741
  13.4 0.0 collective-permute-done.second_ref
  13.4 0.6 %shard_map.106 = (bf16[96,16,128]{2,1,0:T(8,128)(2,1)S(1)}, f32[16,128]{1,0:T(8,128)S(1)}, bf16[416,128]{1,0:T(8,128)(2,1)S(1)}, bf16[224,128]{1,0:T(8,128)(2,1)S(1)}) custom-call(bf16[592,128]{1,0:T(8,128)(2,1)S(1)} %collective-permute-done.second_ref, bf16[96,16,128]{2,1,0:T(8,128)(2,1)S(1)} %get-tuple-element.17.near_halo_ref, ...), custom_call_target="tpu_custom_call" | custom-call | tf_op jit(solution)/shard_map/pallas_call | solution.py:744
  14.0 0.3 %collective-permute-start.3 = (bf16[224,128]{1,0:T(8,128)(2,1)S(1)}, bf16[224,128]{1,0:T(8,128)(2,1)S(1)}, u32[]{:S(2)}, u32[]{:S(2)}) collective-permute-start(bf16[224,128]{1,0:T(8,128)(2,1)S(1)} %get-tuple-element.26.after_ref), channel_id=1, source_target_pairs={{2,4},{4,2},{6,8},{8,6},{10,12},{12,10},{14,16},{16,14},{18,20},{2... | collective-permute-start | bytes 172040 | tf_op jit(solution)/shard_map/ppermute | solution.py:794
  14.3 0.1 shard_map.107.after_ref
  14.4 0.1 collective-permute-start.2
  14.5 2.5 %shard_map.110.update_ref = f32[2304,128]{1,0:T(8,128)S(1)} custom-call(bf16[96,16,128]{2,1,0:T(8,128)(2,1)S(1)} %copy-done.1, bf16[96,16,128]{2,1,0:T(8,128)(2,1)S(1)} %get-tuple-element.23.halo_ref, bf16[2304,256]{1,0:T(8,128)(2,1)S(1)} %get-tuple-element.20.matrix_ref, ...), custom_call_target="tpu_custom_call", output_to_operand_aliasing={{}: (6, {})} | custom-call | flops 4000000000 | bytes 1048576 | tf_op jit(solution)/shard_map/pallas_call | solution.py:796
  17.0 0.2 shard_map.108.own_ref
  17.2 0.0 collective-permute-done.4.wrap_ref
  17.2 0.0 collective-permute-done.2.core_ref
  17.3 0.9 %collective-permute-done.3.cross_ref = bf16[224,128]{1,0:T(8,128)(2,1)S(1)} collective-permute-done((bf16[224,128]{1,0:T(8,128)(2,1)S(1)}, bf16[224,128]{1,0:T(8,128)(2,1)S(1)}, u32[]{:S(2)}, u32[]{:S(2)}) %collective-permute-start.3) | collective-permute-done | bytes 57376 | tf_op jit(solution)/shard_map/ppermute | solution.py:794
  18.2 1.9 %shard_map.109.strips = f32[2304,128]{1,0:T(8,128)S(1)} custom-call(bf16[224,128]{1,0:T(8,128)(2,1)S(1)} %collective-permute-done.2.core_ref, bf16[224,128]{1,0:T(8,128)(2,1)S(1)} %collective-permute-done.3.cross_ref, bf16[224,128]{1,0:T(8,128)(2,1)S(1)} %collective-permute-done.4.wrap_ref, bf16[224,128]{1,0:T(8,128)(2,1)S(1)} %shard_map.108.own_ref, ...), custom_call_target="tpu_custom_call" | custom-call | tf_op jit(solution)/shard_map/pallas_call | solution.py:807
  20.1 4.3 %shard_map.111 = bf16[96,16,128]{2,1,0:T(8,128)(2,1)} custom-call(bf16[96,16,128]{2,1,0:T(8,128)(2,1)S(1)} %copy-done.1, s32[16,128]{1,0:T(8,128)S(1)} %copy-done.2, bf16[96,16,128]{2,1,0:T(8,128)(2,1)S(1)} %get-tuple-element.23.halo_ref, f32[16,128]{1,0:T(8,128)S(1)} %get-tuple-element.24.halo_mask_ref, ...), custom_call_target="tpu_custom_call" | custom-call | tf_op jit(solution)/shard_map/pallas_call | solution.py:816
  (1 shorter events, 0.0 us)
Async XLA Ops:
  0.0 1.0 %copy-start.1 = (bf16[96,16,128]{2,1,0:T(8,128)(2,1)S(1)}, bf16[96,16,128]{2,1,0:T(8,128)(2,1)}, u32[]{:S(2)}) copy-start(bf16[96,16,128]{2,1,0:T(8,128)(2,1)} %field_ref.11) | copy-start | bytes 1179652
  0.0 1.0 %copy-start.2 = (s32[16,128]{1,0:T(8,128)S(1)}, s32[16,128]{1,0:T(8,128)}, u32[]{:S(2)}) copy-start(s32[16,128]{1,0:T(8,128)} %mask_ref.7) | copy-start | bytes 24580
  1.1 3.3 %copy-start.3 = (bf16[2,384,96]{1,2,0:T(8,128)(2,1)S(1)}, bf16[2,384,96]{1,2,0:T(8,128)(2,1)}, u32[]{:S(2)}) copy-start(bf16[2,384,96]{1,2,0:T(8,128)(2,1)} %param.16) | copy-start | bytes 442372
  1.1 3.3 %copy-start.4 = (f32[2,96,7,7]{1,0,3,2:T(2,128)S(1)}, f32[2,96,7,7]{1,0,3,2:T(2,128)}, u32[]{:S(2)}) copy-start(f32[2,96,7,7]{1,0,3,2:T(2,128)} %param.12) | copy-start | bytes 112900
  1.2 3.3 %copy-start.5 = (f32[2,384]{1,0:T(2,128)S(1)}, f32[2,384]{1,0:T(2,128)}, u32[]{:S(2)}) copy-start(f32[2,384]{1,0:T(2,128)} %expand_bias_ref.1) | copy-start | bytes 9220
  1.2 3.3 %copy-start.6 = (f32[2,96]{1,0:T(2,128)S(1)}, f32[2,96]{1,0:T(2,128)}, u32[]{:S(2)}) copy-start(f32[2,96]{1,0:T(2,128)} %bias_ref.1) | copy-start | bytes 2308
  1.2 3.3 %copy-start.7 = (f32[2,96]{1,0:T(2,128)S(1)}, f32[2,96]{1,0:T(2,128)}, u32[]{:S(2)}) copy-start(f32[2,96]{1,0:T(2,128)} %gain_ref.1) | copy-start | bytes 2308
  1.2 3.3 %copy-start.8 = (f32[2,96]{1,0:T(2,128)S(1)}, f32[2,96]{1,0:T(2,128)}, u32[]{:S(2)}) copy-start(f32[2,96]{1,0:T(2,128)} %norm_bias_ref.1) | copy-start | bytes 2308
  1.2 3.3 %copy-start.9 = (f32[2,96]{1,0:T(2,128)S(1)}, f32[2,96]{1,0:T(2,128)}, u32[]{:S(2)}) copy-start(f32[2,96]{1,0:T(2,128)} %reduce_bias_ref.1) | copy-start | bytes 2308
  1.2 6.9 %collective-permute-start.1 = (bf16[592,128]{1,0:T(8,128)(2,1)S(1)}, bf16[592,128]{1,0:T(8,128)(2,1)S(1)}, u32[]{:S(2)}, u32[]{:S(2)}) collective-permute-start(bf16[592,128]{1,0:T(8,128)(2,1)S(1)} %shard_map.101.after_ref), channel_id=1, source_target_pairs={{0,1},{1,0},{2,3},{3,2},{4,5},{5,4},{6,7},{7,6},{8,9},{9,8},{10,11... | collective-permute-start | bytes 454664 | tf_op jit(solution)/shard_map/ppermute | solution.py:677
  4.4 9.0 %collective-permute-start = (bf16[592,128]{1,0:T(8,128)(2,1)S(1)}, bf16[592,128]{1,0:T(8,128)(2,1)S(1)}, u32[]{:S(2)}, u32[]{:S(2)}) collective-permute-start(bf16[592,128]{1,0:T(8,128)(2,1)S(1)} %shard_map.102.sent_ref), channel_id=1, source_target_pairs={{1,31},{0,2},{3,29},{2,0},{5,27},{4,6},{7,25},{6,4},{9,23},{8,10},... | collective-permute-start | bytes 454664 | tf_op jit(solution)/shard_map/ppermute | solution.py:673
  4.5 1.7 %copy-start = (bf16[2,96,384]{2,1,0:T(8,128)(2,1)S(1)}, bf16[2,96,384]{2,1,0:T(8,128)(2,1)}, u32[]{:S(2)}) copy-start(bf16[2,96,384]{2,1,0:T(8,128)(2,1)} %reduce_ref.7) | copy-start | bytes 442372
  8.7 8.5 %collective-permute-start.4 = (bf16[224,128]{1,0:T(8,128)(2,1)S(1)}, bf16[224,128]{1,0:T(8,128)(2,1)S(1)}, u32[]{:S(2)}, u32[]{:S(2)}) collective-permute-start(bf16[224,128]{1,0:T(8,128)(2,1)S(1)} %get-tuple-element.27), channel_id=1, source_target_pairs={{0,30},{30,0},{2,3},{4,5},{6,7},{8,9},{10,11},{12,13},{14,15},{16,... | collective-permute-start | bytes 172040 | tf_op jit(solution)/shard_map/ppermute | solution.py:741
  14.0 4.2 %collective-permute-start.3 = (bf16[224,128]{1,0:T(8,128)(2,1)S(1)}, bf16[224,128]{1,0:T(8,128)(2,1)S(1)}, u32[]{:S(2)}, u32[]{:S(2)}) collective-permute-start(bf16[224,128]{1,0:T(8,128)(2,1)S(1)} %get-tuple-element.26.after_ref), channel_id=1, source_target_pairs={{2,4},{4,2},{6,8},{8,6},{10,12},{12,10},{14,16},{16,14},{18,20},{2... | collective-permute-start | bytes 172040 | tf_op jit(solution)/shard_map/ppermute | solution.py:794
  14.4 2.8 %collective-permute-start.2 = (bf16[224,128]{1,0:T(8,128)(2,1)S(1)}, bf16[224,128]{1,0:T(8,128)(2,1)S(1)}, u32[]{:S(2)}, u32[]{:S(2)}) collective-permute-start(bf16[224,128]{1,0:T(8,128)(2,1)S(1)} %shard_map.107.after_ref), channel_id=1, source_target_pairs={{0,2},{2,0},{4,6},{6,4},{8,10},{10,8},{12,14},{14,12},{16,18},{18,... | collective-permute-start | bytes 172040 | tf_op jit(solution)/shard_map/ppermute | solution.py:785

commit v9 on v8

--- a/solution.py
+++ b/solution.py
@@ -92,7 +92,7 @@
 
 
 def placed(wide, channels):
-    blocks = wide[...].reshape(channels, APART, wide.shape[1])
+    blocks = wide[: channels * APART, :].reshape(channels, APART, wide.shape[1])
     return blocks[:, :16, :].astype(jnp.bfloat16)
 
 
@@ -642,7 +642,7 @@
             in_specs=vmem(2) + [pl.BlockSpec(memory_space=pl.ANY)],
             out_specs=pl.BlockSpec(memory_space=pltpu.VMEM),
             scratch_shapes=[
-                pltpu.VMEM((channels * APART, width), f32),
+                pltpu.VMEM(((channels + 1) * APART, width), f32),
                 pltpu.VMEM((rows, width), f32),
             ],
             compiler_params=params(),
@@ -688,8 +688,8 @@
         in_specs=vmem(7),
         out_specs=vmem(4),
         scratch_shapes=[
-            pltpu.VMEM((channels * 24, 128), f32),
-            pltpu.VMEM((channels * 24, 128), f32),
+            pltpu.VMEM(((channels + 1) * 24, 128), f32),
+            pltpu.VMEM(((channels + 1) * 24, 128), f32),
             pltpu.VMEM((128, 128), f32),
             pltpu.VMEM((128, hidden), f32),
         ],
@@ -706,10 +706,10 @@
     )
     update = pl.pallas_call(
         inner_rows,
-        out_shape=jax.ShapeDtypeStruct((channels * 24, width), f32),
+        out_shape=jax.ShapeDtypeStruct(((channels + 1) * 24, width), f32),
         in_specs=vmem(5),
         out_specs=pl.BlockSpec(memory_space=pltpu.VMEM),
-        scratch_shapes=[pltpu.VMEM((pitch(channels) * 16, width), f32)] + buffers(len(INNER)),
+        scratch_shapes=[pltpu.VMEM((pitch(channels) * 17, width), f32)] + buffers(len(INNER)),
         compiler_params=params(),
         cost_estimate=cost(4e9),
     )(field, matrix_one, by_channel, expand, w_reduce)
@@ -727,7 +727,7 @@
         in_specs=vmem(3),
         out_specs=vmem(4),
         scratch_shapes=[
-            pltpu.VMEM((channels * APART, width), f32),
+            pltpu.VMEM(((channels + 1) * APART, width), f32),
             pltpu.VMEM((groups * 32, width), bf16),
         ],
         compiler_params=params(),
@@ -752,7 +752,7 @@
         in_specs=vmem(4) + [pl.BlockSpec(memory_space=pl.ANY)],
         out_specs=vmem(4),
         scratch_shapes=[
-            pltpu.VMEM((channels * APART, width), f32),
+            pltpu.VMEM(((channels + 1) * APART, width), f32),
             pltpu.VMEM((16, width), f32),
         ],
         compiler_params=params(),
@@ -771,7 +771,7 @@
         in_specs=vmem(1) + [pl.BlockSpec(memory_space=pl.ANY)],
         out_specs=pl.BlockSpec(memory_space=pltpu.VMEM),
         scratch_shapes=[
-            pltpu.VMEM((channels * APART, width), f32),
+            pltpu.VMEM(((channels + 1) * APART, width), f32),
             pltpu.VMEM((16, width), f32),
             pltpu.VMEM((channels, 16, width), bf16),
             pltpu.VMEM((groups * 32, width), bf16),
@@ -795,10 +795,10 @@
 
     update = pl.pallas_call(
         edge_rows,
-        out_shape=jax.ShapeDtypeStruct((channels * 24, width), f32),
+        out_shape=jax.ShapeDtypeStruct(((channels + 1) * 24, width), f32),
         in_specs=vmem(7),
         out_specs=pl.BlockSpec(memory_space=pltpu.VMEM),
-        scratch_shapes=[pltpu.VMEM((pitch(channels) * 16, width), f32)] + buffers(len(EDGE)),
+        scratch_shapes=[pltpu.VMEM((pitch(channels) * 17, width), f32)] + buffers(len(EDGE)),
         input_output_aliases={6: 0},
         compiler_params=params(),
         cost_estimate=cost(4e9),
@@ -806,10 +806,10 @@
 
     strips = pl.pallas_call(
         edge_columns,
-        out_shape=jax.ShapeDtypeStruct((channels * 24, width), f32),
+        out_shape=jax.ShapeDtypeStruct(((channels + 1) * 24, width), f32),
         in_specs=vmem(9),
         out_specs=pl.BlockSpec(memory_space=pltpu.VMEM),
-        scratch_shapes=[pltpu.VMEM((pitch(channels) * 24, width), f32)] + buffers(3),
+        scratch_shapes=[pltpu.VMEM((pitch(channels) * 25, width), f32)] + buffers(3),
         compiler_params=params(),
     )(core, cross, wrap, own, ends, matrix_one, by_channel, expand, w_reduce)
 
@@ -820,8 +820,8 @@
         out_specs=pl.BlockSpec(memory_space=pltpu.VMEM),
         scratch_shapes=[
             pltpu.VMEM((channels, rows, width), bf16),
-            pltpu.VMEM((pitch(channels) * 16, width), f32),
-            pltpu.VMEM((channels * APART, width), f32),
+            pltpu.VMEM((pitch(channels) * 17, width), f32),
+            pltpu.VMEM(((channels + 1) * APART, width), f32),
         ]
         + buffers(rows),
         compiler_params=params(),

time: 24.6 us -> 24.5 us (level)
  transfers between devices with their start and end apart: 5 -> 5, of which waited for: 1 -> 2; matrix products, arithmetic and copies ran while one was open for 0% -> 0% of each run, Pallas kernels for 31% -> 31%
where the time goes in v9:
time: 24.5 us; the launch traced here: 24.4 us
  Pallas kernels  13.9 us (57%)
  starting transfers between devices  8.14 us (33%)
  local copies, waits for them, and re-layouts  1.05 us (4%)
  waiting for transfers between devices  1 us (4%)
    ppermute x1, starting transfers between devices, per_device(): wrap = lax.ppermute(wrap, ('lon', 'lat'), pairs)  4.56 us
    pallas_call x1, Pallas kernels, per_device(): pl.pallas_call(second_layer, out_shape=jax.ShapeDtypeStruct((channels, ro...  4.36 us
    ppermute x1, starting transfers between devices, per_device(): first = lax.ppermute(first, 'lat', pairs)  3 us
    pallas_call x1, Pallas kernels, per_device(): pl.pallas_call(edge_rows, out_shape=jax.ShapeDtypeStruct(((channels + 1)...  2.53 us
    pallas_call x1, Pallas kernels, per_device(): pl.pallas_call(inner_rows, out_shape=jax.ShapeDtypeStruct(((channels + 1)...  1.93 us
    pallas_call x1, Pallas kernels, per_device(): pl.pallas_call(edge_columns, out_shape=jax.ShapeDtypeStruct(((channels +...  1.89 us
    pallas_call x1, Pallas kernels, per_device(): pl.pallas_call(weights, out_shape=[jax.ShapeDtypeStruct((channels * 24, 2...  1.54 us
    unnamed x20, local copies, waits for them, and re-layouts  1.05 us
  transfers between devices with their start and end apart: 5, of which 2 were waited for; matrix products, arithmetic and copies ran while one was open for 0% of the time, Pallas kernels for 31%

profile of v9, /device:TPU:0, one launch (start us, length us, event | category | flops | bytes accessed | tf_op | source)
XLA Modules:
  0.0 24.4 jit_solution(2027540895508239334)
XLA Ops:
  0.0 0.0 copy-start.1
  0.0 0.0 copy-start.2
  0.0 1.0 %copy-done.1 = bf16[96,16,128]{2,1,0:T(8,128)(2,1)S(1)} copy-done((bf16[96,16,128]{2,1,0:T(8,128)(2,1)S(1)}, bf16[96,16,128]{2,1,0:T(8,128)(2,1)}, u32[]{:S(2)}) %copy-start.1) | copy-done | bytes 393240
  1.0 0.0 copy-done.2
  1.0 0.1 shard_map.101.after_ref
  1.1 0.0 copy-start.3
  1.1 0.0 copy-start.4
  1.2 0.0 copy-start.5
  1.2 0.0 copy-start.6
  1.2 0.0 copy-start.7
  1.2 0.0 copy-start.8
  1.2 0.0 copy-start.9
  1.2 3.0 %collective-permute-start.1 = (bf16[592,128]{1,0:T(8,128)(2,1)S(1)}, bf16[592,128]{1,0:T(8,128)(2,1)S(1)}, u32[]{:S(2)}, u32[]{:S(2)}) collective-permute-start(bf16[592,128]{1,0:T(8,128)(2,1)S(1)} %shard_map.101.after_ref), channel_id=1, source_target_pairs={{0,1},{1,0},{2,3},{3,2},{4,5},{5,4},{6,7},{7,6},{8,9},{9,8},{10,11... | collective-permute-start | bytes 454664 | tf_op jit(solution)/shard_map/ppermute | solution.py:677
  4.2 0.1 shard_map.102.sent_ref
  4.4 0.1 collective-permute-start
  4.4 0.0 copy-done.3
  4.4 0.0 copy-done.4
  4.5 0.0 copy-done.5
  4.5 0.0 copy-done.6
  4.5 0.0 copy-done.7
  4.5 0.0 copy-done.8
  4.5 0.0 copy-done.9
  4.5 0.0 copy-start
  4.5 1.5 %shard_map.104 = (bf16[2304,256]{1,0:T(8,128)(2,1)S(1)}, bf16[1536,256]{1,0:T(8,128)(2,1)S(1)}, f32[2,3,96,128]{3,2,1,0:T(8,128)S(1)}, bf16[2,384,112]{2,1,0:T(8,128)(2,1)S(1)}) custom-call(f32[49,2,96]{2,1,0:T(2,128)S(1)} %bitcast.5, f32[2,96]{1,0:T(2,128)S(1)} %copy-done.6, f32[2,96]{1,0:T(2,128)S(1)} %copy-done.7, f32[2,96]{1,0:T(2,128)S(1)} %copy-done.8, ...), custom_call_target="tpu_custom_call" | custom-call | flops 2000000000 | bytes 1048576 | tf_op jit(solution)/shard_map/pallas_call | solution.py:680
  6.1 0.0 copy-done
  6.1 1.9 %shard_map.105.after_ref.old_ref = f32[2328,128]{1,0:T(8,128)S(1)} custom-call(bf16[96,16,128]{2,1,0:T(8,128)(2,1)S(1)} %copy-done.1, bf16[2304,256]{1,0:T(8,128)(2,1)S(1)} %get-tuple-element.20.matrix_ref, f32[2,3,96,128]{3,2,1,0:T(8,128)S(1)} %get-tuple-element.21.rows_ref, bf16[2,384,112]{2,1,0:T(8,128)(2,1)S(1)} %get-tuple-element.22.expand_ref, ...), custom_call_target="tpu_custom_call" | custom-call | flops 4000000000 | bytes 1048576 | tf_op jit(solution)/shard_map/pallas_call | solution.py:707
  8.0 0.1 collective-permute-done.1.first_ref
  8.2 0.5 %shard_map.103 = (bf16[96,16,128]{2,1,0:T(8,128)(2,1)S(1)}, f32[16,128]{1,0:T(8,128)S(1)}, bf16[208,128]{1,0:T(8,128)(2,1)S(1)}, bf16[224,128]{1,0:T(8,128)(2,1)S(1)}) custom-call(bf16[96,16,128]{2,1,0:T(8,128)(2,1)S(1)} %copy-done.1, s32[16,128]{1,0:T(8,128)S(1)} %copy-done.2, bf16[592,128]{1,0:T(8,128)(2,1)S(1)} %collective-permute-done.1.first_ref), custom_call_target="tpu_custom_call" | custom-call | flops 1000000000 | bytes 1048576 | tf_op jit(solution)/shard_map/pallas_call | solution.py:719
  8.7 4.6 %collective-permute-start.4 = (bf16[224,128]{1,0:T(8,128)(2,1)S(1)}, bf16[224,128]{1,0:T(8,128)(2,1)S(1)}, u32[]{:S(2)}, u32[]{:S(2)}) collective-permute-start(bf16[224,128]{1,0:T(8,128)(2,1)S(1)} %get-tuple-element.27), channel_id=1, source_target_pairs={{0,30},{30,0},{2,3},{4,5},{6,7},{8,9},{10,11},{12,13},{14,15},{16,... | collective-permute-start | bytes 172040 | tf_op jit(solution)/shard_map/ppermute | solution.py:741
  13.3 0.0 collective-permute-done.second_ref
  13.3 0.6 %shard_map.106 = (bf16[96,16,128]{2,1,0:T(8,128)(2,1)S(1)}, f32[16,128]{1,0:T(8,128)S(1)}, bf16[416,128]{1,0:T(8,128)(2,1)S(1)}, bf16[224,128]{1,0:T(8,128)(2,1)S(1)}) custom-call(bf16[592,128]{1,0:T(8,128)(2,1)S(1)} %collective-permute-done.second_ref, bf16[96,16,128]{2,1,0:T(8,128)(2,1)S(1)} %get-tuple-element.17.near_halo_ref, ...), custom_call_target="tpu_custom_call" | custom-call | tf_op jit(solution)/shard_map/pallas_call | solution.py:744
  13.9 0.4 %collective-permute-start.3 = (bf16[224,128]{1,0:T(8,128)(2,1)S(1)}, bf16[224,128]{1,0:T(8,128)(2,1)S(1)}, u32[]{:S(2)}, u32[]{:S(2)}) collective-permute-start(bf16[224,128]{1,0:T(8,128)(2,1)S(1)} %get-tuple-element.26.after_ref), channel_id=1, source_target_pairs={{2,4},{4,2},{6,8},{8,6},{10,12},{12,10},{14,16},{16,14},{18,20},{2... | collective-permute-start | bytes 172040 | tf_op jit(solution)/shard_map/ppermute | solution.py:794
  14.3 0.1 shard_map.107.after_ref
  14.4 0.1 collective-permute-start.2
  14.5 2.5 %shard_map.110.update_ref = f32[2328,128]{1,0:T(8,128)S(1)} custom-call(bf16[96,16,128]{2,1,0:T(8,128)(2,1)S(1)} %copy-done.1, bf16[96,16,128]{2,1,0:T(8,128)(2,1)S(1)} %get-tuple-element.23.halo_ref, bf16[2304,256]{1,0:T(8,128)(2,1)S(1)} %get-tuple-element.20.matrix_ref, ...), custom_call_target="tpu_custom_call", output_to_operand_aliasing={{}: (6, {})} | custom-call | flops 4000000000 | bytes 1048576 | tf_op jit(solution)/shard_map/pallas_call | solution.py:796
  17.0 0.2 shard_map.108.own_ref
  17.2 0.0 collective-permute-done.4.wrap_ref
  17.2 0.0 collective-permute-done.2.core_ref
  17.2 0.8 %collective-permute-done.3.cross_ref = bf16[224,128]{1,0:T(8,128)(2,1)S(1)} collective-permute-done((bf16[224,128]{1,0:T(8,128)(2,1)S(1)}, bf16[224,128]{1,0:T(8,128)(2,1)S(1)}, u32[]{:S(2)}, u32[]{:S(2)}) %collective-permute-start.3) | collective-permute-done | bytes 57376 | tf_op jit(solution)/shard_map/ppermute | solution.py:794
  18.1 1.9 %shard_map.109.strips = f32[2328,128]{1,0:T(8,128)S(1)} custom-call(bf16[224,128]{1,0:T(8,128)(2,1)S(1)} %collective-permute-done.2.core_ref, bf16[224,128]{1,0:T(8,128)(2,1)S(1)} %collective-permute-done.3.cross_ref, bf16[224,128]{1,0:T(8,128)(2,1)S(1)} %collective-permute-done.4.wrap_ref, bf16[224,128]{1,0:T(8,128)(2,1)S(1)} %shard_map.108.own_ref, ...), custom_call_target="tpu_custom_call" | custom-call | tf_op jit(solution)/shard_map/pallas_call | solution.py:807
  20.0 4.4 %shard_map.111 = bf16[96,16,128]{2,1,0:T(8,128)(2,1)} custom-call(bf16[96,16,128]{2,1,0:T(8,128)(2,1)S(1)} %copy-done.1, s32[16,128]{1,0:T(8,128)S(1)} %copy-done.2, bf16[96,16,128]{2,1,0:T(8,128)(2,1)S(1)} %get-tuple-element.23.halo_ref, f32[16,128]{1,0:T(8,128)S(1)} %get-tuple-element.24.halo_mask_ref, ...), custom_call_target="tpu_custom_call" | custom-call | tf_op jit(solution)/shard_map/pallas_call | solution.py:816
  (1 shorter events, 0.0 us)
Async XLA Ops:
  0.0 1.0 %copy-start.1 = (bf16[96,16,128]{2,1,0:T(8,128)(2,1)S(1)}, bf16[96,16,128]{2,1,0:T(8,128)(2,1)}, u32[]{:S(2)}) copy-start(bf16[96,16,128]{2,1,0:T(8,128)(2,1)} %field_ref.11) | copy-start | bytes 1179652
  0.0 1.0 %copy-start.2 = (s32[16,128]{1,0:T(8,128)S(1)}, s32[16,128]{1,0:T(8,128)}, u32[]{:S(2)}) copy-start(s32[16,128]{1,0:T(8,128)} %mask_ref.7) | copy-start | bytes 24580
  1.1 3.3 %copy-start.3 = (bf16[2,384,96]{1,2,0:T(8,128)(2,1)S(1)}, bf16[2,384,96]{1,2,0:T(8,128)(2,1)}, u32[]{:S(2)}) copy-start(bf16[2,384,96]{1,2,0:T(8,128)(2,1)} %param.16) | copy-start | bytes 442372
  1.1 3.3 %copy-start.4 = (f32[2,96,7,7]{1,0,3,2:T(2,128)S(1)}, f32[2,96,7,7]{1,0,3,2:T(2,128)}, u32[]{:S(2)}) copy-start(f32[2,96,7,7]{1,0,3,2:T(2,128)} %param.12) | copy-start | bytes 112900
  1.2 3.3 %copy-start.5 = (f32[2,384]{1,0:T(2,128)S(1)}, f32[2,384]{1,0:T(2,128)}, u32[]{:S(2)}) copy-start(f32[2,384]{1,0:T(2,128)} %expand_bias_ref.1) | copy-start | bytes 9220
  1.2 3.3 %copy-start.6 = (f32[2,96]{1,0:T(2,128)S(1)}, f32[2,96]{1,0:T(2,128)}, u32[]{:S(2)}) copy-start(f32[2,96]{1,0:T(2,128)} %bias_ref.1) | copy-start | bytes 2308
  1.2 3.3 %copy-start.7 = (f32[2,96]{1,0:T(2,128)S(1)}, f32[2,96]{1,0:T(2,128)}, u32[]{:S(2)}) copy-start(f32[2,96]{1,0:T(2,128)} %gain_ref.1) | copy-start | bytes 2308
  1.2 3.3 %copy-start.8 = (f32[2,96]{1,0:T(2,128)S(1)}, f32[2,96]{1,0:T(2,128)}, u32[]{:S(2)}) copy-start(f32[2,96]{1,0:T(2,128)} %norm_bias_ref.1) | copy-start | bytes 2308
  1.2 3.3 %copy-start.9 = (f32[2,96]{1,0:T(2,128)S(1)}, f32[2,96]{1,0:T(2,128)}, u32[]{:S(2)}) copy-start(f32[2,96]{1,0:T(2,128)} %reduce_bias_ref.1) | copy-start | bytes 2308
  1.2 6.9 %collective-permute-start.1 = (bf16[592,128]{1,0:T(8,128)(2,1)S(1)}, bf16[592,128]{1,0:T(8,128)(2,1)S(1)}, u32[]{:S(2)}, u32[]{:S(2)}) collective-permute-start(bf16[592,128]{1,0:T(8,128)(2,1)S(1)} %shard_map.101.after_ref), channel_id=1, source_target_pairs={{0,1},{1,0},{2,3},{3,2},{4,5},{5,4},{6,7},{7,6},{8,9},{9,8},{10,11... | collective-permute-start | bytes 454664 | tf_op jit(solution)/shard_map/ppermute | solution.py:677
  4.4 8.9 %collective-permute-start = (bf16[592,128]{1,0:T(8,128)(2,1)S(1)}, bf16[592,128]{1,0:T(8,128)(2,1)S(1)}, u32[]{:S(2)}, u32[]{:S(2)}) collective-permute-start(bf16[592,128]{1,0:T(8,128)(2,1)S(1)} %shard_map.102.sent_ref), channel_id=1, source_target_pairs={{1,31},{0,2},{3,29},{2,0},{5,27},{4,6},{7,25},{6,4},{9,23},{8,10},... | collective-permute-start | bytes 454664 | tf_op jit(solution)/shard_map/ppermute | solution.py:673
  4.5 1.6 %copy-start = (bf16[2,96,384]{2,1,0:T(8,128)(2,1)S(1)}, bf16[2,96,384]{2,1,0:T(8,128)(2,1)}, u32[]{:S(2)}) copy-start(bf16[2,96,384]{2,1,0:T(8,128)(2,1)} %reduce_ref.7) | copy-start | bytes 442372
  8.7 8.5 %collective-permute-start.4 = (bf16[224,128]{1,0:T(8,128)(2,1)S(1)}, bf16[224,128]{1,0:T(8,128)(2,1)S(1)}, u32[]{:S(2)}, u32[]{:S(2)}) collective-permute-start(bf16[224,128]{1,0:T(8,128)(2,1)S(1)} %get-tuple-element.27), channel_id=1, source_target_pairs={{0,30},{30,0},{2,3},{4,5},{6,7},{8,9},{10,11},{12,13},{14,15},{16,... | collective-permute-start | bytes 172040 | tf_op jit(solution)/shard_map/ppermute | solution.py:741
  13.9 4.2 %collective-permute-start.3 = (bf16[224,128]{1,0:T(8,128)(2,1)S(1)}, bf16[224,128]{1,0:T(8,128)(2,1)S(1)}, u32[]{:S(2)}, u32[]{:S(2)}) collective-permute-start(bf16[224,128]{1,0:T(8,128)(2,1)S(1)} %get-tuple-element.26.after_ref), channel_id=1, source_target_pairs={{2,4},{4,2},{6,8},{8,6},{10,12},{12,10},{14,16},{16,14},{18,20},{2... | collective-permute-start | bytes 172040 | tf_op jit(solution)/shard_map/ppermute | solution.py:794
  14.4 2.8 %collective-permute-start.2 = (bf16[224,128]{1,0:T(8,128)(2,1)S(1)}, bf16[224,128]{1,0:T(8,128)(2,1)S(1)}, u32[]{:S(2)}, u32[]{:S(2)}) collective-permute-start(bf16[224,128]{1,0:T(8,128)(2,1)S(1)} %shard_map.107.after_ref), channel_id=1, source_target_pairs={{0,2},{2,0},{4,6},{6,4},{8,10},{10,8},{12,14},{14,12},{16,18},{18,... | collective-permute-start | bytes 172040 | tf_op jit(solution)/shard_map/ppermute | solution.py:785

commit v10 on v9

--- a/solution.py
+++ b/solution.py
@@ -353,7 +353,8 @@
     for n, block in enumerate(blocks):
         at = slice(n * width, (n + 1) * width)
         normed_ref[:channels, at] = norm(rows_ref, layer, block())
-    tiles = [slice(n, min(n + 2 * width, wide)) for n in range(0, wide, 2 * width)]
+    step = 2 if count % 2 == 0 else 3
+    tiles = [slice(n, min(n + step * width, wide)) for n in range(0, wide, step * width)]
     for at in tiles:
         normed = normed_ref[:, at]
         for part in range(0, hidden, 128):
@@ -366,7 +367,7 @@
     for t, at in enumerate(tiles):
         change = jnp.dot(reduce_ref[layer], inner_ref[:, at], preferred_element_type=jnp.float32)
         for n in range((at.stop - at.start) // width):
-            put(t * 2 + n, change[:, n * width : (n + 1) * width] + extra)
+            put(t * step + n, change[:, n * width : (n + 1) * width] + extra)
 
 
 def columns_stack(block, ones):

time: 24.5 us -> 24.5 us (level)
  no operation moved by 1% of the time
where the time goes in v10:
time: 24.5 us; the launch traced here: 24.4 us
  Pallas kernels  14 us (57%)
  starting transfers between devices  8.14 us (33%)
  local copies, waits for them, and re-layouts  1.05 us (4%)
  waiting for transfers between devices  1 us (4%)
    ppermute x1, starting transfers between devices, per_device(): wrap = lax.ppermute(wrap, ('lon', 'lat'), pairs)  4.56 us
    pallas_call x1, Pallas kernels, per_device(): pl.pallas_call(second_layer, out_shape=jax.ShapeDtypeStruct((channels, ro...  4.36 us
    ppermute x1, starting transfers between devices, per_device(): first = lax.ppermute(first, 'lat', pairs)  3 us
    pallas_call x1, Pallas kernels, per_device(): pl.pallas_call(edge_rows, out_shape=jax.ShapeDtypeStruct(((channels + 1)...  2.53 us
    pallas_call x1, Pallas kernels, per_device(): pl.pallas_call(inner_rows, out_shape=jax.ShapeDtypeStruct(((channels + 1)...  1.93 us
    pallas_call x1, Pallas kernels, per_device(): pl.pallas_call(edge_columns, out_shape=jax.ShapeDtypeStruct(((channels +...  1.91 us
    pallas_call x1, Pallas kernels, per_device(): pl.pallas_call(weights, out_shape=[jax.ShapeDtypeStruct((channels * 24, 2...  1.54 us
    unnamed x20, local copies, waits for them, and re-layouts  1.05 us
  transfers between devices with their start and end apart: 5, of which 2 were waited for; matrix products, arithmetic and copies ran while one was open for 0% of the time, Pallas kernels for 31%

profile of v10, /device:TPU:0, one launch (start us, length us, event | category | flops | bytes accessed | tf_op | source)
XLA Modules:
  0.0 24.4 jit_solution(3482138189772363842)
XLA Ops:
  0.0 0.0 copy-start.1
  0.0 0.0 copy-start.2
  0.0 1.0 %copy-done.1 = bf16[96,16,128]{2,1,0:T(8,128)(2,1)S(1)} copy-done((bf16[96,16,128]{2,1,0:T(8,128)(2,1)S(1)}, bf16[96,16,128]{2,1,0:T(8,128)(2,1)}, u32[]{:S(2)}) %copy-start.1) | copy-done | bytes 393240
  1.0 0.0 copy-done.2
  1.0 0.1 shard_map.101.after_ref
  1.1 0.0 copy-start.3
  1.1 0.0 copy-start.4
  1.2 0.0 copy-start.5
  1.2 0.0 copy-start.6
  1.2 0.0 copy-start.7
  1.2 0.0 copy-start.8
  1.2 0.0 copy-start.9
  1.2 3.0 %collective-permute-start.1 = (bf16[592,128]{1,0:T(8,128)(2,1)S(1)}, bf16[592,128]{1,0:T(8,128)(2,1)S(1)}, u32[]{:S(2)}, u32[]{:S(2)}) collective-permute-start(bf16[592,128]{1,0:T(8,128)(2,1)S(1)} %shard_map.101.after_ref), channel_id=1, source_target_pairs={{0,1},{1,0},{2,3},{3,2},{4,5},{5,4},{6,7},{7,6},{8,9},{9,8},{10,11... | collective-permute-start | bytes 454664 | tf_op jit(solution)/shard_map/ppermute | solution.py:678
  4.2 0.1 shard_map.102.sent_ref
  4.4 0.1 collective-permute-start
  4.4 0.0 copy-done.3
  4.4 0.0 copy-done.4
  4.5 0.0 copy-done.5
  4.5 0.0 copy-done.6
  4.5 0.0 copy-done.7
  4.5 0.0 copy-done.8
  4.5 0.0 copy-done.9
  4.5 0.0 copy-start
  4.5 1.5 %shard_map.104 = (bf16[2304,256]{1,0:T(8,128)(2,1)S(1)}, bf16[1536,256]{1,0:T(8,128)(2,1)S(1)}, f32[2,3,96,128]{3,2,1,0:T(8,128)S(1)}, bf16[2,384,112]{2,1,0:T(8,128)(2,1)S(1)}) custom-call(f32[49,2,96]{2,1,0:T(2,128)S(1)} %bitcast.5, f32[2,96]{1,0:T(2,128)S(1)} %copy-done.6, f32[2,96]{1,0:T(2,128)S(1)} %copy-done.7, f32[2,96]{1,0:T(2,128)S(1)} %copy-done.8, ...), custom_call_target="tpu_custom_call" | custom-call | flops 2000000000 | bytes 1048576 | tf_op jit(solution)/shard_map/pallas_call | solution.py:681
  6.1 0.0 copy-done
  6.1 1.9 %shard_map.105.after_ref.old_ref = f32[2328,128]{1,0:T(8,128)S(1)} custom-call(bf16[96,16,128]{2,1,0:T(8,128)(2,1)S(1)} %copy-done.1, bf16[2304,256]{1,0:T(8,128)(2,1)S(1)} %get-tuple-element.20.matrix_ref, f32[2,3,96,128]{3,2,1,0:T(8,128)S(1)} %get-tuple-element.21.rows_ref, bf16[2,384,112]{2,1,0:T(8,128)(2,1)S(1)} %get-tuple-element.22.expand_ref, ...), custom_call_target="tpu_custom_call" | custom-call | flops 4000000000 | bytes 1048576 | tf_op jit(solution)/shard_map/pallas_call | solution.py:708
  8.0 0.1 collective-permute-done.1.first_ref
  8.2 0.5 %shard_map.103 = (bf16[96,16,128]{2,1,0:T(8,128)(2,1)S(1)}, f32[16,128]{1,0:T(8,128)S(1)}, bf16[208,128]{1,0:T(8,128)(2,1)S(1)}, bf16[224,128]{1,0:T(8,128)(2,1)S(1)}) custom-call(bf16[96,16,128]{2,1,0:T(8,128)(2,1)S(1)} %copy-done.1, s32[16,128]{1,0:T(8,128)S(1)} %copy-done.2, bf16[592,128]{1,0:T(8,128)(2,1)S(1)} %collective-permute-done.1.first_ref), custom_call_target="tpu_custom_call" | custom-call | flops 1000000000 | bytes 1048576 | tf_op jit(solution)/shard_map/pallas_call | solution.py:720
  8.7 4.6 %collective-permute-start.4 = (bf16[224,128]{1,0:T(8,128)(2,1)S(1)}, bf16[224,128]{1,0:T(8,128)(2,1)S(1)}, u32[]{:S(2)}, u32[]{:S(2)}) collective-permute-start(bf16[224,128]{1,0:T(8,128)(2,1)S(1)} %get-tuple-element.27), channel_id=1, source_target_pairs={{0,30},{30,0},{2,3},{4,5},{6,7},{8,9},{10,11},{12,13},{14,15},{16,... | collective-permute-start | bytes 172040 | tf_op jit(solution)/shard_map/ppermute | solution.py:742
  13.3 0.0 collective-permute-done.second_ref
  13.3 0.6 %shard_map.106 = (bf16[96,16,128]{2,1,0:T(8,128)(2,1)S(1)}, f32[16,128]{1,0:T(8,128)S(1)}, bf16[416,128]{1,0:T(8,128)(2,1)S(1)}, bf16[224,128]{1,0:T(8,128)(2,1)S(1)}) custom-call(bf16[592,128]{1,0:T(8,128)(2,1)S(1)} %collective-permute-done.second_ref, bf16[96,16,128]{2,1,0:T(8,128)(2,1)S(1)} %get-tuple-element.17.near_halo_ref, ...), custom_call_target="tpu_custom_call" | custom-call | tf_op jit(solution)/shard_map/pallas_call | solution.py:745
  13.9 0.4 %collective-permute-start.3 = (bf16[224,128]{1,0:T(8,128)(2,1)S(1)}, bf16[224,128]{1,0:T(8,128)(2,1)S(1)}, u32[]{:S(2)}, u32[]{:S(2)}) collective-permute-start(bf16[224,128]{1,0:T(8,128)(2,1)S(1)} %get-tuple-element.26.after_ref), channel_id=1, source_target_pairs={{2,4},{4,2},{6,8},{8,6},{10,12},{12,10},{14,16},{16,14},{18,20},{2... | collective-permute-start | bytes 172040 | tf_op jit(solution)/shard_map/ppermute | solution.py:795
  14.3 0.1 shard_map.107.after_ref
  14.4 0.1 collective-permute-start.2
  14.5 2.5 %shard_map.110.update_ref = f32[2328,128]{1,0:T(8,128)S(1)} custom-call(bf16[96,16,128]{2,1,0:T(8,128)(2,1)S(1)} %copy-done.1, bf16[96,16,128]{2,1,0:T(8,128)(2,1)S(1)} %get-tuple-element.23.halo_ref, bf16[2304,256]{1,0:T(8,128)(2,1)S(1)} %get-tuple-element.20.matrix_ref, ...), custom_call_target="tpu_custom_call", output_to_operand_aliasing={{}: (6, {})} | custom-call | flops 4000000000 | bytes 1048576 | tf_op jit(solution)/shard_map/pallas_call | solution.py:797
  17.0 0.2 shard_map.108.own_ref
  17.2 0.0 collective-permute-done.4.wrap_ref
  17.2 0.0 collective-permute-done.2.core_ref
  17.2 0.8 %collective-permute-done.3.cross_ref = bf16[224,128]{1,0:T(8,128)(2,1)S(1)} collective-permute-done((bf16[224,128]{1,0:T(8,128)(2,1)S(1)}, bf16[224,128]{1,0:T(8,128)(2,1)S(1)}, u32[]{:S(2)}, u32[]{:S(2)}) %collective-permute-start.3) | collective-permute-done | bytes 57376 | tf_op jit(solution)/shard_map/ppermute | solution.py:795
  18.1 1.9 %shard_map.109.strips = f32[2328,128]{1,0:T(8,128)S(1)} custom-call(bf16[224,128]{1,0:T(8,128)(2,1)S(1)} %collective-permute-done.2.core_ref, bf16[224,128]{1,0:T(8,128)(2,1)S(1)} %collective-permute-done.3.cross_ref, bf16[224,128]{1,0:T(8,128)(2,1)S(1)} %collective-permute-done.4.wrap_ref, bf16[224,128]{1,0:T(8,128)(2,1)S(1)} %shard_map.108.own_ref, ...), custom_call_target="tpu_custom_call" | custom-call | tf_op jit(solution)/shard_map/pallas_call | solution.py:808
  20.0 4.4 %shard_map.111 = bf16[96,16,128]{2,1,0:T(8,128)(2,1)} custom-call(bf16[96,16,128]{2,1,0:T(8,128)(2,1)S(1)} %copy-done.1, s32[16,128]{1,0:T(8,128)S(1)} %copy-done.2, bf16[96,16,128]{2,1,0:T(8,128)(2,1)S(1)} %get-tuple-element.23.halo_ref, f32[16,128]{1,0:T(8,128)S(1)} %get-tuple-element.24.halo_mask_ref, ...), custom_call_target="tpu_custom_call" | custom-call | tf_op jit(solution)/shard_map/pallas_call | solution.py:817
  (1 shorter events, 0.0 us)
Async XLA Ops:
  0.0 1.0 %copy-start.1 = (bf16[96,16,128]{2,1,0:T(8,128)(2,1)S(1)}, bf16[96,16,128]{2,1,0:T(8,128)(2,1)}, u32[]{:S(2)}) copy-start(bf16[96,16,128]{2,1,0:T(8,128)(2,1)} %field_ref.11) | copy-start | bytes 1179652
  0.0 1.0 %copy-start.2 = (s32[16,128]{1,0:T(8,128)S(1)}, s32[16,128]{1,0:T(8,128)}, u32[]{:S(2)}) copy-start(s32[16,128]{1,0:T(8,128)} %mask_ref.7) | copy-start | bytes 24580
  1.1 3.3 %copy-start.3 = (bf16[2,384,96]{1,2,0:T(8,128)(2,1)S(1)}, bf16[2,384,96]{1,2,0:T(8,128)(2,1)}, u32[]{:S(2)}) copy-start(bf16[2,384,96]{1,2,0:T(8,128)(2,1)} %param.16) | copy-start | bytes 442372
  1.1 3.3 %copy-start.4 = (f32[2,96,7,7]{1,0,3,2:T(2,128)S(1)}, f32[2,96,7,7]{1,0,3,2:T(2,128)}, u32[]{:S(2)}) copy-start(f32[2,96,7,7]{1,0,3,2:T(2,128)} %param.12) | copy-start | bytes 112900
  1.2 3.3 %copy-start.5 = (f32[2,384]{1,0:T(2,128)S(1)}, f32[2,384]{1,0:T(2,128)}, u32[]{:S(2)}) copy-start(f32[2,384]{1,0:T(2,128)} %expand_bias_ref.1) | copy-start | bytes 9220
  1.2 3.3 %copy-start.6 = (f32[2,96]{1,0:T(2,128)S(1)}, f32[2,96]{1,0:T(2,128)}, u32[]{:S(2)}) copy-start(f32[2,96]{1,0:T(2,128)} %bias_ref.1) | copy-start | bytes 2308
  1.2 3.3 %copy-start.7 = (f32[2,96]{1,0:T(2,128)S(1)}, f32[2,96]{1,0:T(2,128)}, u32[]{:S(2)}) copy-start(f32[2,96]{1,0:T(2,128)} %gain_ref.1) | copy-start | bytes 2308
  1.2 3.3 %copy-start.8 = (f32[2,96]{1,0:T(2,128)S(1)}, f32[2,96]{1,0:T(2,128)}, u32[]{:S(2)}) copy-start(f32[2,96]{1,0:T(2,128)} %norm_bias_ref.1) | copy-start | bytes 2308
  1.2 3.3 %copy-start.9 = (f32[2,96]{1,0:T(2,128)S(1)}, f32[2,96]{1,0:T(2,128)}, u32[]{:S(2)}) copy-start(f32[2,96]{1,0:T(2,128)} %reduce_bias_ref.1) | copy-start | bytes 2308
  1.2 6.9 %collective-permute-start.1 = (bf16[592,128]{1,0:T(8,128)(2,1)S(1)}, bf16[592,128]{1,0:T(8,128)(2,1)S(1)}, u32[]{:S(2)}, u32[]{:S(2)}) collective-permute-start(bf16[592,128]{1,0:T(8,128)(2,1)S(1)} %shard_map.101.after_ref), channel_id=1, source_target_pairs={{0,1},{1,0},{2,3},{3,2},{4,5},{5,4},{6,7},{7,6},{8,9},{9,8},{10,11... | collective-permute-start | bytes 454664 | tf_op jit(solution)/shard_map/ppermute | solution.py:678
  4.4 8.9 %collective-permute-start = (bf16[592,128]{1,0:T(8,128)(2,1)S(1)}, bf16[592,128]{1,0:T(8,128)(2,1)S(1)}, u32[]{:S(2)}, u32[]{:S(2)}) collective-permute-start(bf16[592,128]{1,0:T(8,128)(2,1)S(1)} %shard_map.102.sent_ref), channel_id=1, source_target_pairs={{1,31},{0,2},{3,29},{2,0},{5,27},{4,6},{7,25},{6,4},{9,23},{8,10},... | collective-permute-start | bytes 454664 | tf_op jit(solution)/shard_map/ppermute | solution.py:674
  4.5 1.6 %copy-start = (bf16[2,96,384]{2,1,0:T(8,128)(2,1)S(1)}, bf16[2,96,384]{2,1,0:T(8,128)(2,1)}, u32[]{:S(2)}) copy-start(bf16[2,96,384]{2,1,0:T(8,128)(2,1)} %reduce_ref.7) | copy-start | bytes 442372
  8.7 8.5 %collective-permute-start.4 = (bf16[224,128]{1,0:T(8,128)(2,1)S(1)}, bf16[224,128]{1,0:T(8,128)(2,1)S(1)}, u32[]{:S(2)}, u32[]{:S(2)}) collective-permute-start(bf16[224,128]{1,0:T(8,128)(2,1)S(1)} %get-tuple-element.27), channel_id=1, source_target_pairs={{0,30},{30,0},{2,3},{4,5},{6,7},{8,9},{10,11},{12,13},{14,15},{16,... | collective-permute-start | bytes 172040 | tf_op jit(solution)/shard_map/ppermute | solution.py:742
  13.9 4.2 %collective-permute-start.3 = (bf16[224,128]{1,0:T(8,128)(2,1)S(1)}, bf16[224,128]{1,0:T(8,128)(2,1)S(1)}, u32[]{:S(2)}, u32[]{:S(2)}) collective-permute-start(bf16[224,128]{1,0:T(8,128)(2,1)S(1)} %get-tuple-element.26.after_ref), channel_id=1, source_target_pairs={{2,4},{4,2},{6,8},{8,6},{10,12},{12,10},{14,16},{16,14},{18,20},{2... | collective-permute-start | bytes 172040 | tf_op jit(solution)/shard_map/ppermute | solution.py:795
  14.4 2.8 %collective-permute-start.2 = (bf16[224,128]{1,0:T(8,128)(2,1)S(1)}, bf16[224,128]{1,0:T(8,128)(2,1)S(1)}, u32[]{:S(2)}, u32[]{:S(2)}) collective-permute-start(bf16[224,128]{1,0:T(8,128)(2,1)S(1)} %shard_map.107.after_ref), channel_id=1, source_target_pairs={{0,2},{2,0},{4,6},{6,4},{8,10},{10,8},{12,14},{14,12},{16,18},{18,... | collective-permute-start | bytes 172040 | tf_op jit(solution)/shard_map/ppermute | solution.py:786
